TPU v7x, 32 devices: a whole 2x2x4 slice. The times are simulated.
32 devices in a mesh: blk: 4 (over y, x), grp: 8 (over z, core).
Axes of the slice: x: 2, y: 2, z: 4, core: 2. Of those that a mesh axis runs over, the one named last changes fastest.
Arguments:
- tokens: bfloat16 [16, 512, 1024], P('grp', 'blk'), may hold values from -6 to 6
- gain_one: bfloat16 [1024], replicated, may hold values from 0.5 to 1.5
- bias_one: bfloat16 [1024], replicated, may hold values from -1.75 to 1.75
- w_qkv: bfloat16 [1024, 3072], replicated, may hold values from -0.1875 to 0.1875
- w_out: bfloat16 [1024, 1024], replicated, may hold values from -3 to 3
- gain_two: bfloat16 [1024], replicated, may hold values from 0.5 to 1.5
- bias_two: bfloat16 [1024], replicated, may hold values from -1.75 to 1.75
- w_in: bfloat16 [1024, 4096], replicated, may hold values from -0.1875 to 0.1875
- w_down: bfloat16 [4096, 1024], replicated, may hold values from -0.09375 to 0.09375
- mem_keys: bfloat16 [16, 512, 1024], P('grp', 'blk'), may hold values from -6 to 6
- mem_values: bfloat16 [16, 512, 1024], P('grp', 'blk'), may hold values from -6 to 6
- continues: int32 [16], replicated, may hold values from 0 to 15, each once
- block_place: int32 [4], replicated, may hold values from 0 to 3, each once
- cotangent: bfloat16 [16, 512, 1024], P('grp', 'blk'), may hold values from -6 to 6
Outputs:
- mixed: bfloat16 [16, 512, 1024], P('grp', 'blk')
- grad_tokens: float32 [16, 512, 1024], P('grp', 'blk')
- grad_gain_one: float32 [1024], P('blk')
- grad_bias_one: float32 [1024], P('blk')
- grad_qkv: float32 [1024, 3072], P('blk')
- grad_out: float32 [1024, 1024], P('blk')
- grad_gain_two: float32 [1024], P('blk')
- grad_bias_two: float32 [1024], P('blk')
- grad_in: float32 [1024, 4096], P('blk')
- grad_down: float32 [4096, 1024], P('blk')
Inputs may be any that keep to these rules, and one draw needn't show every extreme that they name: Segment s reads cached bank continues[s]; every bank is read by exactly one segment. Blk index b holds positions block_place[b] * 128 to block_place[b] * 128 + 127 of each of its segments; every block is held once.
All inputs are finite; a program needn't handle non-finite values.
Results may differ from a plain program's by a relative error of at most 0.025.
Values may be sent and summed in bfloat16 or wider, within the bound.
No kernel may reach another device: no remote copies, remote signals or barrier semaphores. Data moves between devices by JAX's collectives and lax.ppermute only.
A program may use at most 256 MiB of HBM per device.

v0:
```python
import jax
import jax.numpy as jnp
from jax import lax
from jax.sharding import PartitionSpec as P

HEADS = 16


def layer_norm(values, gain, bias):
    average = jnp.mean(values, -1, keepdims=True)
    centred = values - average
    spread = jnp.mean(centred * centred, -1, keepdims=True)
    return centred * lax.rsqrt(spread + 1e-05) * gain + bias


def key_places(columns, shard_span, tok_rows, block_place):
    device = columns // shard_span
    offset = columns % shard_span
    owners = jnp.arange(block_place.shape[0], dtype=jnp.int32)
    placed = jnp.sum(jnp.where(device[:, None] == owners[None, :], block_place[None, :], 0), 1)
    return jnp.where(offset < tok_rows, placed * tok_rows + offset, -1)


def exp_scores(queries, shard_keys, self_score, query_places, places, score_scale):
    scores = (
        jnp.einsum("sqhd,skhd->shqk", queries, shard_keys, preferred_element_type=jnp.float32)
        * score_scale
    )
    allowed = places[None, None, None, :] <= query_places[None, None, :, None]
    return jnp.exp(jnp.where(allowed, scores - self_score[:, :, :, None], -1e30))


def score_grads(
    queries, scaled_grad, keys, values, self_score, correction, query_places, places, score_scale
):
    weights = exp_scores(queries, keys, self_score, query_places, places, score_scale)
    grad_weights = jnp.einsum(
        "sqhd,skhd->shqk", scaled_grad, values, preferred_element_type=jnp.float32
    )
    return (weights, weights * (grad_weights - correction[:, :, :, None]))


def on_device(
    tokens,
    gain_one,
    bias_one,
    w_qkv,
    w_out,
    gain_two,
    bias_two,
    w_in,
    w_down,
    mem_keys,
    mem_values,
    continues,
    block_place,
    cotangent,
):
    seq_count, tok_rows, model_width = tokens.shape
    head_count = HEADS
    head_dim = model_width // head_count
    score_scale = head_dim ** (-0.5)
    blocks = lax.axis_size("blk")
    my_block = lax.axis_index("blk")
    my_group = lax.axis_index("grp")
    my_place = block_place[my_block]
    row_count = seq_count * tok_rows
    gain_one_f = gain_one.astype(jnp.float32)
    bias_one_f = bias_one.astype(jnp.float32)
    gain_two_f = gain_two.astype(jnp.float32)
    bias_two_f = bias_two.astype(jnp.float32)
    hidden = tokens.astype(jnp.float32)
    normed_one = (
        layer_norm(hidden, gain_one_f, bias_one_f)
        .astype(jnp.bfloat16)
        .reshape(row_count, model_width)
    )
    projected = jnp.dot(normed_one, w_qkv, preferred_element_type=jnp.float32)
    queries = (
        projected[:, :model_width]
        .astype(jnp.bfloat16)
        .reshape(seq_count, tok_rows, head_count, head_dim)
    )
    key_rows = (
        projected[:, model_width : 2 * model_width]
        .astype(jnp.bfloat16)
        .reshape(seq_count, tok_rows, model_width)
    )
    value_rows = (
        projected[:, 2 * model_width :]
        .astype(jnp.bfloat16)
        .reshape(seq_count, tok_rows, model_width)
    )
    banks_keys, banks_values = (
        lax.all_gather(mem_keys, "grp", axis=0, tiled=True),
        lax.all_gather(mem_values, "grp", axis=0, tiled=True),
    )
    chosen = lax.dynamic_slice_in_dim(continues, my_group * seq_count, seq_count)
    memory_keys = jnp.take(banks_keys, chosen, axis=0)
    memory_values = jnp.take(banks_values, chosen, axis=0)
    shard_span = tok_rows + memory_keys.shape[1]
    cached_span = shard_span - tok_rows
    cached_places = jnp.full((cached_span,), -1, jnp.int32)
    bundle = jnp.stack(
        [
            jnp.concatenate([key_rows, memory_keys], 1),
            jnp.concatenate([value_rows, memory_values], 1),
        ],
        1,
    )
    own_keys = key_rows.reshape(seq_count, tok_rows, head_count, head_dim).astype(jnp.float32)
    queries_f = queries.astype(jnp.float32)
    self_score = jnp.transpose(jnp.sum(queries_f * own_keys, -1), (0, 2, 1)) * score_scale
    query_places = my_place * tok_rows + jnp.arange(tok_rows, dtype=jnp.int32)

    def split_shard(shard_rows):
        shard_keys = shard_rows[:, 0].reshape(seq_count, shard_span, head_count, head_dim)
        shard_values = shard_rows[:, 1].reshape(seq_count, shard_span, head_count, head_dim)
        return (shard_keys, shard_values)

    def accumulate(state, keys, values, places):
        weights = exp_scores(queries, keys, self_score, query_places, places, score_scale)
        totals = state[0] + jnp.sum(weights, -1)
        summed = state[1] + jnp.einsum(
            "shqk,skhd->sqhd",
            weights.astype(jnp.bfloat16),
            values,
            preferred_element_type=jnp.float32,
        )
        return (totals, summed)

    def forward_shard(carried, shard_rows, first_col):
        device = first_col // shard_span
        later = block_place[device] > my_place
        shard_keys, shard_values = split_shard(shard_rows)

        def forward_cached_only(state):
            return accumulate(
                state, shard_keys[:, tok_rows:], shard_values[:, tok_rows:], cached_places
            )

        def forward_whole(state):
            places = key_places(
                first_col + jnp.arange(shard_span, dtype=jnp.int32),
                shard_span,
                tok_rows,
                block_place,
            )
            return accumulate(state, shard_keys, shard_values, places)

        return lax.cond(later, forward_cached_only, forward_whole, carried)

    start_state = (
        jnp.zeros((seq_count, head_count, tok_rows), jnp.float32),
        jnp.zeros((seq_count, tok_rows, head_count, head_dim), jnp.float32),
    )
    piece_rows = lax.all_gather(bundle, "blk", axis=2, tiled=True)

    def single(shard_index, inner_state):
        shard_rows = lax.dynamic_slice_in_dim(piece_rows, shard_index * shard_span, shard_span, 2)
        return forward_shard(inner_state, shard_rows, shard_index * shard_span)

    totals, summed = lax.fori_loop(0, piece_rows.shape[2] // shard_span, single, start_state)
    totals_rows = jnp.transpose(totals, (0, 2, 1))[:, :, :, None]
    attended_f = summed / totals_rows
    attended = attended_f.astype(jnp.bfloat16).reshape(row_count, model_width)
    branch = jnp.dot(attended, w_out, preferred_element_type=jnp.float32)
    residual = hidden + branch.reshape(seq_count, tok_rows, model_width)
    normed_two = (
        layer_norm(residual, gain_two_f, bias_two_f)
        .astype(jnp.bfloat16)
        .reshape(row_count, model_width)
    )
    inner_pre = jnp.dot(normed_two, w_in, preferred_element_type=jnp.float32)
    activated = jax.nn.gelu(inner_pre).astype(jnp.bfloat16)
    mixed = (
        residual
        + jnp.dot(activated, w_down, preferred_element_type=jnp.float32).reshape(
            seq_count, tok_rows, model_width
        )
    ).astype(jnp.bfloat16)
    grad_rows = cotangent.reshape(row_count, model_width)
    grad_down = jnp.einsum("rf,rd->fd", activated, grad_rows, preferred_element_type=jnp.float32)
    grad_act = jnp.einsum("rd,fd->rf", grad_rows, w_down, preferred_element_type=jnp.float32)
    gelu_pull = jax.vjp(jax.nn.gelu, inner_pre)[1]
    grad_inner = gelu_pull(grad_act)[0].astype(jnp.bfloat16)
    grad_in = jnp.einsum("rd,rf->df", normed_two, grad_inner, preferred_element_type=jnp.float32)
    grad_normed_two = jnp.einsum("rf,df->rd", grad_inner, w_in, preferred_element_type=jnp.float32)
    norm_two_pull = jax.vjp(layer_norm, residual, gain_two_f, bias_two_f)[1]
    grad_res_part, grad_gain_two, grad_bias_two = norm_two_pull(
        grad_normed_two.reshape(seq_count, tok_rows, model_width)
    )
    grad_residual = cotangent.astype(jnp.float32) + grad_res_part
    grad_branch = grad_residual.reshape(row_count, model_width).astype(jnp.bfloat16)
    grad_out = jnp.einsum("rd,re->de", attended, grad_branch, preferred_element_type=jnp.float32)
    grad_attended = jnp.einsum(
        "re,de->rd", grad_branch, w_out, preferred_element_type=jnp.float32
    ).astype(jnp.bfloat16)
    grad_attended = grad_attended.reshape(seq_count, tok_rows, head_count, head_dim).astype(
        jnp.float32
    )
    scaled_grad = (grad_attended / totals_rows).astype(jnp.bfloat16)
    correction = jnp.transpose(
        jnp.sum(grad_attended * attended_f, -1) / totals_rows[:, :, :, 0], (0, 2, 1)
    )
    source = lax.all_gather(bundle, "blk", axis=2, tiled=True)

    def backward_shard(shard_index, carried):
        shard_rows = lax.dynamic_slice_in_dim(source, shard_index * shard_span, shard_span, 2)
        shard_keys, shard_values = split_shard(shard_rows)
        later = block_place[shard_index] > my_place

        def backward_cached_only(state):
            weights, grad_scores = score_grads(
                queries,
                scaled_grad,
                shard_keys[:, tok_rows:],
                shard_values[:, tok_rows:],
                self_score,
                correction,
                query_places,
                cached_places,
                score_scale,
            )
            grad_queries = state[0] + jnp.einsum(
                "shqk,skhd->sqhd",
                grad_scores.astype(jnp.bfloat16),
                shard_keys[:, tok_rows:],
                preferred_element_type=jnp.float32,
            )
            return (grad_queries, state[1] + jnp.sum(grad_scores, -1)) + tuple(state[2:])

        def backward_whole(state):
            places = key_places(
                shard_index * shard_span + jnp.arange(shard_span, dtype=jnp.int32),
                shard_span,
                tok_rows,
                block_place,
            )
            weights, grad_scores = score_grads(
                queries,
                scaled_grad,
                shard_keys,
                shard_values,
                self_score,
                correction,
                query_places,
                places,
                score_scale,
            )
            diag_sum = state[1] + jnp.sum(grad_scores, -1)
            rounded = grad_scores.astype(jnp.bfloat16)
            grad_queries = state[0] + jnp.einsum(
                "shqk,skhd->sqhd", rounded, shard_keys, preferred_element_type=jnp.float32
            )
            key_part = (
                jnp.einsum(
                    "shqk,sqhd->skhd",
                    rounded[..., :tok_rows],
                    queries,
                    preferred_element_type=jnp.float32,
                )
                * score_scale
            )
            value_part = jnp.einsum(
                "shqk,sqhd->skhd",
                weights[..., :tok_rows].astype(jnp.bfloat16),
                scaled_grad,
                preferred_element_type=jnp.float32,
            )
            update = jnp.stack(
                [
                    key_part.reshape(seq_count, tok_rows, model_width),
                    value_part.reshape(seq_count, tok_rows, model_width),
                ],
                1,
            )
            term = lax.dynamic_update_slice_in_dim(state[2], update, shard_index * tok_rows, 2)
            return (grad_queries, diag_sum, term)

        return lax.cond(later, backward_cached_only, backward_whole, carried)

    back_state = (
        jnp.zeros((seq_count, tok_rows, head_count, head_dim), jnp.float32),
        jnp.zeros((seq_count, head_count, tok_rows), jnp.float32),
    )
    back_state = back_state + (
        jnp.zeros((seq_count, 2, blocks * tok_rows, model_width), jnp.float32),
    )
    back_result = lax.fori_loop(0, blocks, backward_shard, back_state)
    grad_queries, diag_sum = (back_result[0], back_result[1])
    diag_rows = jnp.transpose(diag_sum, (0, 2, 1))[:, :, :, None] * score_scale
    self_fix = (diag_rows * queries_f).reshape(seq_count, tok_rows, model_width)
    grad_q = (
        (grad_queries * score_scale - diag_rows * own_keys)
        .astype(jnp.bfloat16)
        .reshape(row_count, model_width)
    )
    term = back_result[2]
    own_slot = lax.dynamic_slice_in_dim(term, my_block * tok_rows, tok_rows, 2)
    own_slot = own_slot.at[:, 0].add(-self_fix)
    term = lax.dynamic_update_slice_in_dim(term, own_slot, my_block * tok_rows, 2)
    summed_kv = lax.psum_scatter(term.astype(jnp.bfloat16), "blk", scatter_dimension=2, tiled=True)
    grad_k = summed_kv[:, 0].reshape(row_count, model_width)
    grad_v = summed_kv[:, 1].reshape(row_count, model_width)
    grad_proj = jnp.concatenate([grad_q, grad_k, grad_v], 1)
    grad_qkv = jnp.einsum("rd,re->de", normed_one, grad_proj, preferred_element_type=jnp.float32)
    grad_normed_one = jnp.einsum("re,de->rd", grad_proj, w_qkv, preferred_element_type=jnp.float32)
    norm_one_pull = jax.vjp(layer_norm, hidden, gain_one_f, bias_one_f)[1]
    grad_hidden_part, grad_gain_one, grad_bias_one = norm_one_pull(
        grad_normed_one.reshape(seq_count, tok_rows, model_width)
    )
    grad_tokens = grad_residual + grad_hidden_part
    gradients = (
        grad_gain_one,
        grad_bias_one,
        grad_qkv,
        grad_out,
        grad_gain_two,
        grad_bias_two,
        grad_in,
        grad_down,
    )
    packed = jnp.concatenate([gradient.reshape(blocks, -1) for gradient in gradients], 1)
    flat_row = (
        lax.psum_scatter(packed.astype(jnp.bfloat16), "blk", scatter_dimension=0, tiled=True)
        .astype(jnp.float32)
        .reshape(-1)
    )
    flat_row = lax.psum(flat_row.astype(jnp.bfloat16), "grp").astype(jnp.float32)
    pieces = []
    offset = 0
    for gradient in gradients:
        entries = gradient.size // blocks
        piece_shape = (gradient.shape[0] // blocks,) + gradient.shape[1:]
        pieces.append(flat_row[offset : offset + entries].reshape(piece_shape))
        offset = offset + entries
    return (
        mixed,
        grad_tokens,
        pieces[0],
        pieces[1],
        pieces[2],
        pieces[3],
        pieces[4],
        pieces[5],
        pieces[6],
        pieces[7],
    )


def solution(mesh):
    in_specs = (
        P("grp", "blk", None),
        P(),
        P(),
        P(),
        P(),
        P(),
        P(),
        P(),
        P(),
        P("grp", "blk", None),
        P("grp", "blk", None),
        P(),
        P(),
        P("grp", "blk", None),
    )
    out_specs = (
        P("grp", "blk", None),
        P("grp", "blk", None),
        P("blk"),
        P("blk"),
        P("blk", None),
        P("blk", None),
        P("blk"),
        P("blk"),
        P("blk", None),
        P("blk", None),
    )
    return jax.shard_map(
        on_device, mesh=mesh, in_specs=in_specs, out_specs=out_specs, check_vma=False
    )
```

profile of v0, /device:TPU:0, one launch (start us, length us, event | category | flops | bytes accessed | tf_op | source)
XLA Modules:
  0.0 1209.1 jit_solution(14688504417078308679)
XLA Ops:
  21.5 38.0 %all-gather.4.cloned.1.call-done = bf16[16,128,1024]{2,1,0:T(8,128)(2,1)} async-done(((bf16[2,128,1024]{2,1,0:T(8,128)(2,1)}), bf16[16,128,1024]{2,1,0:T(8,128)(2,1)}) %all-gather.4.cloned.1.call-update) | async-done | bytes 4194320 | tf_op jit(solution)/shard_map/all_gather | solution.py:95
  62.3 44.7 %all-gather.6.cloned.1.call-done = bf16[16,128,1024]{2,1,0:T(8,128)(2,1)} async-done(((bf16[2,128,1024]{2,1,0:T(8,128)(2,1)}), bf16[16,128,1024]{2,1,0:T(8,128)(2,1)}) %all-gather.6.cloned.1.call-update) | async-done | bytes 4194320 | tf_op jit(solution)/shard_map/all_gather | solution.py:96
  123.9 8.4 fusion.84
  132.3 68.8 %all-gather.8.cloned.1.call-done = bf16[2,2,1024,1024]{3,2,0,1:T(8,128)(2,1)} async-done(((bf16[2,2,256,1024]{3,2,0,1:T(8,128)(2,1)}), bf16[2,2,1024,1024]{3,2,0,1:T(8,128)(2,1)}) %all-gather.8.cloned.1.call-update) | async-done | bytes 8388624 | tf_op jit(solution)/shard_map/all_gather | solution.py:157
  201.2 11.4 copy.83
  213.7 39.0 %while.37 = (s32[]{:T(128)}, f32[2,16,128]{2,1,0:T(8,128)S(1)}, f32[2,128,16,64]{1,3,2,0:T(8,128)}, s32[4]{0:T(128)S(1)}, s32[]{:T(128)}, /*index=5*/bf16[2,2,10...) while((s32[]{:T(128)}, f32[2,16,128]{2,1,0:T(8,128)S(1)}, ...), condition=%wide.region_9.11_spmd.clone, body=%wide.region_3.10_spmd.clone.sunk | while | flops 277130144 | bytes 17505892 | solution.py:163
  227.5 6.6 conditional.6
  245.9 6.6 conditional.6
  259.5 10.5 fusion.41
  293.7 63.1 %while.38 = (s32[]{:T(128)}, f32[2,128,16,64]{1,3,2,0:T(8,128)}, f32[2,16,128]{2,1,0:T(8,128)S(1)}, f32[2,2,512,1024]{2,3,0,1:T(8,128)}, s32[4]{0:T(128)S(1)}, /...) while((s32[]{:T(128)}, f32[2,128,16,64]{1,3,2,0:T(8,128)}, ...), condition=%wide.region_21.23_spmd.clone, body=%wide.region_15.22_spmd.clone.sunk | while | flops 545303424 | bytes 55746164 | solution.py:290
  298.3 12.8 %conditional.7 = (f32[2,128,16,64]{1,3,2,0:T(8,128)}, f32[2,16,128]{2,1,0:T(8,128)S(1)}, f32[2,2,512,1024]{2,3,0,1:T(8,128)}) conditional(s32[]{:T(128)} %convert_element_type.222, (s32[]{:T(128)}, s32[4]{0:T(128)S(1)}, s32[128]{0:T(128)S(1)}, bf16[2,128,16,64]{1,3,2,0:T(8,128)(2,1)}, bf16[2,256,16,64]{1,3,2,0:T(8,128)(2,1)S(1)}, ...), branch_computations={%region_16.19_spmd, %region_19.21_spmd} | conditional | flops 545303296 | bytes 51550912 | solution.py:281
  315.8 12.8 %conditional.7 = (f32[2,128,16,64]{1,3,2,0:T(8,128)}, f32[2,16,128]{2,1,0:T(8,128)S(1)}, f32[2,2,512,1024]{2,3,0,1:T(8,128)}) conditional(s32[]{:T(128)} %convert_element_type.222, (s32[]{:T(128)}, s32[4]{0:T(128)S(1)}, s32[128]{0:T(128)S(1)}, bf16[2,128,16,64]{1,3,2,0:T(8,128)(2,1)}, bf16[2,256,16,64]{1,3,2,0:T(8,128)(2,1)S(1)}, ...), branch_computations={%region_16.19_spmd, %region_19.21_spmd} | conditional | flops 545303296 | bytes 51550912 | solution.py:281
  344.1 12.7 %conditional.7 = (f32[2,128,16,64]{1,3,2,0:T(8,128)}, f32[2,16,128]{2,1,0:T(8,128)S(1)}, f32[2,2,512,1024]{2,3,0,1:T(8,128)}) conditional(s32[]{:T(128)} %convert_element_type.222, (s32[]{:T(128)}, s32[4]{0:T(128)S(1)}, s32[128]{0:T(128)S(1)}, bf16[2,128,16,64]{1,3,2,0:T(8,128)(2,1)}, bf16[2,256,16,64]{1,3,2,0:T(8,128)(2,1)S(1)}, ...), branch_computations={%region_16.19_spmd, %region_19.21_spmd} | conditional | flops 545303296 | bytes 51550912 | solution.py:281
  356.8 8.7 copy.100
  383.2 7.6 convolution_convert_fusion.1
  390.9 13.4 %reshape.436 = bf16[4,1048576]{1,0:T(4,128)(2,1)} reshape(bf16[1024,4096]{1,0:T(8,128)(2,1)} %convolution_convert_fusion.1) | data formatting | bytes 16777216 | tf_op jit(solution)/shard_map/reshape | solution.py:324
  404.2 8.7 convolution_convert_fusion
  413.0 13.2 %reshape.437 = bf16[4,1048576]{1,0:T(4,128)(2,1)} reshape(bf16[4096,1024]{1,0:T(8,128)(2,1)} %convolution_convert_fusion) | data formatting | bytes 16777216 | tf_op jit(solution)/shard_map/reshape | solution.py:324
  426.2 10.4 reduce-scatter.2.cloned.1.call-done
  451.2 10.3 reshape.431
  462.2 8.6 constant_dynamic-update-slice_fusion.5
  484.1 442.1 %all-reduce.6.cloned.1.call-done = bf16[4,3146752]{1,0:T(4,128)(2,1)} async-done(((bf16[4,3146752]{1,0:T(4,128)(2,1)}), bf16[4,3146752]{1,0:T(4,128)(2,1)}) %all-reduce.6.cloned.1.call-update) | async-done | bytes 25174032
  926.3 114.5 %dynamic-slice_reduce_fusion = bf16[3146752]{0:T(1024)(128)(2,1)} fusion(bf16[4,3146752]{1,0:T(4,128)(2,1)} %all-reduce.6.cloned.1.call-done, u32[]{:T(128)} %bitcast.39), kind=kLoop, calls=%fused_computation.71 | loop fusion | bytes 12587012 | tf_op jit(solution)/shard_map/convert_element_type | solution.py:330
  1043.4 135.1 %all-reduce.4.cloned.1.call-done = bf16[3146752]{0:T(1024)(128)(2,1)} async-done(((bf16[3146752]{0:T(1024)(128)(2,1)}), bf16[3146752]{0:T(1024)(128)(2,1)}) %all-reduce.4.cloned.1.call-update) | async-done | bytes 6293520 | tf_op jit(solution)/shard_map/psum | solution.py:330
  (307 shorter events, 244.7 us)
Async XLA Ops:
  7.2 249.8 %copy-start = (bf16[1024,1024]{1,0:T(8,128)(2,1)S(1)}, bf16[1024,1024]{1,0:T(8,128)(2,1)}, u32[]{:S(2)}) copy-start(bf16[1024,1024]{1,0:T(8,128)(2,1)} %param.30) | copy-start | bytes 6291460
  7.2 52.3 %all-gather.4.cloned.1.call-start = ((), (), s32[]{:S(2)}) async-start(), calls=%async_computation.1 | async-start | bytes 4718592 | tf_op jit(solution)/shard_map/all_gather | solution.py:95
  7.9 99.1 %all-gather.6.cloned.1.call-start = ((), (), s32[]{:S(2)}) async-start(), calls=%async_computation.2 | async-start | bytes 4718592 | tf_op jit(solution)/shard_map/all_gather | solution.py:96
  8.7 192.5 %all-gather.8.cloned.1.call-start = ((), (), s32[]{:S(2)}) async-start(), calls=%async_computation.3 | async-start | bytes 10485760 | tf_op jit(solution)/shard_map/all_gather | solution.py:157
  21.5 93.2 %copy-start.16 = (bf16[256,1024]{1,0:T(8,128)(2,1)}, bf16[256,1024]{1,0:T(8,128)(2,1)S(1)}, u32[]{:S(2)}) copy-start(bf16[256,1024]{1,0:T(8,128)(2,1)S(1)} %get-tuple-element.793) | copy-start | bytes 1572868
  114.7 321.8 %reduce-scatter.2.cloned.1.call-start = ((), (), s32[]{:S(2)}) async-start(), calls=%async_computation.4 | async-start | bytes 5242880 | tf_op jit(solution)/shard_map/reduce_scatter | solution.py:303
  114.9 7.5 copy-start.28
  115.0 8.9 copy-start.35
  115.0 8.9 copy-start.36
  120.4 11.9 copy-start.8
  252.7 6.8 copy-start.38
  256.9 13.1 %slice-start.4 = ((s8[8388608]{0:T(1024)(128)(4,1)}), s8[4194304]{0:T(1024)(128)(4,1)S(1)}, s32[]{:S(2)}) async-start(s8[8388608]{0:T(1024)(128)(4,1)} %bitcast.170), calls=%async_computation.11 | async-start | bytes 8388608
  256.9 15.9 %slice-start.6 = ((s8[8388608]{0:T(1024)(128)(4,1)}), s8[4194304]{0:T(1024)(128)(4,1)S(1)}, s32[]{:S(2)}) async-start(s8[8388608]{0:T(1024)(128)(4,1)} %bitcast.172), calls=%async_computation.13 | async-start | bytes 8388608
  259.5 10.6 copy-start.20
  259.5 10.6 slice-start.5
  259.5 13.3 %slice-start.7 = ((s8[8388608]{0:T(1024)(128)(4,1)}), s8[4194304]{0:T(1024)(128)(4,1)S(1)}, s32[]{:S(2)}) async-start(s8[8388608]{0:T(1024)(128)(4,1)} %bitcast.172), calls=%async_computation.14 | async-start | bytes 8388608
  375.1 551.2 %all-reduce.6.cloned.1.call-start = ((), (), s32[]{:S(2)}) async-start(), calls=%async_computation.6 | async-start | bytes 50348032
  390.9 13.4 %copy-start.18 = (bf16[2,128,1024]{2,1,0:T(8,128)(2,1)S(1)}, bf16[2,128,1024]{2,1,0:T(8,128)(2,1)}, u32[]{:S(2)}) copy-start(bf16[2,128,1024]{2,1,0:T(8,128)(2,1)} %param.39) | copy-start | bytes 1572868
  426.2 13.6 %copy-start.23 = (bf16[128,8,2,128]{3,1,2,0:T(8,128)(2,1)S(1)}, bf16[128,8,2,128]{3,1,2,0:T(8,128)(2,1)}, u32[]{:S(2)}) copy-start(bf16[128,8,2,128]{3,1,2,0:T(8,128)(2,1)} %copy.124) | copy-start | bytes 1572868
  461.6 12.2 %slice-start = ((s8[8388608]{0:T(1024)(128)(4,1)}), s8[4194304]{0:T(1024)(128)(4,1)S(1)}, s32[]{:S(2)}) async-start(s8[8388608]{0:T(1024)(128)(4,1)} %bitcast.140), calls=%async_computation.7 | async-start | bytes 8388608
  462.2 8.7 copy-start.10
  462.2 11.6 slice-start.1
  470.8 7.5 slice-start.2
  482.9 695.6 %all-reduce.4.cloned.1.call-start = ((), (), s32[]{:S(2)}) async-start(), calls=%async_computation.5 | async-start | bytes 12587008 | tf_op jit(solution)/shard_map/psum | solution.py:330
  (35 other events, 121.7 us)
Sparse Core Ops, SparseCore 0:
  9.6 49.8 all-gather.3
  61.1 45.8 all-gather.5
  114.8 86.3 all-gather.7
  375.2 61.2 reduce-scatter.1
  483.0 443.1 all-reduce.5
  1040.9 137.5 all-reduce.3
where the time goes:
time: 1220 us; the launch traced here: 1210 us
  waiting for transfers between devices  741 us (61%)
  local copies, waits for them, and re-layouts  276 us (23%)
  matrix products  124 us (10%)
  other arithmetic  40.5 us (3%)
  between operations  15.9 us (1%)
    unnamed x7, waiting for transfers between devices  444 us
    psum x1, waiting for transfers between devices, on_device(): lax.psum(flat_row.astype(jnp.bfloat16), 'grp').astype(jnp.float32)  135 us
    convert_element_type x1, local copies, waits for them, and re-layouts, on_device(): flat_row.astype(jnp.bfloat16)  114 us
    all_gather x1, waiting for transfers between devices, on_device(): piece_rows = lax.all_gather(bundle, 'blk', axis=2, tiled=True)  68.8 us
    all_gather x1, waiting for transfers between devices, on_device(): lax.all_gather(mem_values, 'grp', axis=0, tiled=True)  44.7 us
    reshape x8, local copies, waits for them, and re-layouts, on_device(): gradient.reshape(blocks, -1)  39.9 us
    all_gather x1, waiting for transfers between devices, on_device(): lax.all_gather(mem_keys, 'grp', axis=0, tiled=True)  38 us
    unnamed x102, local copies, waits for them, and re-layouts  36.7 us
  transfers between devices with their start and end apart: 6, of which 6 were waited for; matrix products, arithmetic and copies ran while one was open for 7% of the time, Pallas kernels for 0%

commit v1 on v0

v1 whole, which is shorter than its diff:
```python
import jax
import jax.numpy as jnp
from jax import lax
from jax.sharding import PartitionSpec as P

HEADS = 16
F32 = jnp.float32
BF16 = jnp.bfloat16


def layer_norm(values, gain, bias):
    average = jnp.mean(values, -1, keepdims=True)
    centred = values - average
    spread = jnp.mean(centred * centred, -1, keepdims=True)
    return centred * lax.rsqrt(spread + 1e-05) * gain + bias


def norm_back(values, gain, grad):
    average = jnp.mean(values, -1, keepdims=True)
    centred = values - average
    spread = jnp.mean(centred * centred, -1, keepdims=True)
    scale = lax.rsqrt(spread + 1e-05)
    unit = centred * scale
    scaled = grad * gain
    mean_one = jnp.mean(scaled, -1, keepdims=True)
    mean_two = jnp.mean(scaled * unit, -1, keepdims=True)
    return (
        scale * (scaled - mean_one - unit * mean_two),
        jnp.sum(grad * unit, 0),
        jnp.sum(grad, 0),
    )


def swap(values, axis, mask):
    size = lax.axis_size(axis)
    return lax.ppermute(values, axis, [(i, i ^ mask) for i in range(size)])


def pick(values, index, dim=0):
    return lax.dynamic_index_in_dim(values, index, dim, keepdims=False)


def dot(left, right, dims):
    return lax.dot_general(left, right, ((dims[0], dims[1]), ((), ())), preferred_element_type=F32)


def fetch_banks(mem_keys, mem_values, continues, groups, my_group, blocks, my_block):
    seq_count, rows, width = mem_keys.shape
    core, chips = my_group % 2, groups // 2
    my_chip = my_group // 2
    kept = jnp.where(core == 0, mem_keys, mem_values)
    sent = jnp.where(core == 0, mem_values, mem_keys)
    came = swap(sent, "grp", 1)
    pair = jnp.where(core == 0, jnp.stack([kept, came]), jnp.stack([came, kept]))
    per_chip = 2 * seq_count
    pair = pair.reshape(per_chip, chips, rows // chips, width)
    parts = [pick(pair, my_chip, 1)]
    for mask in range(1, chips):
        parts.append(swap(pick(pair, my_chip ^ mask, 1), "grp", 2 * mask))
    order = my_chip ^ jnp.arange(chips)
    every = jnp.take(jnp.stack(parts), order, axis=0).reshape(
        chips * per_chip, rows // chips, width
    )
    def needed(chip):
        banks = lax.dynamic_slice_in_dim(continues, chip * per_chip, per_chip)
        return jnp.take(every, banks, axis=0)

    parts = [needed(my_chip)]
    for mask in range(1, chips):
        parts.append(swap(needed(my_chip ^ mask), "grp", 2 * mask))
    held = jnp.stack(parts, 1).reshape(2, seq_count, rows, width)
    kept = pick(held, core)
    came = swap(pick(held, 1 - core), "grp", 1)
    keys = jnp.where(core == 0, kept, came)
    values = jnp.where(core == 0, came, kept)
    both = jnp.stack([keys, values]).reshape(2, seq_count, rows, blocks, width // blocks)
    parts = [pick(both, my_block, 3)]
    for mask in range(1, blocks):
        parts.append(swap(pick(both, my_block ^ mask, 3), "blk", mask))
    whole = jnp.stack(parts, 2).reshape(2, seq_count, blocks * rows, width // blocks)
    return whole[0], whole[1]


def reduce_blocks(values, blocks, my_block):
    bits = blocks.bit_length() - 1
    half = values.shape[1] // 2
    results = []
    for part in range(2):
        held = values[:, :half] if part == 0 else values[:, half:]
        order = range(bits) if part == 0 else reversed(range(bits))
        left = list(range(bits))
        held = held.reshape((2,) * bits + held.shape[1:])
        for bit in order:
            dim = left.index(bit)
            axis = len(left) - 1 - dim
            mine = (my_block >> bit) & 1
            sent = pick(held, 1 - mine, axis)
            came = swap(sent, "blk", 1 << bit)
            held = (pick(held, mine, axis).astype(F32) + came.astype(F32)).astype(BF16)
            left.remove(bit)
        results.append(held)
    return results


def reduce_groups(values, groups, my_group):
    bits = groups.bit_length() - 1
    rows = values.shape[0]
    low = (my_group >> 1) & 1
    halves = values.reshape((2, rows // 2) + values.shape[1:])
    came = swap(pick(halves, 1 - low), "grp", 2)
    held = (pick(halves, low).astype(F32) + came.astype(F32)).astype(BF16)
    for bit in range(2, bits):
        came = swap(held, "grp", 1 << bit)
        held = (held.astype(F32) + came.astype(F32)).astype(BF16)
    came = swap(held, "grp", 2)
    return jnp.where(low == 0, jnp.stack([held, came]), jnp.stack([came, held])).reshape(
        values.shape
    )


def join_cores(values, core):
    came = swap(values, "grp", 1)
    return jnp.where(core == 0, jnp.stack([values, came]), jnp.stack([came, values]))


def on_device(
    tokens,
    gain_one,
    bias_one,
    w_qkv,
    w_out,
    gain_two,
    bias_two,
    w_in,
    w_down,
    mem_keys,
    mem_values,
    continues,
    block_place,
    cotangent,
):
    seq_count, tok_rows, width = tokens.shape
    hidden_width = w_in.shape[1]
    blocks, groups = lax.axis_size("blk"), lax.axis_size("grp")
    my_block, my_group = lax.axis_index("blk"), lax.axis_index("grp")
    core = my_group % 2
    heads = HEADS // blocks
    part = width // blocks
    head_dim = width // HEADS
    score_scale = head_dim ** (-0.5)
    rows = seq_count * tok_rows
    seg_rows = blocks * tok_rows
    gain_one_f, bias_one_f = gain_one.astype(F32), bias_one.astype(F32)
    gain_two_f, bias_two_f = gain_two.astype(F32), bias_two.astype(F32)
    hidden = tokens.reshape(rows, width).astype(F32)

    pieces = [tokens] + [swap(tokens, "blk", mask) for mask in range(1, blocks)]
    places = [block_place[my_block ^ mask] for mask in range(blocks)]
    mem_k, mem_v = fetch_banks(
        mem_keys, mem_values, continues, groups, my_group, blocks, my_block
    )

    def to_positions(parts):
        masks = jnp.stack(places)
        order = jnp.argsort(masks)
        stacked = jnp.take(jnp.stack(parts, 1), order, axis=1)
        return stacked.reshape((seq_count, seg_rows) + parts[0].shape[2:])

    def from_positions(values, mask):
        return pick(
            values.reshape((seq_count, blocks, tok_rows) + values.shape[2:]), places[mask], 1
        )

    def from_heads(values, dim):
        parts = [from_positions(values, 0)]
        for mask in range(1, blocks):
            parts.append(swap(from_positions(values, mask), "blk", mask))
        order = my_block ^ jnp.arange(blocks)
        stacked = jnp.take(jnp.stack(parts, 0), order, axis=0)
        return jnp.moveaxis(stacked, 0, -2)

    all_rows = to_positions(pieces)
    normed_all = (
        layer_norm(all_rows.astype(F32), gain_one_f, bias_one_f)
        .astype(BF16)
        .reshape(seq_count * seg_rows, width)
    )
    w_heads = pick(w_qkv.reshape(width, 3, blocks, part), my_block, 2).reshape(width, 3 * part)
    projected = dot(normed_all, w_heads, ((1,), (0,))).astype(BF16)
    projected = projected.reshape(seq_count, seg_rows, 3, heads, head_dim)
    queries, keys, values = projected[:, :, 0], projected[:, :, 1], projected[:, :, 2]
    mem_k = mem_k.reshape(seq_count, -1, heads, head_dim)
    mem_v = mem_v.reshape(seq_count, -1, heads, head_dim)
    self_score = (
        jnp.transpose(jnp.sum(queries.astype(F32) * keys.astype(F32), -1), (0, 2, 1)) * score_scale
    )
    causal = jnp.arange(seg_rows)[None, :] <= jnp.arange(seg_rows)[:, None]

    def weights_of(some_keys, masked):
        scores = (
            jnp.einsum("sqhd,skhd->shqk", queries, some_keys, preferred_element_type=F32)
            * score_scale
        )
        scores = scores - self_score[:, :, :, None]
        if masked:
            scores = jnp.where(causal[None, None], scores, -1e30)
        return jnp.exp(scores)

    own_w = weights_of(keys, True)
    mem_w = weights_of(mem_k, False)
    totals = jnp.sum(own_w, -1) + jnp.sum(mem_w, -1)
    summed = jnp.einsum(
        "shqk,skhd->sqhd", own_w.astype(BF16), values, preferred_element_type=F32
    ) + jnp.einsum("shqk,skhd->sqhd", mem_w.astype(BF16), mem_v, preferred_element_type=F32)
    totals_rows = jnp.transpose(totals, (0, 2, 1))[:, :, :, None]
    attended_f = summed / totals_rows
    attended_heads = attended_f.astype(BF16).reshape(seq_count, seg_rows, part)
    attended = from_heads(attended_heads, 0).reshape(rows, width)

    residual = hidden + dot(attended, w_out, ((1,), (0,)))
    normed_two = layer_norm(residual, gain_two_f, bias_two_f).astype(BF16)
    inner = dot(normed_two, w_in, ((1,), (0,)))
    activated, gelu_pull = jax.vjp(jax.nn.gelu, inner)
    activated = activated.astype(BF16)
    mixed = (residual + dot(activated, w_down, ((1,), (0,)))).astype(BF16)
    cot = cotangent.reshape(rows, width)
    grad_act = dot(cot, w_down, ((1,), (1,)))
    grad_inner = gelu_pull(grad_act)[0].astype(BF16)
    grad_normed_two = dot(grad_inner, w_in, ((1,), (1,)))
    grad_res, grad_gain_two, grad_bias_two = norm_back(residual, gain_two_f, grad_normed_two)
    grad_residual = cot.astype(F32) + grad_res
    grad_branch = grad_residual.astype(BF16)
    grad_attended = dot(grad_branch, w_out, ((1,), (1,))).astype(BF16)
    by_block = grad_attended.reshape(seq_count, tok_rows, blocks, part)
    pieces = [pick(by_block, my_block, 2)]
    for mask in range(1, blocks):
        pieces.append(swap(pick(by_block, my_block ^ mask, 2), "blk", mask))
    grad_att = to_positions(pieces).reshape(seq_count, seg_rows, heads, head_dim).astype(F32)

    scaled = (grad_att / totals_rows).astype(BF16)
    correction = jnp.transpose(
        jnp.sum(grad_att * attended_f, -1) / totals_rows[:, :, :, 0], (0, 2, 1)
    )

    def score_grads(weights, some_values):
        grad_w = jnp.einsum("sqhd,skhd->shqk", scaled, some_values, preferred_element_type=F32)
        return weights * (grad_w - correction[:, :, :, None])

    own_g = score_grads(own_w, values)
    mem_g = score_grads(mem_w, mem_v)
    diag = jnp.sum(own_g, -1) + jnp.sum(mem_g, -1)
    diag = jnp.transpose(diag, (0, 2, 1))[:, :, :, None]
    own_b, mem_b = own_g.astype(BF16), mem_g.astype(BF16)
    grad_q = score_scale * (
        jnp.einsum("shqk,skhd->sqhd", own_b, keys, preferred_element_type=F32)
        + jnp.einsum("shqk,skhd->sqhd", mem_b, mem_k, preferred_element_type=F32)
        - diag * keys.astype(F32)
    )
    grad_k = score_scale * (
        jnp.einsum("shqk,sqhd->skhd", own_b, queries, preferred_element_type=F32)
        - diag * queries.astype(F32)
    )
    grad_v = jnp.einsum("shqk,sqhd->skhd", own_w.astype(BF16), scaled, preferred_element_type=F32)
    grad_heads = (
        jnp.stack([grad_q, grad_k, grad_v], 2)
        .astype(BF16)
        .reshape(seq_count, seg_rows, 3, part)
    )
    grad_proj = from_heads(grad_heads, 0).reshape(rows, 3 * width)
    grad_normed_one = dot(grad_proj, w_qkv, ((1,), (1,)))
    grad_hid, grad_gain_one, grad_bias_one = norm_back(hidden, gain_one_f, grad_normed_one)
    grad_tokens = (grad_residual + grad_hid).reshape(seq_count, tok_rows, width)

    def both_rows(values):
        return jnp.concatenate([values, swap(values, "grp", 1)], 0)

    def column_half(values, count, whose):
        return pick(values.reshape(values.shape[0], count, 2, -1), whose, 2).reshape(
            values.shape[0], -1
        )

    def halves_of(values, count):
        return jnp.concatenate(
            [
                column_half(values, count, core),
                swap(column_half(values, count, 1 - core), "grp", 1),
            ],
            0,
        )

    cot_two = both_rows(cot)
    act_half = halves_of(activated, blocks)
    down = dot(act_half, cot_two, ((0,), (0,))).astype(BF16).reshape(blocks, -1, width)
    normed_half = halves_of(normed_two, blocks)
    inner_two = both_rows(grad_inner)
    into = dot(normed_half, inner_two, ((0,), (0,))).astype(BF16).reshape(blocks, -1, hidden_width)
    branch_two = both_rows(grad_branch)
    attended_half = halves_of(attended, blocks)
    out = dot(attended_half, branch_two, ((0,), (0,))).astype(BF16).reshape(blocks, -1, width)

    def finish(values, shape):
        pieces = reduce_blocks(values, blocks, my_block)
        joined = reduce_groups(jnp.concatenate(pieces, 0), groups, my_group)
        return join_cores(joined, core).reshape(shape).astype(F32)

    grad_down = finish(down, (hidden_width // blocks, width))
    grad_in = finish(into, (part, hidden_width))
    grad_out = finish(out, (part, width))
    heads_rows = grad_heads.reshape(seq_count * seg_rows, 3 * part)
    qkv = dot(normed_all, heads_rows, ((0,), (0,))).astype(BF16)
    qkv = qkv.reshape(blocks, 2, part // 2, 3 * part)
    came = swap(pick(qkv, 1 - core, 1), "grp", 1)
    qkv = (pick(qkv, core, 1).astype(F32) + came.astype(F32)).astype(BF16)
    pieces = [pick(qkv, my_block)]
    for mask in range(1, blocks):
        pieces.append(swap(pick(qkv, my_block ^ mask), "blk", mask))
    order = my_block ^ jnp.arange(blocks)
    qkv = jnp.take(jnp.stack(pieces), order, axis=0).reshape(blocks, part // 2, 3, part)
    qkv = jnp.transpose(qkv, (1, 2, 0, 3)).reshape(part // 2, 3 * width)
    qkv = reduce_groups(qkv, groups, my_group)
    grad_qkv = join_cores(qkv, core).reshape(part, 3 * width).astype(F32)

    vectors = jnp.stack([grad_gain_one, grad_bias_one, grad_gain_two, grad_bias_two])
    for bit in range(groups.bit_length() - 1):
        vectors = vectors + swap(vectors, "grp", 1 << bit)
    for bit in range(blocks.bit_length() - 1):
        vectors = vectors + swap(vectors, "blk", 1 << bit)
    vectors = pick(vectors.reshape(4, blocks, part), my_block, 1)
    return (
        mixed.reshape(tokens.shape),
        grad_tokens,
        vectors[0],
        vectors[1],
        grad_qkv,
        grad_out,
        vectors[2],
        vectors[3],
        grad_in,
        grad_down,
    )


def solution(mesh):
    rows = P("grp", "blk", None)
    in_specs = (rows,) + (P(),) * 8 + (rows, rows, P(), P(), rows)
    out_specs = (rows, rows) + (P("blk"),) * 2 + (P("blk", None),) * 2
    out_specs = out_specs + (P("blk"),) * 2 + (P("blk", None),) * 2
    return jax.shard_map(
        on_device, mesh=mesh, in_specs=in_specs, out_specs=out_specs, check_vma=False
    )
```

time: 1220 us -> 574 us (0.47)
  waiting for transfers between devices: 741 us -> 191 us
  local copies, waits for them, and re-layouts: 276 us -> 135 us
  starting transfers between devices: 0.9 us -> 71.8 us
  matrix products: 124 us -> 104 us
  other arithmetic: 40.5 us -> 57.5 us
    unnamed x7 -> x0, waiting for transfers between devices: 444 us -> none
    ppermute x0 -> x66, waiting for transfers between devices: none -> 191 us  [swap(): return lax.ppermute(values, axis, [(i, i ^ mask) for i in range(size)])]
    all_gather x3 -> x0, waiting for transfers between devices: 152 us -> none  [the longest x1 68.8 us: on_device(): piece_rows = lax.all_gather(bundle, 'blk', axis=2, tiled=True)]
    psum x1 -> x0, waiting for transfers between devices: 135 us -> none  [on_device(): lax.psum(flat_row.astype(jnp.bfloat16), 'grp').astype(jnp.float32)]
    convert_element_type x5 -> x1, local copies, waits for them, and re-layouts: 121 us -> 1.55 us  [on_device(): normed_all = layer_norm(all_rows.astype(F32), gain_one_f, bias_one_f).ast...]
    ppermute x0 -> x66, starting transfers between devices: none -> 71.8 us  [swap(): return lax.ppermute(values, axis, [(i, i ^ mask) for i in range(size)])]
    reshape x12 -> x6, local copies, waits for them, and re-layouts: 48 us -> 15.2 us  [the longest x2 6.68 us: column_half(): values.reshape(values.shape[0], count, 2, -1)]
    slice x15 -> x8, local copies, waits for them, and re-layouts: 34.3 us -> 8.37 us  [the longest x3 4.48 us: fetch_banks(): return (whole[0], whole[1])]
  transfers between devices with their start and end apart: 6 -> 66, of which waited for: 6 -> 33; matrix products, arithmetic and copies ran while one was open for 7% -> 50% of each run, Pallas kernels for 0% -> 0%
where the time goes in v1:
time: 574 us; the launch traced here: 569 us
  waiting for transfers between devices  191 us (33%)
  local copies, waits for them, and re-layouts  135 us (24%)
  matrix products  104 us (18%)
  starting transfers between devices  71.8 us (13%)
  other arithmetic  57.5 us (10%)
  between operations  10.3 us (2%)
    ppermute x66, waiting for transfers between devices, swap(): return lax.ppermute(values, axis, [(i, i ^ mask) for i in range(size)])  191 us
    ppermute x66, starting transfers between devices, swap(): return lax.ppermute(values, axis, [(i, i ^ mask) for i in range(size)])  71.8 us
    dot_general x12, matrix products, dot(): lax.dot_general(left, right, ((dims[0], dims[1]), ((), ())), preferred_el...  59.8 us
    unnamed x144, local copies, waits for them, and re-layouts  48.3 us
    dynamic_slice x13, local copies, waits for them, and re-layouts, pick(): return lax.dynamic_index_in_dim(values, index, dim, keepdims=False)  21.3 us
    dot_general x2, matrix products, score_grads(): jnp.einsum('sqhd,skhd->shqk', scaled, some_values, preferred_element_type...  11.5 us
  transfers between devices with their start and end apart: 66, of which 33 were waited for; matrix products, arithmetic and copies ran while one was open for 50% of the time, Pallas kernels for 0%

profile of v1, /device:TPU:0, one launch (start us, length us, event | category | flops | bytes accessed | tf_op | source)
XLA Modules:
  0.0 569.2 jit_solution(17609045703251987384)
XLA Ops:
  20.5 8.6 %copy.174 = bf16[1024,3072]{0,1:T(8,128)(2,1)} copy(bf16[1024,3072]{1,0:T(8,128)(2,1)} %param.19) | data formatting | bytes 12582912 | tf_op args[3]
  34.5 8.0 %fusion.133 = f32[256,4096]{1,0:T(8,128)} fusion(bf16[256,1024]{1,0:T(8,128)(2,1)} %bitcast.476, bf16[4096,1024]{1,0:T(8,128)(2,1)} %param.24), kind=kOutput, calls=%fused_computation.319 | convolution fusion | flops 2147483648 | bytes 13107200 | tf_op jit(solution)/shard_map/dot_general | solution.py:44
  65.0 15.2 %collective-permute-done.5 = bf16[4,32,1024]{2,1,0:T(8,128)(2,1)S(1)} collective-permute-done((bf16[4,32,1024]{2,1,0:T(8,128)(2,1)S(1)}, bf16[4,32,1024]{2,1,0:T(8,128)(2,1)S(1)}, u32[]{:S(2)}, u32[]{:S(2)}) %collective-permute-start.5) | collective-permute-done | bytes 262176 | tf_op jit(solution)/shard_map/ppermute | solution.py:36
  100.1 5.7 %reshape.862 = bf16[2,512,3,4,64]{4,3,2,1,0:T(4,128)(2,1)} reshape(bf16[1024,768]{1,0:T(8,128)(2,1)} %convolution_convert_fusion.3) | data formatting | bytes 3145728 | tf_op jit(solution)/shard_map/reshape | solution.py:190
  119.4 14.3 %copy.231 = bf16[2,512,1,4,64]{1,4,3,0,2:T(8,128)(2,1)S(1)} copy(bf16[2,512,1,4,64]{4,3,2,1,0:T(4,128)(2,1)} %get-tuple-element.41) | data formatting | bytes 1048576
  175.4 6.6 %fusion = (f32[2,4,512]{2,1,0:T(4,128)S(1)}, f32[2,4,512]{2,1,0:T(4,128)S(1)}, f32[2,4,512,512]{2,3,1,0:T(8,128)S(1)}) fusion(f32[2,4,512]{2,1,0:T(4,128)S(1)} %multiply_bitcast_fusion, f32[2,4,512,512]{2,3,1,0:T(8,128)} %fusion.94, pred[512,512]{0,1:T(8,128)(4,1)S(1)} %copy-done.40, bf16[2,512,4,64]{1,3,2,0:T(8,128)(2,1)} %reshape_squeeze.7, ...), kind=kOutput, calls=%fused_computation.17 | convolution fusion | flops 283107328 | bytes 18137088 | tf_op jit(solution)/shard_map/sqhd,skhd->shqk/dot_general | solution.py:201
  185.3 6.6 %fusion.129 = (bf16[2,512,4,64]{1,3,2,0:T(8,128)(2,1)S(1)}, f32[2,512,4,64]{1,3,2,0:T(8,128)}) fusion(f32[2,512,4]{1,2,0:T(4,128)S(1)} %bitcast.505, f32[2,4,64,512]{3,2,1,0:T(8,128)S(1)} %fusion.4, f32[2,4,512,512]{2,3,1,0:T(8,128)} %fusion.94, f32[2,4,512]{2,1,0:T(4,128)S(1)} %multiply_bitcast_fusion, pred[512,512]{0,1:T(8,128)(4,1)S(1)} %copy-done.40, ...), kind=kOutput, calls=%fused_computation.315 | convolution fusion | flops 277610496 | bytes 11829248 | tf_op jit(solution)/shard_map/shqk,skhd->sqhd/dot_general | solution.py:212
  212.1 11.6 %fusion.12 = (bf16[256,4096]{1,0:T(8,128)(2,1)}, bf16[256,4096]{1,0:T(8,128)(2,1)S(1)}) fusion(f32[256,4096]{1,0:T(8,128)} %fusion.133, bf16[256,1024]{1,0:T(8,128)(2,1)} %add_convert_fusion.2, bf16[1024,4096]{1,0:T(8,128)(2,1)} %param.23), kind=kOutput, calls=%fused_computation.28 | convolution fusion | flops 2170552320 | bytes 17301504 | tf_op jit(solution)/shard_map/dot_general | solution.py:44
  225.0 6.6 %fusion.61 = bf16[256,1024]{1,0:T(8,128)(2,1)} fusion(f32[256,1024]{1,0:T(8,128)S(1)} %get-tuple-element.100, bf16[256,4096]{1,0:T(8,128)(2,1)S(1)} %get-tuple-element.38, bf16[4096,1024]{1,0:T(8,128)(2,1)} %param.24), kind=kOutput, calls=%fused_computation.103 | convolution fusion | flops 2148007936 | bytes 12058624 | tf_op jit(solution)/shard_map/dot_general | solution.py:44
  236.0 7.4 %multiply_reduce_fusion = (f32[1024]{0:T(1024)}, f32[256]{0:T(256)S(1)}, f32[256]{0:T(256)S(1)}, f32[1024]{0:T(1024)}, f32[256,1024]{1,0:T(8,128)S(1)}) fusion(f32[256,1024]{1,0:T(8,128)S(1)} %get-tuple-element.100, f32[256]{0:T(256)S(1)} %add_rsqrt_fusion.1, f32[256]{0:T(256)S(1)} %broadcast_multiply_fusion.6, f32[1024]{0:T(1024)S(1)} %convert_element_type.411, ...), kind=kOutput, calls=%fused_computation.146 | convolution fusion | flops 2149840384 | bytes 12599296 | tf_op jit(solution)/shard_map/dot_general | solution.py:44
  254.6 6.3 %constant_dynamic-slice_fusion.3 = (bf16[256,4,1,512]{3,2,1,0:T(2,128)(2,1)}, bf16[256,4,1,512]{3,2,1,0:T(2,128)(2,1)}) fusion(bf16[256,4,2,512]{3,2,1,0:T(2,128)(2,1)S(1)} %copy-done.3, s32[]{:T(128)S(6)} %select_n.443, s32[]{:T(128)S(6)} %select_n.444), kind=kLoop, calls=%fused_computation.244 | loop fusion | bytes 4194312 | tf_op jit(solution)/shard_map/jit(dynamic_index_in_dim)/dynamic_slice | solution.py:40
  264.3 5.8 %copy.244 = bf16[256,4,1,512]{0,3,1,2:T(8,128)(2,1)} copy(bf16[256,4,1,512]{3,2,1,0:T(2,128)(2,1)} %get-tuple-element.42) | data formatting | bytes 2097152
  276.3 5.7 %convolution_convert_fusion.5 = bf16[2,4,64,512]{3,2,1,0:T(8,128)(2,1)S(1)} fusion(f32[2,4,512,512]{2,3,1,0:T(8,128)} %fusion.94, f32[2,4,512]{2,1,0:T(4,128)S(1)} %multiply_bitcast_fusion, pred[512,512]{0,1:T(8,128)(4,1)S(1)} %copy-done.41, f32[2,512,4]{1,2,0:T(4,128)S(1)} %bitcast.506, bf16[2,512,4,64]{1,3,2,0:T(8,128)(2,1)S(1)} %gather.38, ...), kind=kOutput, calls=%fused_computation.105 | convolution fusion | flops 278134784 | bytes 9732608 | tf_op jit(solution)/shard_map/shqk,sqhd->skhd/dot_general | solution.py:263
  282.3 6.9 %fusion.132 = (f32[2,4,512]{2,1,0:T(4,128)S(1)}, bf16[2,4,512,512]{2,3,1,0:T(8,128)(2,1)}) fusion(f32[2,4,512]{2,1,0:T(4,128)S(1)} %bitcast_divide_fusion, bf16[2,512,4,64]{1,3,2,0:T(8,128)(2,1)S(1)} %copy-done.23, f32[2,512,4]{1,2,0:T(4,128)S(1)} %bitcast.507, bf16[2,512,4,64]{1,3,2,0:T(8,128)(2,1)S(1)} %gather.38, pred[512]{0:T(512)(128)(4,1)S(1)} %copy-done.60, ...), kind=kOutput, calls=%fused_computation.318 | convolution fusion | flops 282062848 | bytes 13697536 | tf_op jit(solution)/shard_map/sqhd,skhd->shqk/dot_general | solution.py:246
  317.8 6.6 %collective-permute-done.22 = bf16[2,128,3,256]{3,1,2,0:T(8,128)(2,1)S(1)} collective-permute-done((bf16[2,128,3,256]{3,1,2,0:T(8,128)(2,1)S(1)}, bf16[2,128,3,256]{3,1,2,0:T(8,128)(2,1)S(1)}, u32[]{:S(2)}, u32[]{:S(2)}) %collective-permute-start.22) | collective-permute-done | bytes 393248 | tf_op jit(solution)/shard_map/ppermute | solution.py:36
  324.4 7.0 %collective-permute-done.21 = bf16[2,128,3,256]{3,1,2,0:T(8,128)(2,1)S(1)} collective-permute-done((bf16[2,128,3,256]{3,1,2,0:T(8,128)(2,1)S(1)}, bf16[2,128,3,256]{3,1,2,0:T(8,128)(2,1)S(1)}, u32[]{:S(2)}, u32[]{:S(2)}) %collective-permute-start.21) | collective-permute-done | bytes 393248 | tf_op jit(solution)/shard_map/ppermute | solution.py:36
  371.6 6.2 %collective-permute-done.40 = bf16[2,64,1024]{2,1,0:T(8,128)(2,1)S(1)} collective-permute-done((bf16[2,64,1024]{2,1,0:T(8,128)(2,1)S(1)}, bf16[2,64,1024]{2,1,0:T(8,128)(2,1)S(1)}, u32[]{:S(2)}, u32[]{:S(2)}) %collective-permute-start.40) | collective-permute-done | bytes 262176 | tf_op jit(solution)/shard_map/ppermute | solution.py:36
  418.1 9.2 %collective-permute-done.44 = bf16[64,1024]{1,0:T(8,128)(2,1)S(1)} collective-permute-done((bf16[64,1024]{1,0:T(8,128)(2,1)S(1)}, bf16[64,1024]{1,0:T(8,128)(2,1)S(1)}, u32[]{:S(2)}, u32[]{:S(2)}) %collective-permute-start.44) | collective-permute-done | bytes 131104 | tf_op jit(solution)/shard_map/ppermute | solution.py:36
  434.4 19.0 %collective-permute-done.60 = bf16[2,256,1024]{2,1,0:T(8,128)(2,1)S(1)} collective-permute-done((bf16[2,256,1024]{2,1,0:T(8,128)(2,1)S(1)}, bf16[2,256,1024]{2,1,0:T(8,128)(2,1)S(1)}, u32[]{:S(2)}, u32[]{:S(2)}) %collective-permute-start.60) | collective-permute-done | bytes 1048608 | tf_op jit(solution)/shard_map/ppermute | solution.py:36
  470.7 11.4 %collective-permute-done.48 = bf16[2,64,4096]{2,1,0:T(8,128)(2,1)S(1)} collective-permute-done((bf16[2,64,4096]{2,1,0:T(8,128)(2,1)S(1)}, bf16[2,64,4096]{2,1,0:T(8,128)(2,1)S(1)}, u32[]{:S(2)}, u32[]{:S(2)}) %collective-permute-start.48) | collective-permute-done | bytes 1048608 | tf_op jit(solution)/shard_map/ppermute | solution.py:36
  501.4 19.1 %collective-permute-done.52 = bf16[64,4096]{1,0:T(8,128)(2,1)S(1)} collective-permute-done((bf16[64,4096]{1,0:T(8,128)(2,1)S(1)}, bf16[64,4096]{1,0:T(8,128)(2,1)S(1)}, u32[]{:S(2)}, u32[]{:S(2)}) %collective-permute-start.52) | collective-permute-done | bytes 524320 | tf_op jit(solution)/shard_map/ppermute | solution.py:36
  520.7 5.9 %collective-permute-done.34 = bf16[64,3072]{1,0:T(8,128)(2,1)S(1)} collective-permute-done((bf16[64,3072]{1,0:T(8,128)(2,1)S(1)}, bf16[64,3072]{1,0:T(8,128)(2,1)S(1)}, u32[]{:S(2)}, u32[]{:S(2)}) %collective-permute-start.34) | collective-permute-done | bytes 393248 | tf_op jit(solution)/shard_map/ppermute | solution.py:36
  530.7 12.9 %collective-permute-done.53 = bf16[64,4096]{1,0:T(8,128)(2,1)S(1)} collective-permute-done((bf16[64,4096]{1,0:T(8,128)(2,1)S(1)}, bf16[64,4096]{1,0:T(8,128)(2,1)S(1)}, u32[]{:S(2)}, u32[]{:S(2)}) %collective-permute-start.53) | collective-permute-done | bytes 524320 | tf_op jit(solution)/shard_map/ppermute | solution.py:36
  551.1 9.5 %collective-permute-done.54 = bf16[64,4096]{1,0:T(8,128)(2,1)S(1)} collective-permute-done((bf16[64,4096]{1,0:T(8,128)(2,1)S(1)}, bf16[64,4096]{1,0:T(8,128)(2,1)S(1)}, u32[]{:S(2)}, u32[]{:S(2)}) %collective-permute-start.54) | collective-permute-done | bytes 524320 | tf_op jit(solution)/shard_map/ppermute | solution.py:36
  (467 shorter events, 336.9 us)
Async XLA Ops:
  0.7 41.7 %collective-permute-start = (bf16[2,128,1024]{2,1,0:T(8,128)(2,1)}, bf16[2,128,1024]{2,1,0:T(8,128)(2,1)}, u32[]{:S(2)}, u32[]{:S(2)}) collective-permute-start(bf16[2,128,1024]{2,1,0:T(8,128)(2,1)} %param.16), channel_id=1, source_target_pairs={{0,8},{8,0},{16,24},{24,16},{1,9},{9,1},{17,25},{25,17},{2,10},{10... | collective-permute-start | bytes 1572872 | tf_op jit(solution)/shard_map/ppermute | solution.py:36
  3.7 38.7 %collective-permute-start.1 = (bf16[2,128,1024]{2,1,0:T(8,128)(2,1)}, bf16[2,128,1024]{2,1,0:T(8,128)(2,1)}, u32[]{:S(2)}, u32[]{:S(2)}) collective-permute-start(bf16[2,128,1024]{2,1,0:T(8,128)(2,1)} %param.16), channel_id=1, source_target_pairs={{0,16},{8,24},{16,0},{24,8},{1,17},{9,25},{17,1},{25,9},{2,18},{10... | collective-permute-start | bytes 1572872 | tf_op jit(solution)/shard_map/ppermute | solution.py:36
  5.2 37.2 %collective-permute-start.2 = (bf16[2,128,1024]{2,1,0:T(8,128)(2,1)}, bf16[2,128,1024]{2,1,0:T(8,128)(2,1)}, u32[]{:S(2)}, u32[]{:S(2)}) collective-permute-start(bf16[2,128,1024]{2,1,0:T(8,128)(2,1)} %param.16), channel_id=1, source_target_pairs={{0,24},{8,16},{16,8},{24,0},{1,25},{9,17},{17,9},{25,1},{2,26},{10... | collective-permute-start | bytes 1572872 | tf_op jit(solution)/shard_map/ppermute | solution.py:36
  5.3 384.6 %collective-permute-start.57 = (bf16[256,1024]{1,0:T(8,128)(2,1)}, bf16[256,1024]{1,0:T(8,128)(2,1)}, u32[]{:S(2)}, u32[]{:S(2)}) collective-permute-start(bf16[256,1024]{1,0:T(8,128)(2,1)} %bitcast.475), channel_id=1, source_target_pairs={{0,1},{1,0},{2,3},{3,2},{4,5},{5,4},{6,7},{7,6},{8,9},{9,8},{10,11... | collective-permute-start | bytes 1572872 | tf_op jit(solution)/shard_map/ppermute | solution.py:36
  7.3 44.8 %collective-permute-start.3 = (bf16[2,128,1024]{2,1,0:T(8,128)(2,1)}, bf16[2,128,1024]{2,1,0:T(8,128)(2,1)}, u32[]{:S(2)}, u32[]{:S(2)}) collective-permute-start(bf16[2,128,1024]{2,1,0:T(8,128)(2,1)} %get-tuple-element.63), channel_id=1, source_target_pairs={{0,1},{1,0},{2,3},{3,2},{4,5},{5,4},{6,7},{7,6},{8,9},{9,8},{10,11... | collective-permute-start | bytes 1572872 | tf_op jit(solution)/shard_map/ppermute | solution.py:36
  57.7 22.5 %collective-permute-start.5 = (bf16[4,32,1024]{2,1,0:T(8,128)(2,1)S(1)}, bf16[4,32,1024]{2,1,0:T(8,128)(2,1)S(1)}, u32[]{:S(2)}, u32[]{:S(2)}) collective-permute-start(bf16[4,32,1024]{2,1,0:T(8,128)(2,1)S(1)} %get-tuple-element.60), channel_id=1, source_target_pairs={{0,4},{1,5},{2,6},{3,7},{4,0},{5,1},{6,2},{7,3},{8,12},{9,13},{10,... | collective-permute-start | bytes 786440 | tf_op jit(solution)/shard_map/ppermute | solution.py:36
  57.7 22.5 %collective-permute-start.4 = (bf16[4,32,1024]{2,1,0:T(8,128)(2,1)S(1)}, bf16[4,32,1024]{2,1,0:T(8,128)(2,1)S(1)}, u32[]{:S(2)}, u32[]{:S(2)}) collective-permute-start(bf16[4,32,1024]{2,1,0:T(8,128)(2,1)S(1)} %get-tuple-element.61), channel_id=1, source_target_pairs={{0,2},{1,3},{2,0},{3,1},{4,6},{5,7},{6,4},{7,5},{8,10},{9,11},{10,... | collective-permute-start | bytes 786440 | tf_op jit(solution)/shard_map/ppermute | solution.py:36
  114.9 23.6 %collective-permute-start.10 = (bf16[2,128,1024]{2,1,0:T(8,128)(2,1)}, bf16[2,128,1024]{2,1,0:T(8,128)(2,1)}, u32[]{:S(2)}, u32[]{:S(2)}) collective-permute-start(bf16[2,128,1024]{2,1,0:T(8,128)(2,1)} %dynamic-slice_bitcast_fusion.11), channel_id=1, source_target_pairs={{0,1},{1,0},{2,3},{3,2},{4,5},{5,4},{6,7},{7,6},{8,9},{9,8},{10,11... | collective-permute-start | bytes 1572872 | tf_op jit(solution)/shard_map/ppermute | solution.py:36
  246.8 98.2 %collective-permute-start.37 = (bf16[256,1024]{1,0:T(8,128)(2,1)}, bf16[256,1024]{1,0:T(8,128)(2,1)}, u32[]{:S(2)}, u32[]{:S(2)}) collective-permute-start(bf16[256,1024]{1,0:T(8,128)(2,1)} %get-tuple-element.23), channel_id=1, source_target_pairs={{0,1},{1,0},{2,3},{3,2},{4,5},{5,4},{6,7},{7,6},{8,9},{9,8},{10,11... | collective-permute-start | bytes 1572872 | tf_op jit(solution)/shard_map/ppermute | solution.py:36
  251.1 22.7 %collective-permute-start.19 = (bf16[2,128,256]{2,1,0:T(8,128)(2,1)S(1)}, bf16[2,128,256]{2,1,0:T(8,128)(2,1)}, u32[]{:S(2)}, u32[]{:S(2)}) collective-permute-start(bf16[2,128,256]{2,1,0:T(8,128)(2,1)S(1)} %bitcast.500), channel_id=1, source_target_pairs={{0,24},{8,16},{16,8},{24,0},{1,25},{9,17},{17,9},{25,1},{2,26},{10... | collective-permute-start | bytes 393224 | tf_op jit(solution)/shard_map/ppermute | solution.py:36
  324.4 130.1 %collective-permute-start.47 = (bf16[256,4096]{1,0:T(8,128)(2,1)}, bf16[256,4096]{1,0:T(8,128)(2,1)}, u32[]{:S(2)}, u32[]{:S(2)}) collective-permute-start(bf16[256,4096]{1,0:T(8,128)(2,1)} %get-tuple-element.37), channel_id=1, source_target_pairs={{0,1},{1,0},{2,3},{3,2},{4,5},{5,4},{6,7},{7,6},{8,9},{9,8},{10,11... | collective-permute-start | bytes 6291464 | tf_op jit(solution)/shard_map/ppermute | solution.py:36
  331.4 60.0 %collective-permute-start.56 = (bf16[256,2048]{0,1:T(8,128)(2,1)}, bf16[256,2048]{0,1:T(8,128)(2,1)}, u32[]{:S(2)}, u32[]{:S(2)}) collective-permute-start(bf16[256,2048]{0,1:T(8,128)(2,1)} %bitcast.159), channel_id=1, source_target_pairs={{0,1},{1,0},{2,3},{3,2},{4,5},{5,4},{6,7},{7,6},{8,9},{9,8},{10,11... | collective-permute-start | bytes 3145736 | tf_op jit(solution)/shard_map/ppermute | solution.py:36
  387.9 66.5 %collective-permute-start.46 = (bf16[256,512]{0,1:T(8,128)(2,1)}, bf16[256,512]{0,1:T(8,128)(2,1)}, u32[]{:S(2)}, u32[]{:S(2)}) collective-permute-start(bf16[256,512]{0,1:T(8,128)(2,1)} %bitcast.137), channel_id=1, source_target_pairs={{0,1},{1,0},{2,3},{3,2},{4,5},{5,4},{6,7},{7,6},{8,9},{9,8},{10,11... | collective-permute-start | bytes 786440 | tf_op jit(solution)/shard_map/ppermute | solution.py:36
  400.0 31.1 %collective-permute-start.58 = (bf16[2,256,1024]{2,1,0:T(8,128)(2,1)}, bf16[2,256,1024]{2,1,0:T(8,128)(2,1)}, u32[]{:S(2)}, u32[]{:S(2)}) collective-permute-start(bf16[2,256,1024]{2,1,0:T(8,128)(2,1)} %dynamic-slice_bitcast_fusion.1), channel_id=1, source_target_pairs={{0,8},{8,0},{16,24},{24,16},{1,9},{9,1},{17,25},{25,17},{2,10},{10... | collective-permute-start | bytes 3145736 | tf_op jit(solution)/shard_map/ppermute | solution.py:36
  427.3 26.1 %collective-permute-start.60 = (bf16[2,256,1024]{2,1,0:T(8,128)(2,1)S(1)}, bf16[2,256,1024]{2,1,0:T(8,128)(2,1)S(1)}, u32[]{:S(2)}, u32[]{:S(2)}) collective-permute-start(bf16[2,256,1024]{2,1,0:T(8,128)(2,1)S(1)} %dynamic-slice_bitcast_fusion), channel_id=1, source_target_pairs={{0,16},{8,24},{16,0},{24,8},{1,17},{9,25},{17,1},{25,9},{2,18},{10... | collective-permute-start | bytes 3145736 | tf_op jit(solution)/shard_map/ppermute | solution.py:36
  429.5 69.4 %collective-permute-start.33 = (bf16[64,3072]{1,0:T(8,128)(2,1)S(1)}, bf16[64,3072]{1,0:T(8,128)(2,1)S(1)}, u32[]{:S(2)}, u32[]{:S(2)}) collective-permute-start(bf16[64,3072]{1,0:T(8,128)(2,1)S(1)} %fusion.84), channel_id=1, source_target_pairs={{0,4},{1,5},{2,6},{3,7},{4,0},{5,1},{6,2},{7,3},{8,12},{9,13},{10,... | collective-permute-start | bytes 1179656 | tf_op jit(solution)/shard_map/ppermute | solution.py:36
  432.9 31.7 %collective-permute-start.59 = (bf16[256,1024]{1,0:T(8,128)(2,1)S(1)}, bf16[256,1024]{1,0:T(8,128)(2,1)S(1)}, u32[]{:S(2)}, u32[]{:S(2)}) collective-permute-start(bf16[256,1024]{1,0:T(8,128)(2,1)S(1)} %dynamic-slice_bitcast_fusion.7), channel_id=1, source_target_pairs={{0,16},{8,24},{16,0},{24,8},{1,17},{9,25},{17,1},{25,9},{2,18},{10... | collective-permute-start | bytes 1572872 | tf_op jit(solution)/shard_map/ppermute | solution.py:36
  461.3 26.2 %collective-permute-start.50 = (bf16[2,64,4096]{2,1,0:T(8,128)(2,1)S(1)}, bf16[2,64,4096]{2,1,0:T(8,128)(2,1)S(1)}, u32[]{:S(2)}, u32[]{:S(2)}) collective-permute-start(bf16[2,64,4096]{2,1,0:T(8,128)(2,1)S(1)} %dynamic-slice_bitcast_fusion.2), channel_id=1, source_target_pairs={{0,16},{8,24},{16,0},{24,8},{1,17},{9,25},{17,1},{25,9},{2,18},{10... | collective-permute-start | bytes 3145736 | tf_op jit(solution)/shard_map/ppermute | solution.py:36
  469.1 30.4 %collective-permute-start.62 = (bf16[256,1024]{1,0:T(8,128)(2,1)S(1)}, bf16[256,1024]{1,0:T(8,128)(2,1)S(1)}, u32[]{:S(2)}, u32[]{:S(2)}) collective-permute-start(bf16[256,1024]{1,0:T(8,128)(2,1)S(1)} %dynamic-slice_bitcast_fusion.5), channel_id=1, source_target_pairs={{0,2},{1,3},{2,0},{3,1},{4,6},{5,7},{6,4},{7,5},{8,10},{9,11},{10,... | collective-permute-start | bytes 1572872 | tf_op jit(solution)/shard_map/ppermute | solution.py:36
  497.2 23.2 %collective-permute-start.52 = (bf16[64,4096]{1,0:T(8,128)(2,1)S(1)}, bf16[64,4096]{1,0:T(8,128)(2,1)S(1)}, u32[]{:S(2)}, u32[]{:S(2)}) collective-permute-start(bf16[64,4096]{1,0:T(8,128)(2,1)S(1)} %dynamic-slice_bitcast_fusion.8), channel_id=1, source_target_pairs={{0,2},{1,3},{2,0},{3,1},{4,6},{5,7},{6,4},{7,5},{8,10},{9,11},{10,... | collective-permute-start | bytes 1572872 | tf_op jit(solution)/shard_map/ppermute | solution.py:36
  499.0 27.6 %collective-permute-start.34 = (bf16[64,3072]{1,0:T(8,128)(2,1)S(1)}, bf16[64,3072]{1,0:T(8,128)(2,1)S(1)}, u32[]{:S(2)}, u32[]{:S(2)}) collective-permute-start(bf16[64,3072]{1,0:T(8,128)(2,1)S(1)} %add_convert_fusion.3), channel_id=1, source_target_pairs={{0,2},{1,3},{2,0},{3,1},{4,6},{5,7},{6,4},{7,5},{8,10},{9,11},{10,... | collective-permute-start | bytes 1179656 | tf_op jit(solution)/shard_map/ppermute | solution.py:36
  499.7 28.2 %collective-permute-start.63 = (bf16[256,1024]{1,0:T(8,128)(2,1)S(1)}, bf16[256,1024]{1,0:T(8,128)(2,1)S(1)}, u32[]{:S(2)}, u32[]{:S(2)}) collective-permute-start(bf16[256,1024]{1,0:T(8,128)(2,1)S(1)} %fusion.77), channel_id=1, source_target_pairs={{0,4},{1,5},{2,6},{3,7},{4,0},{5,1},{6,2},{7,3},{8,12},{9,13},{10,... | collective-permute-start | bytes 1572872 | tf_op jit(solution)/shard_map/ppermute | solution.py:36
  520.6 23.1 %collective-permute-start.53 = (bf16[64,4096]{1,0:T(8,128)(2,1)S(1)}, bf16[64,4096]{1,0:T(8,128)(2,1)S(1)}, u32[]{:S(2)}, u32[]{:S(2)}) collective-permute-start(bf16[64,4096]{1,0:T(8,128)(2,1)S(1)} %fusion.80), channel_id=1, source_target_pairs={{0,4},{1,5},{2,6},{3,7},{4,0},{5,1},{6,2},{7,3},{8,12},{9,13},{10,... | collective-permute-start | bytes 1572872 | tf_op jit(solution)/shard_map/ppermute | solution.py:36
  528.1 22.7 %collective-permute-start.64 = (bf16[256,1024]{1,0:T(8,128)(2,1)S(1)}, bf16[256,1024]{1,0:T(8,128)(2,1)S(1)}, u32[]{:S(2)}, u32[]{:S(2)}) collective-permute-start(bf16[256,1024]{1,0:T(8,128)(2,1)S(1)} %add_convert_fusion), channel_id=1, source_target_pairs={{0,2},{1,3},{2,0},{3,1},{4,6},{5,7},{6,4},{7,5},{8,10},{9,11},{10,... | collective-permute-start | bytes 1572872 | tf_op jit(solution)/shard_map/ppermute | solution.py:36
  (105 other events, 1393.7 us)

commit v2 on v1

v2 whole, which is shorter than its diff:
```python
import functools

import jax
import jax.numpy as jnp
from jax import lax
from jax.experimental import pallas as pl
from jax.experimental.pallas import tpu as pltpu
from jax.sharding import PartitionSpec as P

HEADS = 16
F32 = jnp.float32
BF16 = jnp.bfloat16
MIB = 1 << 20
EPS = 1e-05
FAR = -1e30
GELU_A = 0.7978845608028654
GELU_B = 0.044715


def swap(values, axis, mask):
    size = lax.axis_size(axis)
    return lax.ppermute(values, axis, [(i, i ^ mask) for i in range(size)])


def pick(values, index, dim=0):
    return lax.dynamic_index_in_dim(values, index, dim, keepdims=False)


def nn(left, right):
    return lax.dot_general(left, right, (((1,), (0,)), ((), ())), preferred_element_type=F32)


def nt(left, right):
    return lax.dot_general(left, right, (((1,), (1,)), ((), ())), preferred_element_type=F32)


def tn(left, right):
    return lax.dot_general(left, right, (((0,), (0,)), ((), ())), preferred_element_type=F32)


def params(mib):
    return pltpu.CompilerParams(vmem_limit_bytes=mib * MIB)


def call(kernel, name, grid, ins, outs, scratch, scalars, mib, cost):
    def whole(shape):
        return pl.BlockSpec(shape, lambda *_: (0,) * len(shape))

    in_specs, arrays = [], []
    for item in ins:
        if isinstance(item, tuple):
            arrays.append(item[0])
            in_specs.append(pl.BlockSpec(item[1], item[2]))
        else:
            arrays.append(item)
            in_specs.append(whole(item.shape))
    out_shapes, out_specs = [], []
    for item in outs:
        out_shapes.append(jax.ShapeDtypeStruct(item[0], item[1]))
        out_specs.append(whole(item[0]) if len(item) == 2 else pl.BlockSpec(item[2], item[3]))
    spec = pltpu.PrefetchScalarGridSpec(
        num_scalar_prefetch=1,
        grid=grid,
        in_specs=in_specs,
        out_specs=out_specs,
        scratch_shapes=scratch,
    )
    return pl.pallas_call(
        kernel,
        grid_spec=spec,
        out_shape=out_shapes,
        compiler_params=params(mib),
        cost_estimate=pl.CostEstimate(flops=cost[0], bytes_accessed=cost[1], transcendentals=0),
        name=name,
    )(scalars, *arrays)


def norm_stats(values):
    average = jnp.mean(values, -1, keepdims=True)
    centred = values - average
    scale = lax.rsqrt(jnp.mean(centred * centred, -1, keepdims=True) + EPS)
    return centred * scale, scale


def norm_back(unit, scale, gain, grad):
    scaled = grad * gain
    mean_one = jnp.mean(scaled, -1, keepdims=True)
    mean_two = jnp.mean(scaled * unit, -1, keepdims=True)
    return scale * (scaled - mean_one - unit * mean_two)


def project_kernel(sc, rows, gain, bias, wq, wk, wv, normed, qkv):
    part = wq.shape[1]
    unit, _ = norm_stats(rows[...].astype(F32))
    low = (unit * gain[...].astype(F32) + bias[...].astype(F32)).astype(BF16)
    normed[...] = low
    for i, weight in enumerate((wq, wk, wv)):
        qkv[:, i * part : (i + 1) * part] = nn(low, weight[...]).astype(BF16)


def lane_masks():
    lane = lax.broadcasted_iota(jnp.int32, (1, 128), 1)
    return [lane < 64, lane >= 64]


def of_head(values, mask):
    return jnp.where(mask, values, jnp.zeros_like(values))


def by_head(first, second, masks):
    return jnp.where(masks[0], first, second)


BLOCK = 256


def own_kernel(blocks, sc, *refs):
    ins, outs = refs[: 3 * blocks], refs[3 * blocks :]
    q_out, k_out, v_out, t_out, l_out = outs[:5]
    held = outs[5]
    tok = ins[0].shape[1]
    scale = 64 ** (-0.5)
    for mask in range(blocks):
        place = sc[2 + mask]
        for i in range(3):
            values = ins[3 * mask + i][0]
            if i == 0:
                values = (values.astype(F32) * scale).astype(BF16)
            held[i, place] = values
    rows = blocks * tok
    queries = held[0].reshape(rows, 128)
    keys = held[1].reshape(rows, 128)
    values = held[2].reshape(rows, 128)
    q_out[0], k_out[0], v_out[0] = queries, keys, values
    masks = lane_masks()
    size = min(BLOCK, rows)
    lower = lax.broadcasted_iota(jnp.int32, (size, size), 0) >= lax.broadcasted_iota(
        jnp.int32, (size, size), 1
    )
    product = queries.astype(F32) * keys.astype(F32)
    head_keys = [of_head(keys, m) for m in masks]
    head_values = [of_head(values, m) for m in masks]
    selfs = [jnp.sum(of_head(product, m), -1, keepdims=True) for m in masks]
    for i in range(rows // size):
        here = slice(i * size, (i + 1) * size)
        total, sums = jnp.zeros((size, 128), F32), []
        for h in range(2):
            count = jnp.zeros((size, 1), F32)
            for j in range(i + 1):
                there = slice(j * size, (j + 1) * size)
                scores = nt(queries[here], head_keys[h][there]) - selfs[h][here]
                if i == j:
                    scores = jnp.where(lower, scores, FAR)
                weights = jnp.exp(scores)
                count = count + jnp.sum(weights, -1, keepdims=True)
                total = total + nn(weights.astype(BF16), head_values[h][there])
            sums.append(count)
        t_out[0, here] = total
        l_out[0, here] = by_head(sums[0], sums[1], masks)


def load_cached(pieces, mem):
    tok = pieces[0].shape[2]
    for mask, piece in enumerate(pieces):
        mem[:, mask * tok : (mask + 1) * tok] = piece[:, 0]


def cached_kernel(blocks, sc, *refs):
    q_in, k_in, t_in, l_in = refs[:4]
    pieces = refs[4 : 4 + blocks]
    att_out, l_out = refs[4 + blocks : 6 + blocks]
    sends = refs[6 + blocks : 6 + 2 * blocks]
    mem, low = refs[6 + 2 * blocks :]
    load_cached(pieces, mem)
    tok = pieces[0].shape[2]
    queries, keys = q_in[0], k_in[0]
    rows = queries.shape[0]
    masks = lane_masks()
    product = queries.astype(F32) * keys.astype(F32)
    selfs = [jnp.sum(of_head(product, m), -1, keepdims=True) for m in masks]
    head_keys = [of_head(mem[0], m) for m in masks]
    head_values = [of_head(mem[1], m) for m in masks]
    size = min(BLOCK, rows)
    for i in range(rows // size):
        here = slice(i * size, (i + 1) * size)
        total, sums = t_in[0, here], []
        for h in range(2):
            weights = jnp.exp(nt(queries[here], head_keys[h]) - selfs[h][here])
            sums.append(jnp.sum(weights, -1, keepdims=True))
            total = total + nn(weights.astype(BF16), head_values[h])
        count = l_in[0, here] + by_head(sums[0], sums[1], masks)
        attended = total / count
        att_out[0, here] = attended
        l_out[0, here] = count
        low[i * size // tok : (i + 1) * size // tok] = attended.astype(BF16).reshape(
            size // tok, tok, 128
        )
    for mask in range(blocks):
        sends[mask][0] = low[sc[2 + mask]]


def attention_back_kernel(blocks, halved, sc, *refs):
    q_in, k_in, v_in, att_in, l_in = refs[:5]
    pieces = refs[5 : 5 + blocks]
    grads = refs[5 + blocks : 5 + 2 * blocks]
    sends = refs[5 + 2 * blocks : 5 + 3 * blocks]
    rest = refs[5 + 3 * blocks :]
    if halved:
        to_core, rest = rest[0], rest[1:]
    mem, came, low = rest
    load_cached(pieces, mem)
    tok = pieces[0].shape[2]
    for mask in range(blocks):
        came[sc[2 + mask]] = grads[mask][0]
    queries, keys, values = q_in[0], k_in[0], v_in[0]
    rows = queries.shape[0]
    scale = 64 ** (-0.5)
    masks = lane_masks()
    grad = came[...].reshape(rows, 128).astype(F32)
    count = l_in[0]
    scaled_f = grad / count
    scaled = scaled_f.astype(BF16)
    weighed = grad * att_in[0] / count
    product = queries.astype(F32) * keys.astype(F32)
    selfs = [jnp.sum(of_head(product, m), -1, keepdims=True) for m in masks]
    fixes = [jnp.sum(of_head(weighed, m), -1, keepdims=True) for m in masks]
    own_k = [of_head(keys, m) for m in masks]
    own_v = [of_head(values, m) for m in masks]
    mem_k = [of_head(mem[0], m) for m in masks]
    mem_v = [of_head(mem[1], m) for m in masks]
    q_t = [of_head(queries, m).astype(F32).T.astype(BF16) for m in masks]
    s_t = [of_head(scaled, m).astype(F32).T.astype(BF16) for m in masks]
    size = min(BLOCK, rows)
    lower = lax.broadcasted_iota(jnp.int32, (size, size), 0) >= lax.broadcasted_iota(
        jnp.int32, (size, size), 1
    )
    steps = rows // size
    keys_t = [jnp.zeros((128, size), F32) for _ in range(steps)]
    values_t = [jnp.zeros((128, size), F32) for _ in range(steps)]
    diags = []
    for i in range(steps):
        here = slice(i * size, (i + 1) * size)
        total, sums = jnp.zeros((size, 128), F32), []
        for h in range(2):
            diag = jnp.zeros((size, 1), F32)
            for j in range(i + 1):
                there = slice(j * size, (j + 1) * size)
                scores = nt(queries[here], own_k[h][there]) - selfs[h][here]
                if i == j:
                    scores = jnp.where(lower, scores, FAR)
                weights = jnp.exp(scores)
                change = weights * (nt(scaled[here], own_v[h][there]) - fixes[h][here])
                diag = diag + jnp.sum(change, -1, keepdims=True)
                small = change.astype(BF16)
                total = total + nn(small, own_k[h][there])
                keys_t[j] = keys_t[j] + nn(q_t[h][:, here], small)
                values_t[j] = values_t[j] + nn(s_t[h][:, here], weights.astype(BF16))
            weights = jnp.exp(nt(queries[here], mem_k[h]) - selfs[h][here])
            change = weights * (nt(scaled[here], mem_v[h]) - fixes[h][here])
            diag = diag + jnp.sum(change, -1, keepdims=True)
            total = total + nn(change.astype(BF16), mem_k[h])
            sums.append(diag)
        diag = by_head(sums[0], sums[1], masks)
        diags.append(diag)
        grad_q = scale * (total - diag * keys[here].astype(F32))
        low[0, i * size // tok : (i + 1) * size // tok] = grad_q.astype(BF16).reshape(
            size // tok, tok, 128
        )
    for j in range(steps):
        there = slice(j * size, (j + 1) * size)
        grad_k = keys_t[j].T - diags[j] * queries[there].astype(F32)
        blocks_here = slice(j * size // tok, (j + 1) * size // tok)
        low[1, blocks_here] = grad_k.astype(BF16).reshape(size // tok, tok, 128)
        low[2, blocks_here] = values_t[j].T.astype(BF16).reshape(size // tok, tok, 128)
    for mask in range(blocks):
        for i in range(3):
            sends[mask][i, 0] = low[i, sc[2 + mask]]
    if halved:

        @pl.when(pl.program_id(1) != sc[1])
        def _():
            for mask in range(blocks):
                for i in range(3):
                    to_core[mask, i, 0] = low[i, sc[2 + mask]]


def feed_kernel(blocks, sc, *refs):
    att_in = refs[:blocks]
    rest = refs[blocks:]
    tokens, cot, w_out, gain, bias, w_in, w_down = rest[:7]
    mixed, grad_res, act_keep, inner_keep, to_core, normed_out, att_out, branch_keep, rows_core = rest[
        7:16
    ]
    sums = rest[16]
    grad_att = rest[17 : 17 + blocks]
    residual, normed, total, back = rest[17 + blocks :]
    step, steps = pl.program_id(0), pl.num_programs(0)
    part, width = att_in[0].shape[1], tokens.shape[1]
    my_block, core = sc[0], sc[1]

    def out_rows(mask):
        return pl.ds(pl.multiple_of((my_block ^ mask) * part, part), part)

    @pl.when(step == 0)
    def _():
        branch = tokens[...].astype(F32)
        for mask in range(blocks):
            branch = branch + nn(att_in[mask][...], w_out[out_rows(mask), :])
            att_out[:, out_rows(mask)] = att_in[mask][...]
        rows_core[:, width : 2 * width] = att_out[...]
        residual[...] = branch
        unit, _ = norm_stats(branch)
        low = (unit * gain[...].astype(F32) + bias[...].astype(F32)).astype(BF16)
        normed[...] = low
        normed_out[...] = low
        rows_core[:, :width] = low

    inner = nn(normed[...], w_in[...])
    square = inner * inner
    bend = jnp.tanh(GELU_A * inner * (1.0 + GELU_B * square))
    half = 0.5 * (1.0 + bend)
    act = (inner * half).astype(BF16)
    slope = half + (0.5 * GELU_A) * inner * (1.0 - bend * bend) * (1.0 + 3.0 * GELU_B * square)
    grad = (slope * nt(cot[...], w_down[...])).astype(BF16)
    into = nn(act, w_down[...])
    away = nt(grad, w_in[...])

    @pl.when(step == 0)
    def _():
        total[...] = into
        back[...] = away

    @pl.when(step > 0)
    def _():
        total[...] += into
        back[...] += away

    @pl.when(step % 2 == core)
    def _():
        act_keep[0] = act
        inner_keep[0] = grad

    @pl.when(step % 2 != core)
    def _():
        to_core[0, 0] = act
        to_core[1, 0] = grad

    @pl.when(step == steps - 1)
    def _():
        here = residual[...]
        mixed[...] = (here + total[...]).astype(BF16)
        unit, scale = norm_stats(here)
        away = back[...]
        sums[0:1] = jnp.sum(away * unit, 0, keepdims=True)
        sums[1:2] = jnp.sum(away, 0, keepdims=True)
        found = cot[...].astype(F32) + norm_back(unit, scale, gain[...].astype(F32), away)
        grad_res[...] = found
        low = found.astype(BF16)
        left, right = low[:, : width // 2], low[:, width // 2 :]
        branch_keep[...] = jnp.where(core == 0, left, right)
        rows_core[:, 2 * width :] = jnp.where(core == 0, right, left)
        for mask in range(blocks):
            grad_att[mask][...] = nt(low, w_out[out_rows(mask), :]).astype(BF16)


def weight_kernel(blocks, sc, *refs):
    (act, act_two, cot, cot_two, att, att_two, branch, branch_two) = refs[:8]
    normed, normed_two, inner, inner_two = refs[8:12]
    outs = refs[12:]
    step = pl.program_id(0)
    width = cot.shape[1]
    down = tn(act[0], cot[...]) + tn(act_two[0, 0], cot_two[...])
    out = tn(att[...], branch[...]) + tn(att_two[...], branch_two[...])
    part = out.shape[0]
    tile = down.shape[0]
    joined = [down.astype(BF16), out.astype(BF16)]
    half = (tile + part // 2) // 2

    def store_down(ref, lo):
        low, wide = joined
        hi = lo + half
        if lo < tile:
            ref[0, : min(hi, tile) - lo] = low[lo : min(hi, tile)]
        if hi > tile:
            first = max(lo, tile) - tile
            count = hi - tile - first
            at = half - count
            ref[0, at:, : width // 2] = wide[first : first + count]
            ref[0, at:, width // 2 :] = wide[part // 2 + first : part // 2 + first + count]

    ins = []
    for q in range(blocks):
        found = tn(normed[...], inner[q]) + tn(normed_two[...], inner_two[0, q])
        ins.append(found.astype(BF16))

    def store_in(ref, lo):
        tile_in = ins[0].shape[1]
        for q in range(blocks):
            ref[0, :, q * tile_in : (q + 1) * tile_in] = ins[q][lo : lo + part // 2]

    top = blocks // 2
    for i, (bit, lo) in enumerate(((1, 0), (top, 1))):
        @pl.when((step & bit) != 0)
        def _():
            store_down(outs[4 * i], lo * half)
            store_in(outs[4 * i + 2], lo * (part // 2))

        @pl.when((step & bit) == 0)
        def _():
            store_down(outs[4 * i + 1], lo * half)
            store_in(outs[4 * i + 3], lo * (part // 2))


def tokens_kernel(blocks, sc, tokens, grad_res, gain, *refs):
    pieces = refs[:blocks]
    weights = refs[blocks : blocks + 3]
    grad_tokens, sums, total = refs[blocks + 3 :]
    step, steps = pl.program_id(0), pl.num_programs(0)
    for mask in range(blocks):

        @pl.when(step == mask)
        def _():
            found = nt(pieces[mask][0], weights[0][...])
            found = found + nt(pieces[mask][1], weights[1][...])
            found = found + nt(pieces[mask][2], weights[2][...])
            if mask == 0:
                total[...] = found
            else:
                total[...] += found

    @pl.when(step == steps - 1)
    def _():
        unit, scale = norm_stats(tokens[...].astype(F32))
        grad = total[...]
        sums[0:1] = jnp.sum(grad * unit, 0, keepdims=True)
        sums[1:2] = jnp.sum(grad, 0, keepdims=True)
        grad_tokens[...] = grad_res[...] + norm_back(unit, scale, gain[...].astype(F32), grad)


def fetch_banks(mem_keys, mem_values, continues, groups, my_group, blocks, my_block):
    seq_count, rows, width = mem_keys.shape
    core, chips = my_group % 2, groups // 2
    my_chip = my_group // 2
    kept = jnp.where(core == 0, mem_keys, mem_values)
    sent = jnp.where(core == 0, mem_values, mem_keys)
    came = swap(sent, "grp", 1)
    pair = jnp.where(core == 0, jnp.stack([kept, came]), jnp.stack([came, kept]))
    per_chip = 2 * seq_count
    pair = pair.reshape(per_chip, chips, rows // chips, width)
    parts = [pick(pair, my_chip, 1)]
    for mask in range(1, chips):
        parts.append(swap(pick(pair, my_chip ^ mask, 1), "grp", 2 * mask))
    order = my_chip ^ jnp.arange(chips)
    every = jnp.take(jnp.stack(parts), order, axis=0).reshape(
        chips * per_chip, rows // chips, width
    )

    def needed(chip):
        banks = lax.dynamic_slice_in_dim(continues, chip * per_chip, per_chip)
        return jnp.take(every, banks, axis=0)

    parts = [needed(my_chip)]
    for mask in range(1, chips):
        parts.append(swap(needed(my_chip ^ mask), "grp", 2 * mask))
    held = jnp.stack(parts, 1).reshape(2, seq_count, rows, width)
    kept = pick(held, core)
    came = swap(pick(held, 1 - core), "grp", 1)
    keys = jnp.where(core == 0, kept, came)
    values = jnp.where(core == 0, came, kept)
    part = width // blocks
    both = jnp.stack([keys, values])

    def columns(block):
        return lax.dynamic_slice_in_dim(both, block * part, part, 3)

    parts = [columns(my_block)]
    for mask in range(1, blocks):
        parts.append(swap(columns(my_block ^ mask), "blk", mask))
    return parts


def add(*values):
    total = values[0].astype(F32)
    for value in values[1:]:
        total = total + value.astype(F32)
    return total.astype(BF16)


def reduce_blocks(sent, kept, first_bit, order, blocks):
    masks = [m for m in range(blocks) if not m & first_bit]
    came = swap(sent, "blk", first_bit)
    terms = {m: [kept[i], came[i]] for i, m in enumerate(masks)}
    for bit in order:
        away = [m for m in masks if m & bit]
        masks = [m for m in masks if not m & bit]
        if len(away) == 1:
            came = swap(add(*terms[away[0]]), "blk", bit)[None]
        else:
            came = swap(jnp.stack([add(*terms[m]) for m in away]), "blk", bit)
        for i, m in enumerate(masks):
            terms[m].append(came[i])
    return terms[0]


def reduce_groups(parts, groups, my_group):
    bits = groups.bit_length() - 1
    low = (my_group >> 1) & 1
    if len(parts) == 2:
        first, second = add(*parts[0]), add(*parts[1])
        mine = jnp.where(low == 0, first, second)
        other = jnp.where(low == 0, second, first)
    else:
        whole = add(*parts[0])
        halves = whole.reshape((2, whole.shape[0] // 2) + whole.shape[1:])
        mine, other = pick(halves, low), pick(halves, 1 - low)
    came = swap(other, "grp", 2)
    held = add(mine, came)
    for bit in range(2, bits):
        held = add(held, swap(held, "grp", 1 << bit))
    came = swap(held, "grp", 2)
    return jnp.where(low == 0, jnp.stack([held, came]), jnp.stack([came, held]))


def join_cores(values, core):
    came = swap(values, "grp", 1)
    return jnp.where(core == 0, jnp.stack([values, came]), jnp.stack([came, values]))


def on_device(
    tokens,
    gain_one,
    bias_one,
    w_qkv,
    w_out,
    gain_two,
    bias_two,
    w_in,
    w_down,
    mem_keys,
    mem_values,
    continues,
    block_place,
    cotangent,
):
    seq_count, tok, width = tokens.shape
    hidden_width = w_in.shape[1]
    blocks, groups = lax.axis_size("blk"), lax.axis_size("grp")
    my_block, my_group = lax.axis_index("blk"), lax.axis_index("grp")
    core = my_group % 2
    part = width // blocks
    pairs = part // 128
    halved = pairs > 1
    rows = seq_count * tok
    seg_rows = blocks * tok
    tile = hidden_width // (2 * blocks)
    places = [block_place[my_block ^ mask] for mask in range(blocks)]
    scalars = jnp.stack([my_block, core] + places).astype(jnp.int32)
    gain_one, bias_one = gain_one.reshape(1, width), bias_one.reshape(1, width)
    gain_two, bias_two = gain_two.reshape(1, width), bias_two.reshape(1, width)
    flat = tokens.reshape(rows, width)
    cot = cotangent.reshape(rows, width)

    pieces = [flat] + [swap(flat, "blk", mask) for mask in range(1, blocks)]
    cot_two = swap(cot, "grp", 1)
    mem = fetch_banks(mem_keys, mem_values, continues, groups, my_group, blocks, my_block)

    def head_weights(j, at=None):
        def index(i, sc):
            return (0, j * blocks + (sc[0] ^ i if at is None else sc[0]))

        return (w_qkv, (width, part), index)

    normed, qkv = [], []
    for piece in pieces:
        found = call(
            project_kernel,
            "project",
            (1,),
            [piece, gain_one, bias_one] + [head_weights(j, 0) for j in range(3)],
            [((rows, width), BF16), ((rows, 3 * part), BF16)],
            [],
            scalars,
            24,
            (6 * rows * width * part, 4 * rows * width + 6 * width * part),
        )
        normed.append(found[0])
        qkv.append(found[1].reshape(seq_count, tok, 3 * part))

    def heads_block(j):
        return (1, tok, 128), lambda s, p, sc: (s, 0, j * pairs + p)

    seg_block = (1, seg_rows, 128), lambda s, p, sc: (s, 0, p)
    seg_shape = (seq_count, seg_rows, part)
    tok_block = (1, tok, 128), lambda s, p, sc: (s, 0, p)
    mem_block = (2, 1, tok, 128), lambda s, p, sc: (0, s, 0, p)
    queries, keys, values, partial, counts = call(
        functools.partial(own_kernel, blocks),
        "own_keys",
        (seq_count, pairs),
        [(qkv[m],) + heads_block(j) for m in range(blocks) for j in range(3)],
        [(seg_shape, BF16) + seg_block] * 3 + [(seg_shape, F32) + seg_block] * 2,
        [pltpu.VMEM((3, blocks, tok, 128), BF16)],
        scalars,
        32,
        (2 * seq_count * seg_rows * seg_rows * part, 8 * seq_count * seg_rows * part),
    )
    found = call(
        functools.partial(cached_kernel, blocks),
        "cached_keys",
        (seq_count, pairs),
        [(a,) + seg_block for a in (queries, keys, partial, counts)]
        + [(a,) + mem_block for a in mem],
        [(seg_shape, F32) + seg_block] * 2
        + [((seq_count, tok, part), BF16) + tok_block] * blocks,
        [pltpu.VMEM((2, seg_rows, 128), BF16), pltpu.VMEM((blocks, tok, 128), BF16)],
        scalars,
        32,
        (4 * seq_count * seg_rows * seg_rows * part, 16 * seq_count * seg_rows * part),
    )
    attended_f, counts = found[:2]
    attended = [found[2]] + [swap(found[2 + m], "blk", m) for m in range(1, blocks)]
    attended = [a.reshape(rows, part) for a in attended]

    tile_block = (1, rows, tile), lambda j, sc: (j // 2, 0, 0)
    found = call(
        functools.partial(feed_kernel, blocks),
        "feed",
        (2 * blocks,),
        attended
        + [flat, cot, w_out, gain_two, bias_two]
        + [
            (w_in, (width, tile), lambda j, sc: (0, j)),
            (w_down, (tile, width), lambda j, sc: (j, 0)),
        ],
        [
            ((rows, width), BF16),
            ((rows, width), F32),
            ((blocks, rows, tile), BF16) + tile_block,
            ((blocks, rows, tile), BF16) + tile_block,
            ((2, blocks, rows, tile), BF16, (2, 1, rows, tile), lambda j, sc: (0, j // 2, 0, 0)),
            ((rows, width), BF16),
            ((rows, width), BF16),
            ((rows, width // 2), BF16),
            ((rows, 2 * width + width // 2), BF16),
            ((2, width), F32),
        ]
        + [((rows, part), BF16)] * blocks,
        [
            pltpu.VMEM((rows, width), F32),
            pltpu.VMEM((rows, width), BF16),
            pltpu.VMEM((rows, width), F32),
            pltpu.VMEM((rows, width), F32),
        ],
        scalars,
        48,
        (8 * rows * width * hidden_width, 4 * width * hidden_width + 30 * rows * width),
    )
    mixed, grad_res, act_keep, inner_keep, to_core, normed_two, att_all, branch, rows_core = found[:9]
    sums_two = found[9]
    grad_att = found[10:]
    grad_att = [grad_att[0]] + [swap(grad_att[m], "blk", m) for m in range(1, blocks)]
    grad_att = [g.reshape(seq_count, tok, part) for g in grad_att]
    rows_came = swap(rows_core, "grp", 1)
    tiles_came = swap(to_core, "grp", 1)

    height = tile + part // 2
    half_rows = height // 2
    top = blocks // 2

    def of_mask(shape, mask, wanted):
        def index(m, sc):
            if mask == 1:
                return (m >> 1, 0, 0)
            return (jnp.maximum(m - top, 0) if wanted else jnp.minimum(m, top - 1), 0, 0)

        return ((top,) + shape, BF16, (1,) + shape, index)

    down_shape, in_shape = (half_rows, width), (part // 2, blocks * tile)
    outs = []
    for mask in (1, top):
        for shape in (down_shape, in_shape):
            outs += [of_mask(shape, mask, True), of_mask(shape, mask, False)]

    def columns(base):
        return lambda m, sc: (0, base + (sc[0] ^ m))

    found = call(
        functools.partial(weight_kernel, blocks),
        "weights",
        (blocks,),
        [
            (act_keep, (1, rows, tile), lambda m, sc: (sc[0] ^ m, 0, 0)),
            (tiles_came, (1, 1, rows, tile), lambda m, sc: (0, sc[0] ^ m, 0, 0)),
            cot,
            cot_two,
            (att_all, (rows, part), columns(0)),
            (rows_came, (rows, part), columns(blocks)),
            branch,
            (rows_came, (rows, width // 2), lambda m, sc: (0, 4)),
            (normed_two, (rows, part), columns(0)),
            (rows_came, (rows, part), columns(0)),
            inner_keep,
            (tiles_came, (1, blocks, rows, tile), lambda m, sc: (1, 0, 0, 0)),
        ],
        outs,
        [],
        scalars,
        48,
        (8 * rows * width * hidden_width, 10 * width * hidden_width),
    )
    bits = [1 << i for i in range(blocks.bit_length() - 1)]
    down_parts = [
        reduce_blocks(found[0], found[1], 1, bits[1:], blocks),
        reduce_blocks(found[4], found[5], top, bits[:-1][::-1], blocks),
    ]
    in_parts = [
        reduce_blocks(found[2], found[3], 1, bits[1:], blocks),
        reduce_blocks(found[6], found[7], top, bits[:-1][::-1], blocks),
    ]

    def spread(parts):
        joined = reduce_groups(parts, groups, my_group)
        return join_cores(joined.reshape((-1,) + joined.shape[2:]), core)

    found = call(
        functools.partial(attention_back_kernel, blocks, halved),
        "attention_back",
        (seq_count, pairs),
        [(a,) + seg_block for a in (queries, keys, values, attended_f, counts)]
        + [(a,) + mem_block for a in mem]
        + [(a,) + tok_block for a in grad_att],
        [
            (
                (3, seq_count, tok, part),
                BF16,
                (3, 1, tok, 128),
                lambda s, p, sc: (0, s, 0, p),
            )
        ]
        * blocks
        + (
            [
                (
                    (blocks, 3, seq_count, tok, 128),
                    BF16,
                    (blocks, 3, 1, tok, 128),
                    lambda s, p, sc: (0, 0, s, 0, 0),
                )
            ]
            if halved
            else []
        ),
        [
            pltpu.VMEM((2, seg_rows, 128), BF16),
            pltpu.VMEM((blocks, tok, 128), BF16),
            pltpu.VMEM((3, blocks, tok, 128), BF16),
        ],
        scalars,
        48,
        (10 * seq_count * seg_rows * seg_rows * part, 24 * seq_count * seg_rows * part),
    )
    own_grads = [g.reshape(3, rows, part) for g in found[:blocks]]
    grads = [own_grads[0]] + [swap(own_grads[m], "blk", m) for m in range(1, blocks)]

    found_tokens = call(
        functools.partial(tokens_kernel, blocks),
        "tokens_back",
        (blocks,),
        [flat, grad_res, gain_one] + grads + [head_weights(j) for j in range(3)],
        [((rows, width), F32), ((2, width), F32)],
        [pltpu.VMEM((rows, width), F32)],
        scalars,
        32,
        (6 * rows * width * width, 6 * width * width + 12 * rows * width),
    )
    grad_tokens, sums_one = found_tokens

    own = jnp.concatenate([jnp.concatenate([g[i] for i in range(3)], 1) for g in own_grads], 0)
    normed_all = jnp.concatenate(normed, 0)
    qkv_grad = tn(normed_all, own)
    qkv_grad = qkv_grad.astype(BF16).reshape(blocks, part, 3 * part)
    if halved:
        halves = qkv_grad.reshape(blocks, 2, part // 2, 3 * part)
        came = swap(pick(halves, 1 - core, 1), "grp", 1)
        qkv_grad = add(pick(halves, core, 1), came)
    else:
        qkv_grad = add(qkv_grad, swap(qkv_grad, "grp", 1))
    parts = [pick(qkv_grad, my_block)]
    for mask in range(1, blocks):
        parts.append(swap(pick(qkv_grad, my_block ^ mask), "blk", mask))
    order = my_block ^ jnp.arange(blocks)
    parts = jnp.take(jnp.stack(parts), order, axis=0).reshape(blocks, -1, 3, part)
    parts = jnp.transpose(parts, (1, 2, 0, 3)).reshape(-1, 3 * width)
    joined = reduce_groups([[parts]], groups, my_group).reshape(-1, 3 * width)
    if halved:
        joined = join_cores(joined, core)
    grad_qkv = joined.reshape(part, 3 * width).astype(F32)

    both = spread(down_parts)
    grad_down = both[:, :tile].reshape(2 * tile, width).astype(F32)
    grad_out = both[:, tile:].reshape(2, part // 2, 2, width // 2)
    grad_out = jnp.transpose(grad_out, (2, 1, 0, 3)).reshape(part, width).astype(F32)
    both = spread(in_parts).reshape(2, part, blocks, tile)
    grad_in = jnp.transpose(both, (1, 2, 0, 3)).reshape(part, hidden_width).astype(F32)

    vectors = jnp.concatenate([sums_one, sums_two], 0)
    for bit in range(groups.bit_length() - 1):
        vectors = vectors + swap(vectors, "grp", 1 << bit)
    for bit in bits:
        vectors = vectors + swap(vectors, "blk", bit)
    vectors = pick(vectors.reshape(4, blocks, part), my_block, 1)
    return (
        mixed.reshape(tokens.shape),
        grad_tokens.reshape(tokens.shape),
        vectors[0],
        vectors[1],
        grad_qkv,
        grad_out,
        vectors[2],
        vectors[3],
        grad_in,
        grad_down,
    )


def solution(mesh):
    rows = P("grp", "blk", None)
    in_specs = (rows,) + (P(),) * 8 + (rows, rows, P(), P(), rows)
    out_specs = (rows, rows) + (P("blk"),) * 2 + (P("blk", None),) * 2
    out_specs = out_specs + (P("blk"),) * 2 + (P("blk", None),) * 2
    return jax.shard_map(
        on_device, mesh=mesh, in_specs=in_specs, out_specs=out_specs, check_vma=False
    )
```

time: 574 us -> 432 us (0.75)
  matrix products: 104 us -> 1.9 us
  local copies, waits for them, and re-layouts: 135 us -> 50.4 us
  Pallas kernels: 0 us -> 74.1 us
  other arithmetic: 57.5 us -> 36.8 us
  starting transfers between devices: 71.8 us -> 60.8 us
  waiting for transfers between devices: 191 us -> 200 us
  between operations: 10.3 us -> 1.79 us
    dot_general x22 -> x1, matrix products: 104 us -> 1.9 us  [tn(): lax.dot_general(left, right, (((0,), (0,)), ((), ())), preferred_element_...]
    pallas_call x0 -> x10, Pallas kernels: none -> 74.1 us  [call(): pl.pallas_call(kernel, grid_spec=spec, out_shape=out_shapes, compiler_par...]
    unnamed x144 -> x67, local copies, waits for them, and re-layouts: 48.3 us -> 16.9 us
    dynamic_slice x13 -> x1, local copies, waits for them, and re-layouts: 21.3 us -> 0.06 us  [pick(): return lax.dynamic_index_in_dim(values, index, dim, keepdims=False)]
    convert_element_type x1 -> x4, local copies, waits for them, and re-layouts: 1.55 us -> 17.1 us  [the longest x2 11.9 us: on_device(): jnp.transpose(both, (1, 2, 0, 3)).reshape(part, hidden_width).astype(F32)]
    reshape x5, local copies, waits for them, and re-layouts: 15.2 us -> 0.59 us  [the longest x1 0.57 us: reduce_groups(): halves = whole.reshape((2, whole.shape[0] // 2) + whole.shape[1:])]
    ppermute x66 -> x55, starting transfers between devices: 71.8 us -> 60.8 us  [swap(): return lax.ppermute(values, axis, [(i, i ^ mask) for i in range(size)])]
    another operation x11 -> x3, other arithmetic: 13.1 us -> 2.3 us  [the longest x2 2.2 us: fetch_banks(): both = jnp.stack([keys, values])]
  transfers between devices with their start and end apart: 66 -> 55, of which waited for: 33 -> 25; matrix products, arithmetic and copies ran while one was open for 50% -> 13% of each run, Pallas kernels for 0% -> 11%
where the time goes in v2:
time: 432 us; the launch traced here: 426 us
  waiting for transfers between devices  200 us (46%)
  Pallas kernels  74.1 us (17%)
  starting transfers between devices  60.8 us (14%)
  local copies, waits for them, and re-layouts  50.4 us (12%)
  other arithmetic  36.8 us (9%)
    ppermute x55, waiting for transfers between devices, swap(): return lax.ppermute(values, axis, [(i, i ^ mask) for i in range(size)])  200 us
    pallas_call x10, Pallas kernels, call(): pl.pallas_call(kernel, grid_spec=spec, out_shape=out_shapes, compiler_par...  74.1 us
    ppermute x55, starting transfers between devices, swap(): return lax.ppermute(values, axis, [(i, i ^ mask) for i in range(size)])  60.8 us
    unnamed x67, local copies, waits for them, and re-layouts  16.9 us
    convert_element_type x2, local copies, waits for them, and re-layouts, on_device(): jnp.transpose(both, (1, 2, 0, 3)).reshape(part, hidden_width).astype(F32)  11.9 us
    convert_element_type x11, other arithmetic, add(): return total.astype(BF16)  11.5 us
  transfers between devices with their start and end apart: 55, of which 25 were waited for; matrix products, arithmetic and copies ran while one was open for 13% of the time, Pallas kernels for 11%

profile of v2, /device:TPU:0, one launch (start us, length us, event | category | flops | bytes accessed | tf_op | source)
XLA Modules:
  0.0 426.1 jit_solution(11777703042820447444)
XLA Ops:
  4.3 5.0 %collective-permute-start.6 = (bf16[4,32,1024]{2,1,0:T(8,128)(2,1)S(1)}, bf16[4,32,1024]{2,1,0:T(8,128)(2,1)S(1)}, u32[]{:S(2)}, u32[]{:S(2)}) collective-permute-start(bf16[4,32,1024]{2,1,0:T(8,128)(2,1)S(1)} %get-tuple-element.120), channel_id=1, source_target_pairs={{0,6},{1,7},{2,4},{3,5},{4,2},{5,3},{6,0},{7,1},{8,14},{9,15},{10,... | collective-permute-start | bytes 786440 | tf_op jit(solution)/shard_map/ppermute | solution.py:22
  10.2 6.4 %collective-permute-done.6 = bf16[4,32,1024]{2,1,0:T(8,128)(2,1)S(1)} collective-permute-done((bf16[4,32,1024]{2,1,0:T(8,128)(2,1)S(1)}, bf16[4,32,1024]{2,1,0:T(8,128)(2,1)S(1)}, u32[]{:S(2)}, u32[]{:S(2)}) %collective-permute-start.6) | collective-permute-done | bytes 262176 | tf_op jit(solution)/shard_map/ppermute | solution.py:22
  16.6 15.4 %collective-permute-done.5 = bf16[4,32,1024]{2,1,0:T(8,128)(2,1)S(1)} collective-permute-done((bf16[4,32,1024]{2,1,0:T(8,128)(2,1)S(1)}, bf16[4,32,1024]{2,1,0:T(8,128)(2,1)S(1)}, u32[]{:S(2)}, u32[]{:S(2)}) %collective-permute-start.5) | collective-permute-done | bytes 262176 | tf_op jit(solution)/shard_map/ppermute | solution.py:22
  40.2 6.7 %collective-permute-done.7 = bf16[4,32,1024]{2,1,0:T(8,128)(2,1)S(1)} collective-permute-done((bf16[4,32,1024]{2,1,0:T(8,128)(2,1)S(1)}, bf16[4,32,1024]{2,1,0:T(8,128)(2,1)S(1)}, u32[]{:S(2)}, u32[]{:S(2)}) %collective-permute-start.7) | collective-permute-done | bytes 262176 | tf_op jit(solution)/shard_map/ppermute | solution.py:22
  46.9 9.6 %collective-permute-done.8 = bf16[4,32,1024]{2,1,0:T(8,128)(2,1)S(1)} collective-permute-done((bf16[4,32,1024]{2,1,0:T(8,128)(2,1)S(1)}, bf16[4,32,1024]{2,1,0:T(8,128)(2,1)S(1)}, u32[]{:S(2)}, u32[]{:S(2)}) %collective-permute-start.8) | collective-permute-done | bytes 262176 | tf_op jit(solution)/shard_map/ppermute | solution.py:22
  67.2 7.1 %collective-permute-done.2.rows = bf16[256,1024]{1,0:T(8,128)(2,1)} collective-permute-done((bf16[256,1024]{1,0:T(8,128)(2,1)S(1)}, bf16[256,1024]{1,0:T(8,128)(2,1)}, u32[]{:S(2)}, u32[]{:S(2)}) %collective-permute-start.2) | collective-permute-done | bytes 524320 | tf_op jit(solution)/shard_map/ppermute | solution.py:22
  93.1 5.9 %own_keys.1 = (bf16[2,512,256]{2,1,0:T(8,128)(2,1)S(1)}, bf16[2,512,256]{2,1,0:T(8,128)(2,1)S(1)}, bf16[2,512,256]{2,1,0:T(8,128)(2,1)S(1)}, f32[2,512,256]{2,1,0:T(8,128)S(1)}, f32[2,512,256]{2,1,0:T(8,128)S(1)}) custom-call(s32[6]{0:T(128)S(1)} %stack.149.sc, bf16[2,128,768]{2,1,0:T(8,128)(2,1)S(1)} %bitcast.170, bf16[2,128,768]{2,1,0:T(8,128)(2,1)S(1)} %bitcast.171, ...), custom_call_target="tpu_custom_call" | custom-call | flops 268435456 | bytes 2097152 | tf_op jit(solution)/shard_map/own_keys/pallas_call | solution.py:68
  99.0 6.6 %cached_keys.1 = (f32[2,512,256]{2,1,0:T(8,128)S(1)}, f32[2,512,256]{2,1,0:T(8,128)S(1)}, bf16[2,128,256]{2,1,0:T(8,128)(2,1)S(1)}, bf16[2,128,256]{2,1,0:T(8,12...) custom-call(s32[6]{0:T(128)S(1)} %stack.149.sc, ...), custom_call_target="tpu_custom_call" | custom-call | flops 536870912 | bytes 4194304 | tf_op jit(solution)/shard_map/cached_keys/pallas_call | solution.py:68
  116.3 20.5 %feed.1 = (bf16[256,1024]{1,0:T(8,128)(2,1)}, f32[256,1024]{1,0:T(8,128)S(1)}, bf16[4,256,512]{2,1,0:T(8,128)(2,1)S(1)}, bf16[4,256,512]{2,1,0:T(8,128)(2,1)}, b...) custom-call(s32[6]{0:T(128)S(1)} %stack.149.sc, ...), custom_call_target="tpu_custom_call" | custom-call | flops 8589934592 | bytes 24641536 | tf_op jit(solution)/shard_map/feed/pallas_call | solution.py:68
  146.2 14.5 %attention_back.1 = (bf16[3,2,128,256]{3,2,1,0:T(8,128)(2,1)S(1)}, bf16[3,2,128,256]{3,2,1,0:T(8,128)(2,1)S(1)}, bf16[3,2,128,256]{3,2,1,0:T(8,128)(2,1)}, bf16[...) custom-call(s32[6]{0:T(128)S(1)} %stack.149.sc, bf16[2,512,256]{2,1,0:T(8,128)(2,1)S(1)} %get-tuple-element.62.refs_0_, ...), custom_call_target="tpu_custom_call" | custom-call | flops 1342177280 | bytes 6291456 | tf_op jit(solution)/shard_map/attention_back/pallas_call | solution.py:68
  171.4 11.6 %weights.1 = (bf16[2,320,1024]{2,1,0:T(8,128)(2,1)}, bf16[2,320,1024]{2,1,0:T(8,128)(2,1)}, bf16[2,128,2048]{2,1,0:T(8,128)(2,1)}, bf16[2,128,2048]{2,1,0:T(8,12...) custom-call(s32[6]{0:T(128)S(1)} %stack.149.sc, ...), custom_call_target="tpu_custom_call" | custom-call | flops 8589934592 | bytes 41943040 | tf_op jit(solution)/shard_map/weights/pallas_call | solution.py:68
  193.7 6.2 %tokens_back.1 = (f32[256,1024]{1,0:T(8,128)}, f32[2,1024]{1,0:T(2,128)S(1)}) custom-call(s32[6]{0:T(128)S(1)} %stack.149.sc, bf16[256,1024]{1,0:T(8,128)(2,1)S(1)} %bitcast.187, f32[256,1024]{1,0:T(8,128)S(1)} %copy-done.6, bf16[1,1024]{1,0:T(2,128)(2,1)S(1)} %reshape.326.gain, bf16[3,256,256]{2,1,0:T(8,128)(2,1)S(1)} %bitcast.188, ...), custom_call_target="tpu_custom_call" | custom-call | flops 1610612736 | bytes 9437184 | tf_op jit(solution)/shard_map/tokens_back/pallas_call | solution.py:68
  199.9 14.5 %collective-permute-done.31 = bf16[128,768]{1,0:T(8,128)(2,1)S(1)} collective-permute-done((bf16[128,768]{1,0:T(8,128)(2,1)S(1)}, bf16[128,768]{1,0:T(8,128)(2,1)S(1)}, u32[]{:S(2)}, u32[]{:S(2)}) %collective-permute-start.31) | collective-permute-done | bytes 196640 | tf_op jit(solution)/shard_map/ppermute | solution.py:22
  226.0 20.3 %collective-permute-done.39 = bf16[2,320,1024]{2,1,0:T(8,128)(2,1)} collective-permute-done((bf16[2,320,1024]{2,1,0:T(8,128)(2,1)}, bf16[2,320,1024]{2,1,0:T(8,128)(2,1)}, u32[]{:S(2)}, u32[]{:S(2)}) %collective-permute-start.39) | collective-permute-done | bytes 1310752 | tf_op jit(solution)/shard_map/ppermute | solution.py:22
  253.0 8.3 %collective-permute-done.48 = bf16[128,2048]{1,0:T(8,128)(2,1)S(1)} collective-permute-done((bf16[128,2048]{1,0:T(8,128)(2,1)S(1)}, bf16[128,2048]{1,0:T(8,128)(2,1)S(1)}, u32[]{:S(2)}, u32[]{:S(2)}) %collective-permute-start.48) | collective-permute-done | bytes 524320 | tf_op jit(solution)/shard_map/ppermute | solution.py:22
  267.5 6.6 %collective-permute-done.40 = bf16[320,1024]{1,0:T(8,128)(2,1)S(1)} collective-permute-done((bf16[320,1024]{1,0:T(8,128)(2,1)S(1)}, bf16[320,1024]{1,0:T(8,128)(2,1)S(1)}, u32[]{:S(2)}, u32[]{:S(2)}) %collective-permute-start.40) | collective-permute-done | bytes 655392 | tf_op jit(solution)/shard_map/ppermute | solution.py:22
  281.9 19.1 %collective-permute-done.51 = bf16[128,2048]{1,0:T(8,128)(2,1)S(1)} collective-permute-done((bf16[128,2048]{1,0:T(8,128)(2,1)S(1)}, bf16[128,2048]{1,0:T(8,128)(2,1)S(1)}, u32[]{:S(2)}, u32[]{:S(2)}) %collective-permute-start.51) | collective-permute-done | bytes 524320 | tf_op jit(solution)/shard_map/ppermute | solution.py:22
  303.3 8.9 %collective-permute-done.43 = bf16[320,1024]{1,0:T(8,128)(2,1)S(1)} collective-permute-done((bf16[320,1024]{1,0:T(8,128)(2,1)S(1)}, bf16[320,1024]{1,0:T(8,128)(2,1)S(1)}, u32[]{:S(2)}, u32[]{:S(2)}) %collective-permute-start.43) | collective-permute-done | bytes 655392 | tf_op jit(solution)/shard_map/ppermute | solution.py:22
  317.7 27.3 %collective-permute-done.52 = bf16[128,2048]{1,0:T(8,128)(2,1)S(1)} collective-permute-done((bf16[128,2048]{1,0:T(8,128)(2,1)S(1)}, bf16[128,2048]{1,0:T(8,128)(2,1)S(1)}, u32[]{:S(2)}, u32[]{:S(2)}) %collective-permute-start.52) | collective-permute-done | bytes 524320 | tf_op jit(solution)/shard_map/ppermute | solution.py:22
  345.2 8.4 %collective-permute-done.44 = bf16[320,1024]{1,0:T(8,128)(2,1)S(1)} collective-permute-done((bf16[320,1024]{1,0:T(8,128)(2,1)S(1)}, bf16[320,1024]{1,0:T(8,128)(2,1)S(1)}, u32[]{:S(2)}, u32[]{:S(2)}) %collective-permute-start.44) | collective-permute-done | bytes 655392 | tf_op jit(solution)/shard_map/ppermute | solution.py:22
  356.3 17.4 %collective-permute-done.24 = f32[4,1024]{1,0:T(4,128)S(1)} collective-permute-done((f32[4,1024]{1,0:T(4,128)S(1)}, f32[4,1024]{1,0:T(4,128)S(1)}, u32[]{:S(2)}, u32[]{:S(2)}) %collective-permute-start.24) | collective-permute-done | bytes 16416 | tf_op jit(solution)/shard_map/ppermute | solution.py:22
  373.7 4.6 %collective-permute-done.25 = f32[4,1024]{1,0:T(4,128)S(1)} collective-permute-done((f32[4,1024]{1,0:T(4,128)S(1)}, f32[4,1024]{1,0:T(4,128)S(1)}, u32[]{:S(2)}, u32[]{:S(2)}) %collective-permute-start.25) | collective-permute-done | bytes 16416 | tf_op jit(solution)/shard_map/ppermute | solution.py:22
  399.5 5.3 %copy.33 = f32[256,4,2,512]{3,2,1,0:T(2,128)} copy(f32[256,4,2,512]{3,1,0,2:T(4,128)S(1)} %convert_bitcast_fusion) | data formatting | bytes 8388608 | tf_op jit(solution)/shard_map/convert_element_type | solution.py:804
  404.8 6.6 %reshape.356 = f32[256,4096]{1,0:T(8,128)} reshape(f32[256,4,2,512]{3,2,1,0:T(2,128)} %copy.33) | data formatting | bytes 8388608 | tf_op jit(solution)/shard_map/convert_element_type | solution.py:804
  (252 shorter events, 161.4 us)
Async XLA Ops:
  61.5 28.4 %collective-permute-start = (bf16[256,1024]{1,0:T(8,128)(2,1)S(1)}, bf16[256,1024]{1,0:T(8,128)(2,1)}, u32[]{:S(2)}, u32[]{:S(2)}) collective-permute-start(bf16[256,1024]{1,0:T(8,128)(2,1)S(1)} %bitcast.184), channel_id=1, source_target_pairs={{0,8},{8,0},{16,24},{24,16},{1,9},{9,1},{17,25},{25,17},{2,10},{10... | collective-permute-start | bytes 1572872 | tf_op jit(solution)/shard_map/ppermute | solution.py:22
  64.5 34.4 %collective-permute-start.13 = (bf16[2,2,128,256]{3,2,1,0:T(8,128)(2,1)}, bf16[2,2,128,256]{3,2,1,0:T(8,128)(2,1)S(1)}, u32[]{:S(2)}, u32[]{:S(2)}) collective-permute-start(bf16[2,2,128,256]{3,2,1,0:T(8,128)(2,1)} %get-tuple-element.115), channel_id=1, source_target_pairs={{0,24},{8,16},{16,8},{24,0},{1,25},{9,17},{17,9},{25,1},{2,26},{10... | collective-permute-start | bytes 786440 | tf_op jit(solution)/shard_map/ppermute | solution.py:22
  66.7 32.3 %collective-permute-start.11 = (bf16[2,2,128,256]{3,2,1,0:T(8,128)(2,1)}, bf16[2,2,128,256]{3,2,1,0:T(8,128)(2,1)S(1)}, u32[]{:S(2)}, u32[]{:S(2)}) collective-permute-start(bf16[2,2,128,256]{3,2,1,0:T(8,128)(2,1)} %get-tuple-element.117), channel_id=1, source_target_pairs={{0,8},{8,0},{16,24},{24,16},{1,9},{9,1},{17,25},{25,17},{2,10},{10... | collective-permute-start | bytes 786440 | tf_op jit(solution)/shard_map/ppermute | solution.py:22
  142.3 26.7 %collective-permute-start.37 = (bf16[256,1024]{1,0:T(8,128)(2,1)S(1)}, bf16[256,1024]{1,0:T(8,128)(2,1)S(1)}, u32[]{:S(2)}, u32[]{:S(2)}) collective-permute-start(bf16[256,1024]{1,0:T(8,128)(2,1)S(1)} %bitcast.195), channel_id=1, source_target_pairs={{0,1},{1,0},{2,3},{3,2},{4,5},{5,4},{6,7},{7,6},{8,9},{9,8},{10,11... | collective-permute-start | bytes 1572872 | tf_op jit(solution)/shard_map/ppermute | solution.py:22
  142.3 27.3 %collective-permute-start.38 = (bf16[256,2560]{1,0:T(8,128)(2,1)}, bf16[256,2560]{1,0:T(8,128)(2,1)S(1)}, u32[]{:S(2)}, u32[]{:S(2)}) collective-permute-start(bf16[256,2560]{1,0:T(8,128)(2,1)} %get-tuple-element.93), channel_id=1, source_target_pairs={{0,1},{1,0},{2,3},{3,2},{4,5},{5,4},{6,7},{7,6},{8,9},{9,8},{10,11... | collective-permute-start | bytes 3932168 | tf_op jit(solution)/shard_map/ppermute | solution.py:22
  183.0 38.2 %collective-permute-start.47 = (bf16[2,128,2048]{2,1,0:T(8,128)(2,1)}, bf16[2,128,2048]{2,1,0:T(8,128)(2,1)}, u32[]{:S(2)}, u32[]{:S(2)}) collective-permute-start(bf16[2,128,2048]{2,1,0:T(8,128)(2,1)} %get-tuple-element.102), channel_id=1, source_target_pairs={{0,8},{8,0},{16,24},{24,16},{1,9},{9,1},{17,25},{25,17},{2,10},{10... | collective-permute-start | bytes 3145736 | tf_op jit(solution)/shard_map/ppermute | solution.py:22
  186.2 28.2 %collective-permute-start.31 = (bf16[128,768]{1,0:T(8,128)(2,1)S(1)}, bf16[128,768]{1,0:T(8,128)(2,1)S(1)}, u32[]{:S(2)}, u32[]{:S(2)}) collective-permute-start(bf16[128,768]{1,0:T(8,128)(2,1)S(1)} %get-tuple-element.126), channel_id=1, source_target_pairs={{0,24},{8,16},{16,8},{24,0},{1,25},{9,17},{17,9},{25,1},{2,26},{10... | collective-permute-start | bytes 589832 | tf_op jit(solution)/shard_map/ppermute | solution.py:22
  187.7 26.7 %collective-permute-start.30 = (bf16[128,768]{1,0:T(8,128)(2,1)S(1)}, bf16[128,768]{1,0:T(8,128)(2,1)S(1)}, u32[]{:S(2)}, u32[]{:S(2)}) collective-permute-start(bf16[128,768]{1,0:T(8,128)(2,1)S(1)} %get-tuple-element.127), channel_id=1, source_target_pairs={{0,16},{8,24},{16,0},{24,8},{1,17},{9,25},{17,1},{25,9},{2,18},{10... | collective-permute-start | bytes 589832 | tf_op jit(solution)/shard_map/ppermute | solution.py:22
  188.4 28.5 %collective-permute-start.29 = (bf16[128,768]{1,0:T(8,128)(2,1)S(1)}, bf16[128,768]{1,0:T(8,128)(2,1)S(1)}, u32[]{:S(2)}, u32[]{:S(2)}) collective-permute-start(bf16[128,768]{1,0:T(8,128)(2,1)S(1)} %get-tuple-element.128), channel_id=1, source_target_pairs={{0,8},{8,0},{16,24},{24,16},{1,9},{9,1},{17,25},{25,17},{2,10},{10... | collective-permute-start | bytes 589832 | tf_op jit(solution)/shard_map/ppermute | solution.py:22
  189.8 33.4 %collective-permute-start.49 = (bf16[2,128,2048]{2,1,0:T(8,128)(2,1)}, bf16[2,128,2048]{2,1,0:T(8,128)(2,1)}, u32[]{:S(2)}, u32[]{:S(2)}) collective-permute-start(bf16[2,128,2048]{2,1,0:T(8,128)(2,1)} %get-tuple-element.104), channel_id=1, source_target_pairs={{0,16},{8,24},{16,0},{24,8},{1,17},{9,25},{17,1},{25,9},{2,18},{10... | collective-permute-start | bytes 3145736 | tf_op jit(solution)/shard_map/ppermute | solution.py:22
  214.4 139.8 %collective-permute-start.23 = (f32[4,1024]{1,0:T(4,128)S(1)}, f32[4,1024]{1,0:T(4,128)S(1)}, u32[]{:S(2)}, u32[]{:S(2)}) collective-permute-start(f32[4,1024]{1,0:T(4,128)S(1)} %pad_maximum_fusion.3), channel_id=1, source_target_pairs={{0,1},{1,0},{2,3},{3,2},{4,5},{5,4},{6,7},{7,6},{8,9},{9,8},{10,11... | collective-permute-start | bytes 49160 | tf_op jit(solution)/shard_map/ppermute | solution.py:22
  214.4 31.9 %collective-permute-start.39 = (bf16[2,320,1024]{2,1,0:T(8,128)(2,1)}, bf16[2,320,1024]{2,1,0:T(8,128)(2,1)}, u32[]{:S(2)}, u32[]{:S(2)}) collective-permute-start(bf16[2,320,1024]{2,1,0:T(8,128)(2,1)} %get-tuple-element.98), channel_id=1, source_target_pairs={{0,8},{8,0},{16,24},{24,16},{1,9},{9,1},{17,25},{25,17},{2,10},{10... | collective-permute-start | bytes 3932168 | tf_op jit(solution)/shard_map/ppermute | solution.py:22
  218.0 32.1 %collective-permute-start.41 = (bf16[2,320,1024]{2,1,0:T(8,128)(2,1)}, bf16[2,320,1024]{2,1,0:T(8,128)(2,1)}, u32[]{:S(2)}, u32[]{:S(2)}) collective-permute-start(bf16[2,320,1024]{2,1,0:T(8,128)(2,1)} %get-tuple-element.100), channel_id=1, source_target_pairs={{0,16},{8,24},{16,0},{24,8},{1,17},{9,25},{17,1},{25,9},{2,18},{10... | collective-permute-start | bytes 3932168 | tf_op jit(solution)/shard_map/ppermute | solution.py:22
  222.5 38.7 %collective-permute-start.48 = (bf16[128,2048]{1,0:T(8,128)(2,1)S(1)}, bf16[128,2048]{1,0:T(8,128)(2,1)S(1)}, u32[]{:S(2)}, u32[]{:S(2)}) collective-permute-start(bf16[128,2048]{1,0:T(8,128)(2,1)S(1)} %fusion.42), channel_id=1, source_target_pairs={{0,16},{8,24},{16,0},{24,8},{1,17},{9,25},{17,1},{25,9},{2,18},{10... | collective-permute-start | bytes 1572872 | tf_op jit(solution)/shard_map/ppermute | solution.py:22
  224.5 41.2 %collective-permute-start.50 = (bf16[128,2048]{1,0:T(8,128)(2,1)S(1)}, bf16[128,2048]{1,0:T(8,128)(2,1)S(1)}, u32[]{:S(2)}, u32[]{:S(2)}) collective-permute-start(bf16[128,2048]{1,0:T(8,128)(2,1)S(1)} %fusion.43), channel_id=1, source_target_pairs={{0,8},{8,0},{16,24},{24,16},{1,9},{9,1},{17,25},{25,17},{2,10},{10... | collective-permute-start | bytes 1572872 | tf_op jit(solution)/shard_map/ppermute | solution.py:22
  267.5 33.6 %collective-permute-start.51 = (bf16[128,2048]{1,0:T(8,128)(2,1)S(1)}, bf16[128,2048]{1,0:T(8,128)(2,1)S(1)}, u32[]{:S(2)}, u32[]{:S(2)}) collective-permute-start(bf16[128,2048]{1,0:T(8,128)(2,1)S(1)} %broadcast_select_fusion.1), channel_id=1, source_target_pairs={{0,2},{1,3},{2,0},{3,1},{4,6},{5,7},{6,4},{7,5},{8,10},{9,11},{10,... | collective-permute-start | bytes 1572872 | tf_op jit(solution)/shard_map/ppermute | solution.py:22
  276.2 36.0 %collective-permute-start.43 = (bf16[320,1024]{1,0:T(8,128)(2,1)S(1)}, bf16[320,1024]{1,0:T(8,128)(2,1)S(1)}, u32[]{:S(2)}, u32[]{:S(2)}) collective-permute-start(bf16[320,1024]{1,0:T(8,128)(2,1)S(1)} %broadcast_select_fusion), channel_id=1, source_target_pairs={{0,2},{1,3},{2,0},{3,1},{4,6},{5,7},{6,4},{7,5},{8,10},{9,11},{10,... | collective-permute-start | bytes 1966088 | tf_op jit(solution)/shard_map/ppermute | solution.py:22
  280.9 34.1 %collective-permute-start.33 = (bf16[64,3072]{1,0:T(8,128)(2,1)S(1)}, bf16[64,3072]{1,0:T(8,128)(2,1)S(1)}, u32[]{:S(2)}, u32[]{:S(2)}) collective-permute-start(bf16[64,3072]{1,0:T(8,128)(2,1)S(1)} %fusion.39), channel_id=1, source_target_pairs={{0,4},{1,5},{2,6},{3,7},{4,0},{5,1},{6,2},{7,3},{8,12},{9,13},{10,... | collective-permute-start | bytes 1179656 | tf_op jit(solution)/shard_map/ppermute | solution.py:22
  302.8 42.2 %collective-permute-start.52 = (bf16[128,2048]{1,0:T(8,128)(2,1)S(1)}, bf16[128,2048]{1,0:T(8,128)(2,1)S(1)}, u32[]{:S(2)}, u32[]{:S(2)}) collective-permute-start(bf16[128,2048]{1,0:T(8,128)(2,1)S(1)} %add_convert_fusion.5), channel_id=1, source_target_pairs={{0,4},{1,5},{2,6},{3,7},{4,0},{5,1},{6,2},{7,3},{8,12},{9,13},{10,... | collective-permute-start | bytes 1572872 | tf_op jit(solution)/shard_map/ppermute | solution.py:22
  314.5 39.1 %collective-permute-start.44 = (bf16[320,1024]{1,0:T(8,128)(2,1)S(1)}, bf16[320,1024]{1,0:T(8,128)(2,1)S(1)}, u32[]{:S(2)}, u32[]{:S(2)}) collective-permute-start(bf16[320,1024]{1,0:T(8,128)(2,1)S(1)} %add_convert_fusion.1), channel_id=1, source_target_pairs={{0,4},{1,5},{2,6},{3,7},{4,0},{5,1},{6,2},{7,3},{8,12},{9,13},{10,... | collective-permute-start | bytes 1966088 | tf_op jit(solution)/shard_map/ppermute | solution.py:22
  315.1 38.9 %collective-permute-start.34 = (bf16[64,3072]{1,0:T(8,128)(2,1)S(1)}, bf16[64,3072]{1,0:T(8,128)(2,1)S(1)}, u32[]{:S(2)}, u32[]{:S(2)}) collective-permute-start(bf16[64,3072]{1,0:T(8,128)(2,1)S(1)} %add_convert_fusion.8), channel_id=1, source_target_pairs={{0,2},{1,3},{2,0},{3,1},{4,6},{5,7},{6,4},{7,5},{8,10},{9,11},{10,... | collective-permute-start | bytes 1179656 | tf_op jit(solution)/shard_map/ppermute | solution.py:22
  345.1 41.3 %collective-permute-start.53 = (bf16[128,2048]{1,0:T(8,128)(2,1)S(1)}, bf16[128,2048]{1,0:T(8,128)(2,1)S(1)}, u32[]{:S(2)}, u32[]{:S(2)}) collective-permute-start(bf16[128,2048]{1,0:T(8,128)(2,1)S(1)} %add_convert_fusion.4), channel_id=1, source_target_pairs={{0,2},{1,3},{2,0},{3,1},{4,6},{5,7},{6,4},{7,5},{8,10},{9,11},{10,... | collective-permute-start | bytes 1572872 | tf_op jit(solution)/shard_map/ppermute | solution.py:22
  353.9 34.9 %collective-permute-start.45 = (bf16[320,1024]{1,0:T(8,128)(2,1)S(1)}, bf16[320,1024]{1,0:T(8,128)(2,1)}, u32[]{:S(2)}, u32[]{:S(2)}) collective-permute-start(bf16[320,1024]{1,0:T(8,128)(2,1)S(1)} %add_convert_fusion), channel_id=1, source_target_pairs={{0,2},{1,3},{2,0},{3,1},{4,6},{5,7},{6,4},{7,5},{8,10},{9,11},{10,... | collective-permute-start | bytes 1966088 | tf_op jit(solution)/shard_map/ppermute | solution.py:22
  354.1 37.2 %collective-permute-start.35 = (bf16[128,3072]{1,0:T(8,128)(2,1)S(1)}, bf16[128,3072]{1,0:T(8,128)(2,1)}, u32[]{:S(2)}, u32[]{:S(2)}) collective-permute-start(bf16[128,3072]{1,0:T(8,128)(2,1)S(1)} %bitcast.209), channel_id=1, source_target_pairs={{0,1},{1,0},{2,3},{3,2},{4,5},{5,4},{6,7},{7,6},{8,9},{9,8},{10,11... | collective-permute-start | bytes 2359304 | tf_op jit(solution)/shard_map/ppermute | solution.py:22
  (65 other events, 691.8 us)

commit v3 on v2

v3 whole, which is shorter than its diff:
```python
import functools

import jax
import jax.numpy as jnp
from jax import lax
from jax.experimental import pallas as pl
from jax.experimental.pallas import tpu as pltpu
from jax.sharding import PartitionSpec as P

HEADS = 16
F32 = jnp.float32
BF16 = jnp.bfloat16
MIB = 1 << 20
EPS = 1e-05
FAR = -1e30
GELU_A = 0.7978845608028654
GELU_B = 0.044715


def swap(values, axis, mask):
    size = lax.axis_size(axis)
    return lax.ppermute(values, axis, [(i, i ^ mask) for i in range(size)])


def pick(values, index, dim=0):
    return lax.dynamic_index_in_dim(values, index, dim, keepdims=False)


def nn(left, right):
    return lax.dot_general(left, right, (((1,), (0,)), ((), ())), preferred_element_type=F32)


def nt(left, right):
    return lax.dot_general(left, right, (((1,), (1,)), ((), ())), preferred_element_type=F32)


def tn(left, right):
    return lax.dot_general(left, right, (((0,), (0,)), ((), ())), preferred_element_type=F32)


def params(mib):
    return pltpu.CompilerParams(vmem_limit_bytes=mib * MIB)


ANYWHERE = pl.BlockSpec(memory_space=pl.ANY)
EVERY = range(100)
COMPUTE = (
    "project",
    "own_keys",
    "cached_keys",
    "feed",
    "attention_back",
    "grad_qkv",
    "grad_in",
    "grad_down",
    "tokens_back",
)
LONG = pl.CostEstimate(flops=10**11, bytes_accessed=10**6, transcendentals=0)
SHORT = pl.CostEstimate(flops=10**10, bytes_accessed=10**11, transcendentals=0)
OUT_HBM = {
    "project": (0,),
    "own_keys": EVERY,
    "cached_keys": (0, 1),
    "feed": (0, 1, 2, 4, 5, 6, 8, 9, 10, 11, 12, 13, 14, 15),
}
IN_HBM = {"cached_keys": (0, 1, 2, 3), "attention_back": EVERY, "grad_qkv": (0, 1, 2, 3)}


def call(kernel, name, grid, ins, outs, scratch, scalars, mib, tokens=()):
    def whole(shape):
        return pl.BlockSpec(shape, lambda *_: (0,) * len(shape))

    in_specs, arrays = [], []
    for item in ins:
        if isinstance(item, tuple):
            arrays.append(item[0])
            in_specs.append(pl.BlockSpec(item[1], item[2]))
        else:
            arrays.append(item)
            in_specs.append(whole(item.shape))
    out_shapes, out_specs = [], []
    for item in outs:
        out_shapes.append(jax.ShapeDtypeStruct(item[0], item[1]))
        out_specs.append(whole(item[0]) if len(item) == 2 else pl.BlockSpec(item[2], item[3]))
    count = len(arrays)

    pinned = IN_HBM.get(name, ())
    arrays = [
        pltpu.with_memory_space_constraint(a, pltpu.HBM) if i in pinned else a
        for i, a in enumerate(arrays)
    ]
    pinned = OUT_HBM.get(name, ())
    out_shapes = [
        pltpu.HBM(o.shape, o.dtype) if i in pinned else o for i, o in enumerate(out_shapes)
    ]

    def body(sc, *refs):
        kernel(sc, *refs[:count], *refs[count + len(tokens) :])

    spec = pltpu.PrefetchScalarGridSpec(
        num_scalar_prefetch=1,
        grid=grid,
        in_specs=in_specs + [ANYWHERE] * len(tokens),
        out_specs=out_specs,
        scratch_shapes=scratch,
    )
    return pl.pallas_call(
        body,
        grid_spec=spec,
        out_shape=out_shapes,
        compiler_params=params(mib),
        cost_estimate=LONG if name in COMPUTE else SHORT,
        name=name,
    )(scalars, *arrays, *tokens)


def gate(values, tokens):
    count = len(values)
    return pl.pallas_call(
        lambda *refs: None,
        in_specs=[ANYWHERE] * (count + len(tokens)),
        out_specs=[ANYWHERE] * count,
        out_shape=[jax.ShapeDtypeStruct(v.shape, v.dtype) for v in values],
        input_output_aliases={i: i for i in range(count)},
        name="gate",
    )(*values, *tokens)


def norm_stats(values):
    average = jnp.mean(values, -1, keepdims=True)
    centred = values - average
    scale = lax.rsqrt(jnp.mean(centred * centred, -1, keepdims=True) + EPS)
    return centred * scale, scale


def norm_back(unit, scale, gain, grad):
    scaled = grad * gain
    mean_one = jnp.mean(scaled, -1, keepdims=True)
    mean_two = jnp.mean(scaled * unit, -1, keepdims=True)
    return scale * (scaled - mean_one - unit * mean_two)


def project_kernel(sc, rows, gain, bias, wq, wk, wv, normed, qkv):
    part = wq.shape[1]
    unit, _ = norm_stats(rows[...].astype(F32))
    low = (unit * gain[...].astype(F32) + bias[...].astype(F32)).astype(BF16)
    normed[...] = low
    for i, weight in enumerate((wq, wk, wv)):
        qkv[:, i * part : (i + 1) * part] = nn(low, weight[...]).astype(BF16)


def lane_masks():
    lane = lax.broadcasted_iota(jnp.int32, (1, 128), 1)
    return [lane < 64, lane >= 64]


def of_head(values, mask):
    return jnp.where(mask, values, jnp.zeros_like(values))


def by_head(first, second, masks):
    return jnp.where(masks[0], first, second)


BLOCK = 256


def own_kernel(blocks, sc, *refs):
    ins, outs = refs[: 3 * blocks], refs[3 * blocks :]
    q_out, k_out, v_out, t_out, l_out = outs[:5]
    held = outs[5]
    tok = ins[0].shape[1]
    scale = 64 ** (-0.5)
    for mask in range(blocks):
        place = sc[2 + mask]
        for i in range(3):
            values = ins[3 * mask + i][0]
            if i == 0:
                values = (values.astype(F32) * scale).astype(BF16)
            held[i, place] = values
    rows = blocks * tok
    queries = held[0].reshape(rows, 128)
    keys = held[1].reshape(rows, 128)
    values = held[2].reshape(rows, 128)
    q_out[0], k_out[0], v_out[0] = queries, keys, values
    masks = lane_masks()
    size = min(BLOCK, rows)
    lower = lax.broadcasted_iota(jnp.int32, (size, size), 0) >= lax.broadcasted_iota(
        jnp.int32, (size, size), 1
    )
    product = queries.astype(F32) * keys.astype(F32)
    head_keys = [of_head(keys, m) for m in masks]
    head_values = [of_head(values, m) for m in masks]
    selfs = [jnp.sum(of_head(product, m), -1, keepdims=True) for m in masks]
    for i in range(rows // size):
        here = slice(i * size, (i + 1) * size)
        total, sums = jnp.zeros((size, 128), F32), []
        for h in range(2):
            count = jnp.zeros((size, 1), F32)
            for j in range(i + 1):
                there = slice(j * size, (j + 1) * size)
                scores = nt(queries[here], head_keys[h][there]) - selfs[h][here]
                if i == j:
                    scores = jnp.where(lower, scores, FAR)
                weights = jnp.exp(scores)
                count = count + jnp.sum(weights, -1, keepdims=True)
                total = total + nn(weights.astype(BF16), head_values[h][there])
            sums.append(count)
        t_out[0, here] = total
        l_out[0, here] = by_head(sums[0], sums[1], masks)


def load_cached(pieces, mem):
    tok = pieces[0].shape[2]
    for mask, piece in enumerate(pieces):
        mem[:, mask * tok : (mask + 1) * tok] = piece[:, 0]


def cached_kernel(blocks, sc, *refs):
    q_in, k_in, t_in, l_in = refs[:4]
    pieces = refs[4 : 4 + blocks]
    att_out, l_out = refs[4 + blocks : 6 + blocks]
    sends = refs[6 + blocks : 6 + 2 * blocks]
    mem, low = refs[6 + 2 * blocks :]
    load_cached(pieces, mem)
    tok = pieces[0].shape[2]
    queries, keys = q_in[0], k_in[0]
    rows = queries.shape[0]
    masks = lane_masks()
    product = queries.astype(F32) * keys.astype(F32)
    selfs = [jnp.sum(of_head(product, m), -1, keepdims=True) for m in masks]
    head_keys = [of_head(mem[0], m) for m in masks]
    head_values = [of_head(mem[1], m) for m in masks]
    size = min(BLOCK, rows)
    for i in range(rows // size):
        here = slice(i * size, (i + 1) * size)
        total, sums = t_in[0, here], []
        for h in range(2):
            weights = jnp.exp(nt(queries[here], head_keys[h]) - selfs[h][here])
            sums.append(jnp.sum(weights, -1, keepdims=True))
            total = total + nn(weights.astype(BF16), head_values[h])
        count = l_in[0, here] + by_head(sums[0], sums[1], masks)
        attended = total / count
        att_out[0, here] = attended
        l_out[0, here] = count
        low[i * size // tok : (i + 1) * size // tok] = attended.astype(BF16).reshape(
            size // tok, tok, 128
        )
    for mask in range(blocks):
        sends[mask][0] = low[sc[2 + mask]]


def attention_back_kernel(blocks, sc, *refs):
    q_in, k_in, v_in, att_in, l_in = refs[:5]
    pieces = refs[5 : 5 + blocks]
    grads = refs[5 + blocks : 5 + 2 * blocks]
    sends = refs[5 + 2 * blocks : 5 + 3 * blocks]
    mem, came, low = refs[5 + 3 * blocks :]
    load_cached(pieces, mem)
    tok = pieces[0].shape[2]
    for mask in range(blocks):
        came[sc[2 + mask]] = grads[mask][0]
    queries, keys, values = q_in[0], k_in[0], v_in[0]
    rows = queries.shape[0]
    scale = 64 ** (-0.5)
    masks = lane_masks()
    grad = came[...].reshape(rows, 128).astype(F32)
    count = l_in[0]
    scaled_f = grad / count
    scaled = scaled_f.astype(BF16)
    weighed = grad * att_in[0] / count
    product = queries.astype(F32) * keys.astype(F32)
    selfs = [jnp.sum(of_head(product, m), -1, keepdims=True) for m in masks]
    fixes = [jnp.sum(of_head(weighed, m), -1, keepdims=True) for m in masks]
    own_k = [of_head(keys, m) for m in masks]
    own_v = [of_head(values, m) for m in masks]
    mem_k = [of_head(mem[0], m) for m in masks]
    mem_v = [of_head(mem[1], m) for m in masks]
    q_t = [of_head(queries, m).astype(F32).T.astype(BF16) for m in masks]
    s_t = [of_head(scaled, m).astype(F32).T.astype(BF16) for m in masks]
    size = min(BLOCK, rows)
    lower = lax.broadcasted_iota(jnp.int32, (size, size), 0) >= lax.broadcasted_iota(
        jnp.int32, (size, size), 1
    )
    steps = rows // size
    keys_t = [jnp.zeros((128, size), F32) for _ in range(steps)]
    values_t = [jnp.zeros((128, size), F32) for _ in range(steps)]
    diags = []
    for i in range(steps):
        here = slice(i * size, (i + 1) * size)
        total, sums = jnp.zeros((size, 128), F32), []
        for h in range(2):
            diag = jnp.zeros((size, 1), F32)
            for j in range(i + 1):
                there = slice(j * size, (j + 1) * size)
                scores = nt(queries[here], own_k[h][there]) - selfs[h][here]
                if i == j:
                    scores = jnp.where(lower, scores, FAR)
                weights = jnp.exp(scores)
                change = weights * (nt(scaled[here], own_v[h][there]) - fixes[h][here])
                diag = diag + jnp.sum(change, -1, keepdims=True)
                small = change.astype(BF16)
                total = total + nn(small, own_k[h][there])
                keys_t[j] = keys_t[j] + nn(q_t[h][:, here], small)
                values_t[j] = values_t[j] + nn(s_t[h][:, here], weights.astype(BF16))
            weights = jnp.exp(nt(queries[here], mem_k[h]) - selfs[h][here])
            change = weights * (nt(scaled[here], mem_v[h]) - fixes[h][here])
            diag = diag + jnp.sum(change, -1, keepdims=True)
            total = total + nn(change.astype(BF16), mem_k[h])
            sums.append(diag)
        diag = by_head(sums[0], sums[1], masks)
        diags.append(diag)
        grad_q = scale * (total - diag * keys[here].astype(F32))
        low[0, i * size // tok : (i + 1) * size // tok] = grad_q.astype(BF16).reshape(
            size // tok, tok, 128
        )
    for j in range(steps):
        there = slice(j * size, (j + 1) * size)
        grad_k = keys_t[j].T - diags[j] * queries[there].astype(F32)
        blocks_here = slice(j * size // tok, (j + 1) * size // tok)
        low[1, blocks_here] = grad_k.astype(BF16).reshape(size // tok, tok, 128)
        low[2, blocks_here] = values_t[j].T.astype(BF16).reshape(size // tok, tok, 128)
    for mask in range(blocks):
        for i in range(3):
            sends[mask][i, 0] = low[i, sc[2 + mask]]


def feed_kernel(blocks, sc, *refs):
    att_in = refs[:blocks]
    rest = refs[blocks:]
    tokens, cot, w_out, gain, bias, w_in, w_down = rest[:7]
    mixed, grad_res, inner_keep, to_core, normed_out, att_out, branch_keep, sums = rest[7:15]
    acts = rest[15 : 15 + blocks]
    grad_att = rest[15 + blocks : 15 + 2 * blocks]
    residual, normed, total, back = rest[15 + 2 * blocks :]
    step, steps = pl.program_id(0), pl.num_programs(0)
    part, width, tile = att_in[0].shape[1], tokens.shape[1], w_in.shape[1]
    my_block, core = sc[0], sc[1]
    base = blocks * tile

    def out_rows(mask):
        return pl.ds(pl.multiple_of((my_block ^ mask) * part, part), part)

    @pl.when(step == 0)
    def _():
        branch = tokens[...].astype(F32)
        for mask in range(blocks):
            branch = branch + nn(att_in[mask][...], w_out[out_rows(mask), :])
            att_out[:, out_rows(mask)] = att_in[mask][...]
        to_core[:, base + width : base + 2 * width] = att_out[...]
        residual[...] = branch
        unit, _ = norm_stats(branch)
        low = (unit * gain[...].astype(F32) + bias[...].astype(F32)).astype(BF16)
        normed[...] = low
        normed_out[...] = low
        to_core[:, base : base + width] = low

    inner = nn(normed[...], w_in[...])
    square = inner * inner
    bend = jnp.tanh(GELU_A * inner * (1.0 + GELU_B * square))
    half = 0.5 * (1.0 + bend)
    act = (inner * half).astype(BF16)
    slope = half + (0.5 * GELU_A) * inner * (1.0 - bend * bend) * (1.0 + 3.0 * GELU_B * square)
    grad = (slope * nt(cot[...], w_down[...])).astype(BF16)
    into = nn(act, w_down[...])
    away = nt(grad, w_in[...])

    @pl.when(step == 0)
    def _():
        total[...] = into
        back[...] = away

    @pl.when(step > 0)
    def _():
        total[...] += into
        back[...] += away

    for j in range(2 * blocks):

        @pl.when(step == j)
        def _():
            acts[j // 2][:, (j % 2) * tile : (j % 2 + 1) * tile] = act

    columns = pl.ds(pl.multiple_of((my_block ^ (step // 2)) * tile, tile), tile)

    @pl.when(step % 2 == core)
    def _():
        inner_keep[:, columns] = grad

    @pl.when(step % 2 != core)
    def _():
        to_core[:, columns] = grad

    @pl.when(step == steps - 1)
    def _():
        here = residual[...]
        mixed[...] = (here + total[...]).astype(BF16)
        unit, scale = norm_stats(here)
        away = back[...]
        sums[0:1] = jnp.sum(away * unit, 0, keepdims=True)
        sums[1:2] = jnp.sum(away, 0, keepdims=True)
        found = cot[...].astype(F32) + norm_back(unit, scale, gain[...].astype(F32), away)
        grad_res[...] = found
        low = found.astype(BF16)
        left, right = low[:, : width // 2], low[:, width // 2 :]
        branch_keep[...] = jnp.where(core == 0, left, right)
        to_core[:, base + 2 * width :] = jnp.where(core == 0, right, left)
        for mask in range(blocks):
            grad_att[mask][...] = nt(low, w_out[out_rows(mask), :]).astype(BF16)


def in_kernel(blocks, sc, *refs):
    (normed, normed_two, inner, inner_two, att, att_two, branch, branch_two) = refs[:8]
    outs, held = refs[8:12], refs[12]
    part = normed.shape[1]
    tile = inner.shape[1] // blocks
    for q in range(blocks):
        columns = slice(q * tile, (q + 1) * tile)
        found = tn(normed[...], inner[:, columns]) + tn(normed_two[...], inner_two[:, columns])
        held[:part, columns] = found.astype(BF16)
    out = (tn(att[...], branch[...]) + tn(att_two[...], branch_two[...])).astype(BF16)
    width = out.shape[1]
    cuts = held.shape[1] // width
    high = part // cuts
    for i in range(cuts):
        held[part : part + high, i * width : (i + 1) * width] = out[i * high : (i + 1) * high]
    step = pl.program_id(0)
    half = held.shape[0] // 2
    for i, bit in enumerate((1, blocks // 2)):

        @pl.when((step & bit) != 0)
        def _():
            outs[2 * i][0] = held[i * half : (i + 1) * half]

        @pl.when((step & bit) == 0)
        def _():
            outs[2 * i + 1][0] = held[i * half : (i + 1) * half]


def down_kernel(blocks, sc, *refs):
    acts, cots, (sent, kept) = refs[:blocks], refs[blocks : 2 * blocks], refs[2 * blocks :]
    total = tn(acts[0][...], cots[0][...])
    for mask in range(1, blocks):
        total = total + tn(acts[mask][...], cots[mask][...])
    low = total.astype(BF16)

    @pl.when(pl.program_id(0) == 0)
    def _():
        sent[...] = low

    @pl.when(pl.program_id(0) == 1)
    def _():
        kept[...] = low


def qkv_kernel(blocks, halved, sc, *refs):
    normed, grads = refs[:blocks], refs[blocks : 2 * blocks]
    weights = refs[2 * blocks : 2 * blocks + 3]
    gain, bias, sums_two = refs[2 * blocks + 3 : 2 * blocks + 6]
    outs = refs[2 * blocks + 6 :]
    part = grads[0].shape[2]
    share = part // 2 if halved else part
    ahead = jnp.zeros((part, 1), F32)
    plain = jnp.zeros((part, 1), F32)
    for j in range(3):
        total = tn(normed[0][...], grads[0][j])
        count = jnp.sum(grads[0][j].astype(F32), 0, keepdims=True)
        for mask in range(1, blocks):
            total = total + tn(normed[mask][...], grads[mask][j])
            count = count + jnp.sum(grads[mask][j].astype(F32), 0, keepdims=True)
        weight = weights[j][...].astype(F32)
        ahead = ahead + jnp.sum(weight * total, -1, keepdims=True)
        plain = plain + jnp.sum(weight * count, -1, keepdims=True)
        low = total.astype(BF16)
        columns = slice(j * part, (j + 1) * part)
        if halved:
            first, second = low[:share], low[share:]
            outs[0][0, :share, columns] = jnp.where(sc[1] == 0, second, first)
            outs[1][0, :share, columns] = jnp.where(sc[1] == 0, first, second)
        else:
            outs[0][0, :share, columns] = low
    flat = [jnp.broadcast_to(v, (part, 128)).T[0:1] for v in (ahead, plain)]
    shift = (flat[0] - bias[...].astype(F32) * flat[1]) / gain[...].astype(F32)
    row = lax.broadcasted_iota(jnp.int32, (16, part), 0)
    vectors = jnp.zeros((16, part), F32)
    for i, vector in enumerate((shift, flat[1], sums_two[0:1], sums_two[1:2])):
        vectors = jnp.where(row == i, vector, vectors)
    vectors = vectors.astype(BF16)
    for out in outs:
        out[0, share:] = jnp.zeros((16, 3 * part), BF16)
    outs[-1][0, share:, :part] = vectors


def down_finish_kernel(sc, *refs):
    parts, grad_down = refs[:4], refs[4]
    core, low = sc[1], sc[sc.shape[0] - 1]
    for i in range(4):
        wanted = 2 * (core ^ (i // 2)) + (low ^ (i % 2))

        @pl.when(pl.program_id(0) == wanted)
        def _():
            grad_down[...] = parts[i][...].astype(F32)


def in_finish_kernel(blocks, sc, *refs):
    parts, (grad_in, grad_out, held) = refs[:4], refs[4:]
    step = pl.program_id(0)
    core, low = sc[1], sc[sc.shape[0] - 1]
    half, columns = parts[0].shape
    part, tile = grad_in.shape
    width = grad_out.shape[1]
    cuts = columns // width
    high = part // cuts

    @pl.when(step == 0)
    def _():
        for i in range(4):
            rows = pl.ds(pl.multiple_of((low ^ (i % 2)) * half, 16), half)
            held[i // 2, rows] = parts[i][...]

    which = jnp.where(step % 2 == core, 0, 1)
    at = pl.ds(pl.multiple_of((step // 2) * tile, tile), tile)
    grad_in[...] = held[which, :part, at].astype(F32)

    @pl.when(step < 2)
    def _():
        for i in range(cuts):
            grad_out[i * high : (i + 1) * high] = held[
                which, part : part + high, i * width : (i + 1) * width
            ].astype(F32)


def qkv_finish_kernel(blocks, halved, sc, *refs):
    parts, (grad_qkv, sums, held) = refs[:4], refs[4:]
    half, _, part = parts[0].shape
    share = grad_qkv.shape[0]
    core, low = sc[1], sc[sc.shape[0] - 1]
    mine = (pl.program_id(0) == core) if halved else True
    for i in range(4):
        for j in range(half):
            held[i // 2, (low ^ (i % 2)) * half + j] = parts[i][j].astype(F32)
    for mask in range(blocks):
        columns = pl.ds(pl.multiple_of((sc[0] ^ mask) * part, part), part)
        grad_qkv[:, columns] = jnp.where(mine, held[0, mask, :share], held[1, mask, :share])

    @pl.when((pl.program_id(0) == 0) & (pl.program_id(1) == 0))
    def _():
        total = jnp.zeros((8, part), F32)
        for i in range(2 if halved else 1):
            for mask in range(blocks):
                total = total + held[i, mask, share : share + 8]
        sums[...] = total


def tokens_kernel(blocks, sc, tokens, grad_res, gain, *refs):
    pieces = refs[:blocks]
    weights = refs[blocks : blocks + 3]
    grad_tokens, total = refs[blocks + 3 :]
    step, steps = pl.program_id(0), pl.num_programs(0)
    for mask in range(blocks):

        @pl.when(step == mask)
        def _():
            found = nt(pieces[mask][0], weights[0][...])
            found = found + nt(pieces[mask][1], weights[1][...])
            found = found + nt(pieces[mask][2], weights[2][...])
            if mask == 0:
                total[...] = found
            else:
                total[...] += found

    @pl.when(step == steps - 1)
    def _():
        unit, scale = norm_stats(tokens[...].astype(F32))
        grad_tokens[...] = grad_res[...] + norm_back(
            unit, scale, gain[...].astype(F32), total[...]
        )


def index_kernel(blocks, place, continues, scalars, banks):
    my_block, my_group = lax.axis_index("blk"), lax.axis_index("grp")
    chip, core = my_group // 2, my_group % 2
    scalars[0], scalars[1] = my_block, core
    for mask in range(blocks):
        scalars[2 + mask] = place[my_block ^ mask]
    scalars[2 + blocks] = chip % 2
    banks[0], banks[1] = chip, core
    for i in range(continues.shape[0]):
        banks[2 + i] = continues[i]


def indices(place, continues):
    smem = pl.BlockSpec(memory_space=pltpu.SMEM)
    blocks, banks = place.shape[0], continues.shape[0]
    return pl.pallas_call(
        functools.partial(index_kernel, blocks),
        in_specs=[smem, smem],
        out_specs=[smem, smem],
        out_shape=[
            jax.ShapeDtypeStruct((3 + blocks,), jnp.int32),
            jax.ShapeDtypeStruct((2 + banks,), jnp.int32),
        ],
        name="indices",
    )(place, continues)


def cross_kernel(sc, one, two, top, low):
    half = one.shape[1] // 2
    top[...], low[...] = one[:, :half], two[:, half:]


def join_kernel(sc, top, low, out):
    half = top.shape[1]
    out[:, :half], out[:, half:] = top[...], low[...]


def sum_kernel(sc, *refs):
    total = refs[0][...].astype(F32)
    for ref in refs[1:-1]:
        total = total + ref[...].astype(F32)
    refs[-1][...] = total.astype(BF16)


def stack_kernel(sc, *refs):
    for i, ref in enumerate(refs[:-1]):
        refs[-1][i] = ref[...]


def sums_kernel(count, sc, *refs):
    outs = refs[len(refs) - len(refs) // (count + 1) :]
    for i, out in enumerate(outs):
        total = refs[i * count][...].astype(F32)
        for ref in refs[i * count + 1 : (i + 1) * count]:
            total = total + ref[...].astype(F32)
        out[...] = total.astype(BF16)


def exchange_sum_kernel(sc, kept, came, away, held):
    for i in range(held.shape[0]):
        held[i] = (kept[2 * i].astype(F32) + came[2 * i].astype(F32)).astype(BF16)
        away[i] = (kept[2 * i + 1].astype(F32) + came[2 * i + 1].astype(F32)).astype(BF16)


def place_halves(sc, first, second, mine, other):
    low = sc[sc.shape[0] - 1] == 1
    mine[...] = jnp.where(low, second, first)
    other[...] = jnp.where(low, first, second)


def split_sum_kernel(count, sc, *refs):
    totals = []
    for i in range(2):
        total = refs[i * count][...].astype(F32)
        for ref in refs[i * count + 1 : (i + 1) * count]:
            total = total + ref[...].astype(F32)
        totals.append(total.astype(BF16))
    place_halves(sc, *totals, *refs[2 * count :])


def split_stack_kernel(sc, *refs):
    pieces, (mine, other) = refs[:-2], refs[-2:]
    half = len(pieces) // 2
    low = sc[sc.shape[0] - 1] == 1
    for i in range(half):
        first, second = pieces[i][...], pieces[half + i][...]
        mine[i] = jnp.where(low, second, first)
        other[i] = jnp.where(low, first, second)


def cut(chips, tok, width, piece):
    high = max(16, tok // chips)
    across = high * chips // tok
    wide = width // across
    return (
        pl.ds(pl.multiple_of((piece // across) * high, high), high),
        pl.ds(pl.multiple_of((piece % across) * wide, wide), wide),
    )


def piece_shape(chips, tok, width):
    high = max(16, tok // chips)
    return high, tok * width // (chips * high)


def split_kernel(chips, sc, keys, values, came, *outs):
    _, tok, width = keys.shape
    for mask in range(chips):
        rows, columns = cut(chips, tok, width, sc[0] ^ mask)
        own = jnp.where(sc[1] == 0, keys[:, rows, columns], values[:, rows, columns])
        outs[mask][0] = own
        outs[mask][1] = came[:, rows, columns]


def route_kernel(chips, sc, *refs):
    ins, outs, held = refs[:chips], refs[chips : 2 * chips], refs[2 * chips]
    count = ins[0].shape[1]
    per_chip = 2 * count
    for mask in range(chips):
        held[mask] = ins[mask][...]
    for mask in range(chips):
        for i in range(per_chip):
            bank = sc[2 + (sc[0] ^ mask) * per_chip + i]
            outs[mask][i] = held[
                (bank // per_chip) ^ sc[0], ((bank // count) % 2) ^ sc[1], bank % count
            ]


def gather_kernel(chips, sc, *refs):
    ins, (kept, sent) = refs[:chips], refs[chips:]
    count, tok, width = kept.shape
    high, wide = ins[0].shape[1:]
    across = width // wide
    for mask in range(chips):
        _, columns = cut(chips, tok, width, sc[0] ^ mask)
        rows = slice((mask // across) * high, (mask // across + 1) * high)
        for i in range(count):
            kept[i, rows, columns] = ins[mask][sc[1] * count + i]
            sent[i, rows, columns] = ins[mask][(1 - sc[1]) * count + i]


def columns_kernel(blocks, sc, kept, came, *outs):
    part = kept.shape[2] // blocks
    for mask in range(blocks):
        columns = pl.ds(pl.multiple_of((sc[0] ^ mask) * part, part), part)
        mine, other = kept[:, :, columns], came[:, :, columns]
        outs[mask][0] = jnp.where(sc[1] == 0, mine, other)
        outs[mask][1] = jnp.where(sc[1] == 0, other, mine)


def fetch_banks(mem_keys, mem_values, places, groups, my_group, blocks, scalars, meanwhile):
    count, tok, width = mem_keys.shape
    core, chips = my_group % 2, groups // 2
    came = swap(jnp.where(core == 0, mem_values, mem_keys), "grp", 1)
    piece = piece_shape(chips, tok, width)

    def line(parts):
        return [parts[0]] + [swap(parts[m], "grp", 2 * m) for m in range(1, chips)]

    parts = call(
        functools.partial(split_kernel, chips),
        "split_banks",
        (1,),
        [mem_keys, mem_values, came],
        [((2, count) + piece, BF16)] * chips,
        [],
        places,
        10,
    )
    meanwhile(0, parts)
    parts = call(
        functools.partial(route_kernel, chips),
        "route_banks",
        (1,),
        line(parts),
        [((2 * count,) + piece, BF16)] * chips,
        [pltpu.VMEM((chips, 2, count) + piece, BF16)],
        places,
        10,
        meanwhile(1, parts),
    )
    meanwhile(2, parts)
    kept, sent = call(
        functools.partial(gather_kernel, chips),
        "gather_banks",
        (1,),
        line(parts),
        [((count, tok, width), BF16)] * 2,
        [],
        places,
        10,
        meanwhile(3, parts),
    )
    parts = call(
        functools.partial(columns_kernel, blocks),
        "bank_columns",
        (1,),
        [kept, swap(sent, "grp", 1)],
        [((2, count, tok, width // blocks), BF16)] * blocks,
        [],
        scalars,
        10,
    )
    return [parts[0]] + [swap(parts[m], "blk", m) for m in range(1, blocks)]


class Order:
    def __init__(self, scalars, last=()):
        self.scalars, self.last = scalars, last

    def call(self, kernel, name, grid, ins, outs, scratch, mib):
        found = call(
            kernel, name, grid, ins, outs, scratch, self.scalars, mib, tuple(self.last)
        )
        self.last = (found[0],)
        return found

    def small(self, kernel, name, items, outs):
        ins = []
        for item in items:
            if isinstance(item, tuple) and len(item) == 2:
                array, at = item
                block = (None,) + array.shape[1:]
                zeros = (0,) * (array.ndim - 1)
                ins.append((array, block, lambda i, sc, at=at, zeros=zeros: (at,) + zeros))
            else:
                ins.append(item)
        return self.call(kernel, name, (1,), ins, [(o, BF16) for o in outs], [], 8)

    def gate(self, values):
        found = gate(values, self.last)
        self.last = (found[0],)
        return found


def on_device(
    tokens,
    gain_one,
    bias_one,
    w_qkv,
    w_out,
    gain_two,
    bias_two,
    w_in,
    w_down,
    mem_keys,
    mem_values,
    continues,
    block_place,
    cotangent,
):
    seq_count, tok, width = tokens.shape
    hidden_width = w_in.shape[1]
    blocks, groups = lax.axis_size("blk"), lax.axis_size("grp")
    my_block, my_group = lax.axis_index("blk"), lax.axis_index("grp")
    core = my_group % 2
    part = width // blocks
    pairs = part // 128
    halved = pairs > 1
    rows = seq_count * tok
    seg_rows = blocks * tok
    tile = hidden_width // (2 * blocks)
    scalars, banks = indices(block_place, continues)
    gain_one, bias_one = gain_one.reshape(1, width), bias_one.reshape(1, width)
    gain_two, bias_two = gain_two.reshape(1, width), bias_two.reshape(1, width)
    flat = tokens.reshape(rows, width)
    cot = cotangent.reshape(rows, width)

    def gather_rows(values, order):
        if blocks != 4:
            return [values] + [swap(values, "blk", mask) for mask in range(1, blocks)]
        one, two = swap(values, "blk", 1), swap(values, "blk", 2)
        half = (2, rows // 2, width)
        top, low = order.call(
            cross_kernel, "cross", (1,), [one, two], [(half, BF16)] * 2, [], 8
        )
        top, low = swap(top, "blk", 2), swap(low, "blk", 1)
        return [values, one, two, (top, low)]

    def head_weights(j, at=None):
        def index(i, sc):
            return (0, j * blocks + (sc[0] ^ i if at is None else sc[0]))

        return (w_qkv, (width, part), index)

    def heads_block(j):
        return (1, tok, 128), lambda s, p, sc: (s, 0, j * pairs + p)

    seg_block = (1, seg_rows, 128), lambda s, p, sc: (s, 0, p)
    seg_shape = (seq_count, seg_rows, part)
    tok_block = (1, tok, 128), lambda s, p, sc: (s, 0, p)
    mem_block = (2, 1, tok, 128), lambda s, p, sc: (0, s, 0, p)
    early = {}

    rows_block = (None, rows, width)

    def meanwhile(stage, parts):
        if stage == 0:
            both = call(
                stack_kernel,
                "stack",
                (1,),
                [flat, cot],
                [((2, rows, width), BF16)],
                [],
                scalars,
                8,
                (parts[0],),
            )
            early["both"] = both[0]
            return ()
        if stage == 1:
            return (early["both"],)
        if stage == 3:
            return (early["own"][0],)
        order = Order(scalars, (parts[0],))
        pieces = early["pieces"] = gather_rows(early["both"], order)
        normed, qkv = [], []
        for mask, piece in enumerate(pieces):
            if isinstance(piece, tuple):
                (piece,) = order.call(
                    join_kernel, "join", (1,), piece, [(early["both"].shape, BF16)], [], 8
                )
                pieces[mask] = piece
            found = order.call(
                project_kernel,
                "project",
                (1,),
                [(piece, rows_block, lambda i, sc: (0, 0, 0)), gain_one, bias_one]
                + [head_weights(j, 0) for j in range(3)],
                [((rows, width), BF16), ((rows, 3 * part), BF16)],
                [],
                12,
            )
            normed.append(found[0])
            qkv.append(found[1].reshape(seq_count, tok, 3 * part))
        early["normed"] = normed
        early["own"] = order.call(
            functools.partial(own_kernel, blocks),
            "own_keys",
            (seq_count, pairs),
            [(qkv[m],) + heads_block(j) for m in range(blocks) for j in range(3)],
            [(seg_shape, BF16) + seg_block] * 3 + [(seg_shape, F32) + seg_block] * 2,
            [pltpu.VMEM((3, blocks, tok, 128), BF16)],
            16,
        )
        return ()

    mem = fetch_banks(
        mem_keys, mem_values, banks, groups, my_group, blocks, scalars, meanwhile
    )
    queries, keys, values, partial, counts = early["own"]
    normed = early["normed"]
    found = call(
        functools.partial(cached_kernel, blocks),
        "cached_keys",
        (seq_count, pairs),
        [(a,) + seg_block for a in (queries, keys, partial, counts)]
        + [(a,) + mem_block for a in mem],
        [(seg_shape, F32) + seg_block] * 2
        + [((seq_count, tok, part), BF16) + tok_block] * blocks,
        [pltpu.VMEM((2, seg_rows, 128), BF16), pltpu.VMEM((blocks, tok, 128), BF16)],
        scalars,
        16,
    )
    attended_f, counts = found[:2]
    attended = [found[2]] + [swap(found[2 + m], "blk", m) for m in range(1, blocks)]
    attended = [a.reshape(rows, part) for a in attended]

    def ff_tile(j, sc):
        return 2 * (sc[0] ^ (j // 2)) + j % 2

    base = blocks * tile
    found = call(
        functools.partial(feed_kernel, blocks),
        "feed",
        (2 * blocks,),
        attended
        + [flat, cot, w_out, gain_two, bias_two]
        + [
            (w_in, (width, tile), lambda j, sc: (0, ff_tile(j, sc))),
            (w_down, (tile, width), lambda j, sc: (ff_tile(j, sc), 0)),
        ],
        [
            ((rows, width), BF16),
            ((rows, width), F32),
            ((rows, base), BF16),
            ((rows, base + 2 * width + width // 2), BF16),
            ((rows, width), BF16),
            ((rows, width), BF16),
            ((rows, width // 2), BF16),
            ((2, width), F32),
        ]
        + [((rows, 2 * tile), BF16)] * blocks
        + [((rows, part), BF16)] * blocks,
        [
            pltpu.VMEM((rows, width), F32),
            pltpu.VMEM((rows, width), BF16),
            pltpu.VMEM((rows, width), F32),
            pltpu.VMEM((rows, width), F32),
        ],
        scalars,
        28,
    )
    mixed, grad_res, inner_keep, to_core, normed_two, att_all, branch, sums_two = found[:8]
    acts, grad_att = found[8 : 8 + blocks], found[8 + blocks :]
    grad_att = [grad_att[0]] + [swap(grad_att[m], "blk", m) for m in range(1, blocks)]
    grad_att = [g.reshape(seq_count, tok, part) for g in grad_att]
    core_came = swap(to_core, "grp", 1)
    order = Order(scalars, tuple(grad_att[1:]) + (core_came,))
    acts = [acts[0]] + [swap(a, "blk", m + 1) for m, a in enumerate(order.gate(acts[1:]))]

    top = blocks // 2

    def of_mask(shape, mask, wanted):
        def index(m, sc):
            if mask == 1:
                return (m >> 1, 0, 0)
            return (jnp.maximum(m - top, 0) if wanted else jnp.minimum(m, top - 1), 0, 0)

        return ((top,) + shape, BF16, (1,) + shape, index)

    def columns(start):
        return lambda m, sc: (0, start // part + (sc[0] ^ m))

    in_rows = part + part * width // (2 * base)
    in_shape = (in_rows // 2, base)
    bits = [1 << i for i in range(blocks.bit_length() - 1)]
    results = {}
    paths = {}

    def go(names):
        for name in names:
            if name not in results:
                try:
                    next(paths[name])
                except StopIteration as stop:
                    results[name] = stop.value

    def total(*items):
        first = items[0]
        if not isinstance(first, tuple):
            shape = first.shape
        elif len(first) == 2:
            shape = first[0].shape[1:]
        else:
            shape = first[1]
        return order.small(sum_kernel, "sum", items, [shape])[0]

    def sum_chips(mine, other):
        held = total(mine, swap(other, "grp", 2))
        for bit in range(2, groups.bit_length() - 1):
            came = swap(held, "grp", 1 << bit)
            yield
            held = total(held, came)
        other = swap(held, "grp", 2)
        core_held = swap(held, "grp", 1)
        yield
        return held, other, core_held, swap(other, "grp", 1)

    found = order.call(
        functools.partial(attention_back_kernel, blocks),
        "attention_back",
        (seq_count, pairs),
        [(a,) + seg_block for a in (queries, keys, values, attended_f, counts)]
        + [(a,) + mem_block for a in mem]
        + [(a,) + tok_block for a in grad_att],
        [
            (
                (3, seq_count, tok, part),
                BF16,
                (3, 1, tok, 128),
                lambda s, p, sc: (0, s, 0, p),
            )
        ]
        * blocks,
        [
            pltpu.VMEM((2, seg_rows, 128), BF16),
            pltpu.VMEM((blocks, tok, 128), BF16),
            pltpu.VMEM((3, blocks, tok, 128), BF16),
        ],
        24,
    )
    own_grads = [g.reshape(3, rows, part) for g in found]

    found = order.call(
        functools.partial(in_kernel, blocks),
        "grad_in",
        (blocks,),
        [
            (normed_two, (rows, part), columns(0)),
            (core_came, (rows, part), columns(base)),
            inner_keep,
            (core_came, (rows, base), lambda m, sc: (0, 0)),
            (att_all, (rows, part), columns(0)),
            (core_came, (rows, part), columns(base + width)),
            branch,
            (core_came, (rows, width // 2), lambda m, sc: (0, 2 * (base + 2 * width) // width)),
        ],
        [of_mask(in_shape, mask, sent) for mask in (1, top) for sent in (True, False)],
        [pltpu.VMEM((in_rows, base), BF16)],
        28,
    )
    in_sent, in_kept = (found[0], found[2]), (found[1], found[3])

    def in_path():
        firsts, rests = (1, top), (bits[1:], bits[:-1][::-1])
        masks = [[m for m in range(blocks) if not m & bit] for bit in firsts]
        came = [swap(sent, "blk", bit) for sent, bit in zip(in_sent, firsts)]
        yield
        terms = [
            {m: [(in_kept[h], i), (came[h], i)] for i, m in enumerate(masks[h])} for h in range(2)
        ]
        for bit in range(len(bits) - 1):
            away = [[m for m in masks[h] if m & rests[h][bit]] for h in range(2)]
            masks = [[m for m in masks[h] if not m & rests[h][bit]] for h in range(2)]
            items = [v for h in range(2) for m in away[h] for v in terms[h][m]]
            count = len(away[0])
            sent = order.small(
                functools.partial(sums_kernel, len(items) // (2 * count)),
                "sums",
                items,
                [in_shape] * (2 * count),
            )
            for h in range(2):
                for i, m in enumerate(masks[h]):
                    came = swap(sent[h * count + i], "blk", rests[h][bit])
                    terms[h][m] = terms[h][m] + [came]
            yield
        items = [v for h in range(2) for v in terms[h][0]]
        mine, other = order.small(
            functools.partial(split_sum_kernel, len(items) // 2), "split", items, [in_shape] * 2
        )
        yield
        return (yield from sum_chips(mine, other))

    paths["i"] = in_path()
    go("i")

    found = order.call(
        functools.partial(down_kernel, blocks),
        "grad_down",
        (2,),
        [
            (a, (rows, tile), lambda i, sc: (0, jnp.where(i == 0, 1 - sc[1], sc[1])))
            for a in acts
        ]
        + [(p, rows_block, lambda i, sc: (1, 0, 0)) for p in early["pieces"]],
        [((tile, width), BF16)] * 2,
        [],
        28,
    )
    down_kept, down_came = found[1], swap(found[0], "grp", 1)

    def down_path():
        block = (tile // 2, width)
        items = [
            (v, block, lambda i, sc, h=h: (h, 0)) for h in range(2) for v in (down_kept, down_came)
        ]
        mine, other = order.small(
            functools.partial(split_sum_kernel, 2), "split", items, [block] * 2
        )
        yield
        return (yield from sum_chips(mine, other))

    paths["d"] = down_path()

    share = part // 2 if halved else part
    share_block = (1, share + 16, 3 * part), lambda m, sc: (m, 0, 0)

    def own_weights(j):
        return (w_qkv, (part, part), lambda m, sc: (sc[0] ^ m, j * blocks + sc[0]))

    found = order.call(
        functools.partial(qkv_kernel, blocks, halved),
        "grad_qkv",
        (blocks,),
        [(n, (rows, part), columns(0)) for n in normed]
        + own_grads
        + [own_weights(j) for j in range(3)]
        + [(gain_one, (1, part), columns(0)), (bias_one, (1, part), columns(0))]
        + [(sums_two, (2, part), columns(0))],
        [((blocks, share + 16, 3 * part), BF16) + share_block] * (2 if halved else 1),
        [],
        28,
    )
    qkv_sent, qkv_kept = found[0], found[-1]

    def qkv_path():
        came = swap(qkv_sent, "grp", 1)
        yield
        shape = qkv_kept.shape[1:]
        half = (blocks // 2,) + shape
        away, kept = order.small(
            exchange_sum_kernel, "sums", [qkv_kept, came], [half] * 2
        )
        came = swap(away, "blk", 1)
        yield
        held = {2 * i: [(kept, i), (came, i)] for i in range(blocks // 2)}
        for bit in bits[1:]:
            masks = [m for m in sorted(held) if m & bit]
            items = [v for m in masks for v in held[m]]
            (away,) = order.small(stack_kernel, "stack", items, [(len(items),) + shape])
            came = swap(away, "blk", bit)
            yield
            held = {m: v for m, v in held.items() if not m & bit}
            count = len(held[0])
            for i, m in enumerate(sorted(held)):
                held[m] = held[m] + [(came, i * count + k) for k in range(count)]
        mine, other = order.small(split_stack_kernel, "split", held[0], [half] * 2)
        yield
        return (yield from sum_chips(mine, other))

    paths["q"] = qkv_path()
    go("q")
    def tokens_path():
        held = order.gate(own_grads[1:])
        grads = [own_grads[0]] + [swap(held[m], "blk", m + 1) for m in range(blocks - 1)]
        yield
        return order.call(
            functools.partial(tokens_kernel, blocks),
            "tokens_back",
            (blocks,),
            [flat, grad_res, gain_one] + grads + [head_weights(j) for j in range(3)],
            [((rows, width), F32)],
            [pltpu.VMEM((rows, width), F32)],
            24,
        )

    def down_finish():
        return order.call(
            down_finish_kernel,
            "down_finish",
            (4,),
            list(results["d"]),
            [((2 * tile, width), F32, (tile // 2, width), lambda i, sc: (i, 0))],
            [],
            16,
        )
        yield

    def in_finish():
        return order.call(
            functools.partial(in_finish_kernel, blocks),
            "in_finish",
            (2 * blocks,),
            list(results["i"]),
            [
                ((part, hidden_width), F32, (part, tile), lambda j, sc: (0, j)),
                ((part, width), F32, (part, width // 2), lambda j, sc: (0, jnp.minimum(j, 1))),
            ],
            [pltpu.VMEM((2, in_rows, base), BF16)],
            16,
        )
        yield

    def qkv_finish():
        high = share + 16
        return order.call(
            functools.partial(qkv_finish_kernel, blocks, halved),
            "qkv_finish",
            (2 if halved else 1, 3),
            [(a, (blocks // 2, high, part), lambda k, i, sc: (0, 0, i)) for a in results["q"]],
            [
                ((part, 3 * width), F32, (share, width), lambda k, i, sc: (k, i)),
                ((8, part), F32),
            ],
            [pltpu.VMEM((2, blocks, high, part), F32)],
            16,
        )
        yield

    paths["t"] = tokens_path()
    paths["F"], paths["G"], paths["H"] = down_finish(), qkv_finish(), in_finish()
    if groups == 8 and blocks == 4:
        go("diqdiqdiqtqdFitiqHqG")
    while len(results) < len(paths):
        for name in sorted(paths):
            if name.islower() or "d" in results and "i" in results and "q" in results:
                go(name)
    (grad_down,) = results["F"]
    grad_qkv, sums = results["G"]
    grad_in, grad_out = results["H"]
    (grad_tokens,) = results["t"]
    return (
        mixed.reshape(tokens.shape),
        grad_tokens.reshape(tokens.shape),
        sums[0],
        sums[1],
        grad_qkv,
        grad_out,
        sums[2],
        sums[3],
        grad_in,
        grad_down,
    )


def solution(mesh):
    rows = P("grp", "blk", None)
    in_specs = (rows,) + (P(),) * 8 + (rows, rows, P(), P(), rows)
    out_specs = (rows, rows) + (P("blk"),) * 2 + (P("blk", None),) * 2
    out_specs = out_specs + (P("blk"),) * 2 + (P("blk", None),) * 2
    return jax.shard_map(
        on_device, mesh=mesh, in_specs=in_specs, out_specs=out_specs, check_vma=False
    )
```

time: 432 us -> 336 us (0.78); the launches traced: 426 us -> 335 us
  waiting for transfers between devices: 200 us -> 148 us
  Pallas kernels: 74.1 us -> 112 us
  other arithmetic: 36.8 us -> 1.11 us
  local copies, waits for them, and re-layouts: 50.4 us -> 20.4 us
  starting transfers between devices: 60.8 us -> 52.1 us
    ppermute x55 -> x51, waiting for transfers between devices: 200 us -> 148 us  [swap(): return lax.ppermute(values, axis, [(i, i ^ mask) for i in range(size)])]
    pallas_call x10 -> x37, Pallas kernels: 74.1 us -> 112 us  [the longest x34 110 us: call(): pl.pallas_call(body, grid_spec=spec, out_shape=out_shapes, compiler_param...]
    convert_element_type x15 -> x0, other arithmetic: 19.1 us -> none  [the longest x11 11.5 us: add(): return total.astype(BF16)]
    convert_element_type x4 -> x0, local copies, waits for them, and re-layouts: 17.1 us -> none  [the longest x2 11.9 us: on_device(): jnp.transpose(both, (1, 2, 0, 3)).reshape(part, hidden_width).astype(F32)]
    select_n x14 -> x1, other arithmetic: 12.5 us -> 1.11 us  [fetch_banks(): came = swap(jnp.where(core == 0, mem_values, mem_keys), 'grp', 1)]
    ppermute x55 -> x51, starting transfers between devices: 60.8 us -> 52.1 us  [swap(): return lax.ppermute(values, axis, [(i, i ^ mask) for i in range(size)])]
    another operation x7 -> x0, other arithmetic: 4.94 us -> none  [the longest x2 2.2 us: fetch_banks(): both = jnp.stack([keys, values])]
    another operation x3 -> x0, local copies, waits for them, and re-layouts: 4.61 us -> none  [the longest x1 2.67 us: on_device(): scalars = jnp.stack([my_block, core] + places).astype(jnp.int32)]
  transfers between devices with their start and end apart: 55 -> 51, of which waited for: 25 -> 23; matrix products, arithmetic and copies ran while one was open for 13% -> 0% of each run, Pallas kernels for 11% -> 23%
where the time goes in v3:
time: 336 us; the launch traced here: 335 us
  waiting for transfers between devices  148 us (44%)
  Pallas kernels  112 us (33%)
  starting transfers between devices  52.1 us (16%)
  local copies, waits for them, and re-layouts  20.4 us (6%)
    ppermute x51, waiting for transfers between devices, swap(): return lax.ppermute(values, axis, [(i, i ^ mask) for i in range(size)])  148 us
    pallas_call x34, Pallas kernels, call(): pl.pallas_call(body, grid_spec=spec, out_shape=out_shapes, compiler_param...  110 us
    ppermute x51, starting transfers between devices, swap(): return lax.ppermute(values, axis, [(i, i ^ mask) for i in range(size)])  52.1 us
    unnamed x144, local copies, waits for them, and re-layouts  19.8 us
  transfers between devices with their start and end apart: 51, of which 23 were waited for; matrix products, arithmetic and copies ran while one was open for 0% of the time, Pallas kernels for 23%

profile of v3, /device:TPU:0, one launch (start us, length us, event | category | flops | bytes accessed | tf_op | source)
XLA Modules:
  0.0 335.1 jit_solution(12162862260161448773)
XLA Ops:
  16.8 5.0 %collective-permute-done.3.refs_1_ = bf16[2,2,32,1024]{3,2,1,0:T(8,128)(2,1)S(1)} collective-permute-done((bf16[2,2,32,1024]{3,2,1,0:T(8,128)(2,1)S(1)}, bf16[2,2,32,1024]{3,2,1,0:T(8,128)(2,1)S(1)}, u32[]{:S(2)}, u32[]{:S(2)}) %collective-permute-start.3) | collective-permute-done | bytes 262176 | tf_op jit(solution)/shard_map/ppermute | solution.py:22
  21.8 9.7 %collective-permute-done.4.refs_2_ = bf16[2,2,32,1024]{3,2,1,0:T(8,128)(2,1)S(1)} collective-permute-done((bf16[2,2,32,1024]{3,2,1,0:T(8,128)(2,1)S(1)}, bf16[2,2,32,1024]{3,2,1,0:T(8,128)(2,1)S(1)}, u32[]{:S(2)}, u32[]{:S(2)}) %collective-permute-start.4) | collective-permute-done | bytes 262176 | tf_op jit(solution)/shard_map/ppermute | solution.py:22
  33.1 5.1 %collective-permute-start.8 = (bf16[4,32,1024]{2,1,0:T(8,128)(2,1)}, bf16[4,32,1024]{2,1,0:T(8,128)(2,1)}, u32[]{:S(2)}, u32[]{:S(2)}) collective-permute-start(bf16[4,32,1024]{2,1,0:T(8,128)(2,1)} %get-tuple-element.116), channel_id=1, source_target_pairs={{0,2},{1,3},{2,0},{3,1},{4,6},{5,7},{6,4},{7,5},{8,10},{9,11},{10,... | collective-permute-start | bytes 786440 | tf_op jit(solution)/shard_map/ppermute | solution.py:22
  62.1 5.9 %own_keys.1 = (bf16[2,512,256]{2,1,0:T(8,128)(2,1)}, bf16[2,512,256]{2,1,0:T(8,128)(2,1)}, bf16[2,512,256]{2,1,0:T(8,128)(2,1)}, f32[2,512,256]{2,1,0:T(8,128)}, f32[2,512,256]{2,1,0:T(8,128)}) custom-call(s32[7]{0:T(128)S(1)} %copy-done.37, bf16[2,128,768]{2,1,0:T(8,128)(2,1)S(1)} %bitcast.49, bf16[2,128,768]{2,1,0:T(8,128)(2,1)S(1)} %bitcast.50, ...), custom_call_target="tpu_custom_call" | custom-call | flops 99999997952 | bytes 1000000 | tf_op jit(solution)/shard_map/own_keys/pallas_call | solution.py:107
  77.1 5.7 %collective-permute-done.12.refs_5_.refs_6_ = bf16[2,2,128,256]{3,2,1,0:T(8,128)(2,1)S(1)} collective-permute-done((bf16[2,2,128,256]{3,2,1,0:T(8,128)(2,1)S(1)}, bf16[2,2,128,256]{3,2,1,0:T(8,128)(2,1)S(1)}, u32[]{:S(2)}, u32[]{:S(2)}) %collective-permute-start.12) | collective-permute-done | bytes 262176 | tf_op jit(solution)/shard_map/ppermute | solution.py:22
  82.8 4.1 %collective-permute-done.13.refs_6_.refs_7_ = bf16[2,2,128,256]{3,2,1,0:T(8,128)(2,1)S(1)} collective-permute-done((bf16[2,2,128,256]{3,2,1,0:T(8,128)(2,1)S(1)}, bf16[2,2,128,256]{3,2,1,0:T(8,128)(2,1)S(1)}, u32[]{:S(2)}, u32[]{:S(2)}) %collective-permute-start.13) | collective-permute-done | bytes 262176 | tf_op jit(solution)/shard_map/ppermute | solution.py:22
  88.6 8.3 %cached_keys.1 = (f32[2,512,256]{2,1,0:T(8,128)}, f32[2,512,256]{2,1,0:T(8,128)}, bf16[2,128,256]{2,1,0:T(8,128)(2,1)S(1)}, bf16[2,128,256]{2,1,0:T(8,128)(2,1)S...) custom-call(s32[7]{0:T(128)S(1)} %copy-done.37, ...), custom_call_target="tpu_custom_call" | custom-call | flops 99999997952 | bytes 1000000 | tf_op jit(solution)/shard_map/cached_keys/pallas_call | solution.py:107
  105.6 20.1 %feed.1 = (bf16[256,1024]{1,0:T(8,128)(2,1)}, f32[256,1024]{1,0:T(8,128)}, bf16[256,2048]{1,0:T(8,128)(2,1)}, bf16[256,4608]{1,0:T(8,128)(2,1)S(1)}, bf16[256,10...) custom-call(s32[7]{0:T(128)S(1)} %copy-done.37, ...), custom_call_target="tpu_custom_call" | custom-call | flops 99999997952 | bytes 1000000 | tf_op jit(solution)/shard_map/feed/pallas_call | solution.py:107
  129.3 3.0 collective-permute-done.18
  141.1 13.8 %attention_back.1 = (bf16[3,2,128,256]{3,2,1,0:T(8,128)(2,1)S(1)}, bf16[3,2,128,256]{3,2,1,0:T(8,128)(2,1)S(1)}, bf16[3,2,128,256]{3,2,1,0:T(8,128)(2,1)S(1)}, bf16[3,2,128,256]{3,2,1,0:T(8,128)(2,1)S(1)}) custom-call(s32[7]{0:T(128)S(1)} %copy-done.37, bf16[2,512,256]{2,1,0:T(8,128)(2,1)} %get-tuple-element.112.refs_4_.refs_0_, ...), custom_call_target="tpu_custom_call" | custom-call | flops 99999997952 | bytes 1000000 | tf_op jit(solution)/shard_map/attention_back/pallas_call | solution.py:107
  155.1 6.1 %grad_in.1 = (bf16[2,160,2048]{2,1,0:T(8,128)(2,1)}, bf16[2,160,2048]{2,1,0:T(8,128)(2,1)S(1)}, bf16[2,160,2048]{2,1,0:T(8,128)(2,1)}, bf16[2,160,2048]{2,1,0:T(8,128)(2,1)S(1)}) custom-call(s32[7]{0:T(128)S(1)} %copy-done.37, bf16[256,1024]{1,0:T(8,128)(2,1)S(1)} %copy-done.54, bf16[256,4608]{1,0:T(8,128)(2,1)S(1)} %copy-done.1, ...), custom_call_target="tpu_custom_call" | custom-call | flops 99999997952 | bytes 1000000 | tf_op jit(solution)/shard_map/grad_in/pallas_call | solution.py:107
  163.6 5.1 %grad_down.1 = (bf16[512,1024]{1,0:T(8,128)(2,1)S(1)}, bf16[512,1024]{1,0:T(8,128)(2,1)S(1)}) custom-call(s32[7]{0:T(128)S(1)} %copy-done.37, bf16[256,1024]{1,0:T(8,128)(2,1)S(1)} %copy-done.53, bf16[256,1024]{1,0:T(8,128)(2,1)} %collective-permute-done.22.refs_1_, bf16[256,1024]{1,0:T(8,128)(2,1)} %collective-permute-done.23.refs_2_, ...), custom_call_target="tpu_custom_call" | custom-call | flops 99999997952 | bytes 1000000 | tf_op jit(solution)/shard_map/grad_down/pallas_call | solution.py:107
  168.8 5.6 %grad_qkv.1 = (bf16[4,144,768]{2,1,0:T(8,128)(2,1)S(1)}, bf16[4,144,768]{2,1,0:T(8,128)(2,1)S(1)}) custom-call(s32[7]{0:T(128)S(1)} %copy-done.37, bf16[256,1024]{1,0:T(8,128)(2,1)} %get-tuple-element.104.refs_6_.refs_0_, bf16[256,1024]{1,0:T(8,128)(2,1)} %get-tuple-element.106.refs_6_.refs_1_, bf16[256,1024]{1,0:T(8,128)(2,1)} %get-tuple-element.109.refs_2_, ...), custom_call_target="tpu_custom_call" | custom-call | flops 99999997952 | bytes 1000000 | tf_op jit(solution)/shard_map/grad_qkv/pallas_call | solution.py:107
  176.5 14.4 %collective-permute-done.27.refs_3_.refs_4_ = bf16[2,160,2048]{2,1,0:T(8,128)(2,1)} collective-permute-done((bf16[2,160,2048]{2,1,0:T(8,128)(2,1)}, bf16[2,160,2048]{2,1,0:T(8,128)(2,1)}, u32[]{:S(2)}, u32[]{:S(2)}) %collective-permute-start.27) | collective-permute-done | bytes 1310752 | tf_op jit(solution)/shard_map/ppermute | solution.py:22
  200.2 18.9 %collective-permute-done.31.refs_5_ = bf16[160,2048]{1,0:T(8,128)(2,1)S(1)} collective-permute-done((bf16[160,2048]{1,0:T(8,128)(2,1)S(1)}, bf16[160,2048]{1,0:T(8,128)(2,1)S(1)}, u32[]{:S(2)}, u32[]{:S(2)}) %collective-permute-start.31) | collective-permute-done | bytes 655392 | tf_op jit(solution)/shard_map/ppermute | solution.py:22
  225.8 14.9 %collective-permute-done.34.refs_1_ = bf16[160,2048]{1,0:T(8,128)(2,1)S(1)} collective-permute-done((bf16[160,2048]{1,0:T(8,128)(2,1)S(1)}, bf16[160,2048]{1,0:T(8,128)(2,1)S(1)}, u32[]{:S(2)}, u32[]{:S(2)}) %collective-permute-start.34) | collective-permute-done | bytes 655392 | tf_op jit(solution)/shard_map/ppermute | solution.py:22
  247.7 11.2 %collective-permute-done.40.refs_1_ = bf16[256,1024]{1,0:T(8,128)(2,1)S(1)} collective-permute-done((bf16[256,1024]{1,0:T(8,128)(2,1)S(1)}, bf16[256,1024]{1,0:T(8,128)(2,1)S(1)}, u32[]{:S(2)}, u32[]{:S(2)}) %collective-permute-start.40) | collective-permute-done | bytes 524320 | tf_op jit(solution)/shard_map/ppermute | solution.py:22
  259.1 6.5 %collective-permute-done.43.refs_1_ = bf16[2,144,768]{2,1,0:T(8,128)(2,1)S(1)} collective-permute-done((bf16[2,144,768]{2,1,0:T(8,128)(2,1)}, bf16[2,144,768]{2,1,0:T(8,128)(2,1)S(1)}, u32[]{:S(2)}, u32[]{:S(2)}) %collective-permute-start.43) | collective-permute-done | bytes 442400 | tf_op jit(solution)/shard_map/ppermute | solution.py:22
  272.9 13.4 %collective-permute-done.39.refs_1_ = bf16[160,2048]{1,0:T(8,128)(2,1)S(1)} collective-permute-done((bf16[160,2048]{1,0:T(8,128)(2,1)S(1)}, bf16[160,2048]{1,0:T(8,128)(2,1)S(1)}, u32[]{:S(2)}, u32[]{:S(2)}) %collective-permute-start.39) | collective-permute-done | bytes 655392 | tf_op jit(solution)/shard_map/ppermute | solution.py:22
  289.8 5.4 %tokens_back.1.refs_2_ = f32[256,1024]{1,0:T(8,128)} custom-call(s32[7]{0:T(128)S(1)} %copy-done.37, bf16[256,1024]{1,0:T(8,128)(2,1)S(1)} %bitcast.42, f32[256,1024]{1,0:T(8,128)S(1)} %copy-done.48, bf16[1,1024]{1,0:T(2,128)(2,1)S(1)} %copy-done.13, bf16[3,256,256]{2,1,0:T(8,128)(2,1)S(1)} %bitcast.48, ...), custom_call_target="tpu_custom_call" | custom-call | flops 99999997952 | bytes 1000000 | tf_op jit(solution)/shard_map/tokens_back/pallas_call | solution.py:107
  295.2 14.2 %collective-permute-done.48.refs_1_ = bf16[160,2048]{1,0:T(8,128)(2,1)S(1)} collective-permute-done((bf16[160,2048]{1,0:T(8,128)(2,1)S(1)}, bf16[160,2048]{1,0:T(8,128)(2,1)S(1)}, u32[]{:S(2)}, u32[]{:S(2)}) %collective-permute-start.48) | collective-permute-done | bytes 655392 | tf_op jit(solution)/shard_map/ppermute | solution.py:22
  311.9 12.0 %collective-permute-done.45.refs_1_ = bf16[2,144,768]{2,1,0:T(8,128)(2,1)S(1)} collective-permute-done((bf16[2,144,768]{2,1,0:T(8,128)(2,1)S(1)}, bf16[2,144,768]{2,1,0:T(8,128)(2,1)S(1)}, u32[]{:S(2)}, u32[]{:S(2)}) %collective-permute-start.45) | collective-permute-done | bytes 442400 | tf_op jit(solution)/shard_map/ppermute | solution.py:22
  323.9 4.6 %in_finish.1 = (f32[256,4096]{1,0:T(8,128)}, f32[256,1024]{1,0:T(8,128)}) custom-call(s32[7]{0:T(128)S(1)} %copy-done.37, bf16[160,2048]{1,0:T(8,128)(2,1)S(1)} %sum.10.refs_10_.refs_0_, bf16[160,2048]{1,0:T(8,128)(2,1)S(1)} %collective-permute-done.48.refs_1_, bf16[160,2048]{1,0:T(8,128)(2,1)S(1)} %collective-permute-done.49.refs_2_, ...), custom_call_target="tpu_custom_call" | custom-call | flops 10000000000 | bytes 99999997952 | tf_op jit(solution)/shard_map/in_finish/pallas_call | solution.py:107
  330.8 3.8 %qkv_finish.1 = (f32[256,3072]{1,0:T(8,128)}, f32[8,256]{1,0:T(8,128)S(1)}) custom-call(s32[7]{0:T(128)S(1)} %copy-done.37, bf16[2,144,768]{2,1,0:T(8,128)(2,1)S(1)} %sum.11.refs_4_.refs_0_, bf16[2,144,768]{2,1,0:T(8,128)(2,1)S(1)} %collective-permute-done.45.refs_1_, bf16[2,144,768]{2,1,0:T(8,128)(2,1)S(1)} %collective-permute-done.46.refs_2_, ...), custom_call_target="tpu_custom_call" | custom-call | flops 10000000000 | bytes 99999997952 | tf_op jit(solution)/shard_map/qkv_finish/pallas_call | solution.py:107
  (269 shorter events, 116.8 us)
Async XLA Ops:
  10.2 21.3 %collective-permute-start.4 = (bf16[2,2,32,1024]{3,2,1,0:T(8,128)(2,1)S(1)}, bf16[2,2,32,1024]{3,2,1,0:T(8,128)(2,1)S(1)}, u32[]{:S(2)}, u32[]{:S(2)}) collective-permute-start(bf16[2,2,32,1024]{3,2,1,0:T(8,128)(2,1)S(1)} %get-tuple-element.99), channel_id=1, source_target_pairs={{0,4},{1,5},{2,6},{3,7},{4,0},{5,1},{6,2},{7,3},{8,12},{9,13},{10,... | collective-permute-start | bytes 786440 | tf_op jit(solution)/shard_map/ppermute | solution.py:22
  13.5 27.2 %collective-permute-start.2 = (bf16[2,256,1024]{2,1,0:T(8,128)(2,1)S(1)}, bf16[2,256,1024]{2,1,0:T(8,128)(2,1)S(1)}, u32[]{:S(2)}, u32[]{:S(2)}) collective-permute-start(bf16[2,256,1024]{2,1,0:T(8,128)(2,1)S(1)} %stack.2.refs_4_.refs_0_), channel_id=1, source_target_pairs={{0,16},{8,24},{16,0},{24,8},{1,17},{9,25},{17,1},{25,9},{2,18},{10... | collective-permute-start | bytes 3145736 | tf_op jit(solution)/shard_map/ppermute | solution.py:22
  15.3 25.4 %collective-permute-start.1 = (bf16[2,256,1024]{2,1,0:T(8,128)(2,1)S(1)}, bf16[2,256,1024]{2,1,0:T(8,128)(2,1)S(1)}, u32[]{:S(2)}, u32[]{:S(2)}) collective-permute-start(bf16[2,256,1024]{2,1,0:T(8,128)(2,1)S(1)} %stack.2.refs_4_.refs_0_), channel_id=1, source_target_pairs={{0,8},{8,0},{16,24},{24,16},{1,9},{9,1},{17,25},{25,17},{2,10},{10... | collective-permute-start | bytes 3145736 | tf_op jit(solution)/shard_map/ppermute | solution.py:22
  33.1 35.0 %collective-permute-start.8 = (bf16[4,32,1024]{2,1,0:T(8,128)(2,1)}, bf16[4,32,1024]{2,1,0:T(8,128)(2,1)}, u32[]{:S(2)}, u32[]{:S(2)}) collective-permute-start(bf16[4,32,1024]{2,1,0:T(8,128)(2,1)} %get-tuple-element.116), channel_id=1, source_target_pairs={{0,2},{1,3},{2,0},{3,1},{4,6},{5,7},{6,4},{7,5},{8,10},{9,11},{10,... | collective-permute-start | bytes 786440 | tf_op jit(solution)/shard_map/ppermute | solution.py:22
  38.2 29.9 %collective-permute-start.9 = (bf16[4,32,1024]{2,1,0:T(8,128)(2,1)}, bf16[4,32,1024]{2,1,0:T(8,128)(2,1)}, u32[]{:S(2)}, u32[]{:S(2)}) collective-permute-start(bf16[4,32,1024]{2,1,0:T(8,128)(2,1)} %get-tuple-element.117), channel_id=1, source_target_pairs={{0,4},{1,5},{2,6},{3,7},{4,0},{5,1},{6,2},{7,3},{8,12},{9,13},{10,... | collective-permute-start | bytes 786440 | tf_op jit(solution)/shard_map/ppermute | solution.py:22
  39.2 28.9 %collective-permute-start.10 = (bf16[4,32,1024]{2,1,0:T(8,128)(2,1)}, bf16[4,32,1024]{2,1,0:T(8,128)(2,1)}, u32[]{:S(2)}, u32[]{:S(2)}) collective-permute-start(bf16[4,32,1024]{2,1,0:T(8,128)(2,1)} %get-tuple-element.118), channel_id=1, source_target_pairs={{0,6},{1,7},{2,4},{3,5},{4,2},{5,3},{6,0},{7,1},{8,14},{9,15},{10,... | collective-permute-start | bytes 786440 | tf_op jit(solution)/shard_map/ppermute | solution.py:22
  136.5 27.0 %collective-permute-start.23 = (bf16[256,1024]{1,0:T(8,128)(2,1)}, bf16[256,1024]{1,0:T(8,128)(2,1)}, u32[]{:S(2)}, u32[]{:S(2)}) collective-permute-start(bf16[256,1024]{1,0:T(8,128)(2,1)} %get-tuple-element.149), channel_id=1, source_target_pairs={{0,16},{8,24},{16,0},{24,8},{1,17},{9,25},{17,1},{25,9},{2,18},{10... | collective-permute-start | bytes 1572872 | tf_op jit(solution)/shard_map/ppermute | solution.py:22
  137.9 25.6 %collective-permute-start.24 = (bf16[256,1024]{1,0:T(8,128)(2,1)}, bf16[256,1024]{1,0:T(8,128)(2,1)}, u32[]{:S(2)}, u32[]{:S(2)}) collective-permute-start(bf16[256,1024]{1,0:T(8,128)(2,1)} %get-tuple-element.150), channel_id=1, source_target_pairs={{0,24},{8,16},{16,8},{24,0},{1,25},{9,17},{17,9},{25,1},{2,26},{10... | collective-permute-start | bytes 1572872 | tf_op jit(solution)/shard_map/ppermute | solution.py:22
  139.3 24.2 %collective-permute-start.22 = (bf16[256,1024]{1,0:T(8,128)(2,1)}, bf16[256,1024]{1,0:T(8,128)(2,1)}, u32[]{:S(2)}, u32[]{:S(2)}) collective-permute-start(bf16[256,1024]{1,0:T(8,128)(2,1)} %get-tuple-element.142.refs_13_), channel_id=1, source_target_pairs={{0,8},{8,0},{16,24},{24,16},{1,9},{9,1},{17,25},{25,17},{2,10},{10... | collective-permute-start | bytes 1572872 | tf_op jit(solution)/shard_map/ppermute | solution.py:22
  161.2 29.8 %collective-permute-start.27 = (bf16[2,160,2048]{2,1,0:T(8,128)(2,1)}, bf16[2,160,2048]{2,1,0:T(8,128)(2,1)}, u32[]{:S(2)}, u32[]{:S(2)}) collective-permute-start(bf16[2,160,2048]{2,1,0:T(8,128)(2,1)} %get-tuple-element.161), channel_id=1, source_target_pairs={{0,16},{8,24},{16,0},{24,8},{1,17},{9,25},{17,1},{25,9},{2,18},{10... | collective-permute-start | bytes 3932168 | tf_op jit(solution)/shard_map/ppermute | solution.py:22
  162.5 29.3 %collective-permute-start.26 = (bf16[2,160,2048]{2,1,0:T(8,128)(2,1)}, bf16[2,160,2048]{2,1,0:T(8,128)(2,1)}, u32[]{:S(2)}, u32[]{:S(2)}) collective-permute-start(bf16[2,160,2048]{2,1,0:T(8,128)(2,1)} %get-tuple-element.155.refs_8_), channel_id=1, source_target_pairs={{0,8},{8,0},{16,24},{24,16},{1,9},{9,1},{17,25},{25,17},{2,10},{10... | collective-permute-start | bytes 3932168 | tf_op jit(solution)/shard_map/ppermute | solution.py:22
  175.8 21.9 %collective-permute-start.32 = (bf16[256,1024]{1,0:T(8,128)(2,1)S(1)}, bf16[256,1024]{1,0:T(8,128)(2,1)S(1)}, u32[]{:S(2)}, u32[]{:S(2)}) collective-permute-start(bf16[256,1024]{1,0:T(8,128)(2,1)S(1)} %get-tuple-element.168), channel_id=1, source_target_pairs={{0,2},{1,3},{2,0},{3,1},{4,6},{5,7},{6,4},{7,5},{8,10},{9,11},{10,... | collective-permute-start | bytes 1572872 | tf_op jit(solution)/shard_map/ppermute | solution.py:22
  193.9 25.2 %collective-permute-start.30 = (bf16[160,2048]{1,0:T(8,128)(2,1)S(1)}, bf16[160,2048]{1,0:T(8,128)(2,1)S(1)}, u32[]{:S(2)}, u32[]{:S(2)}) collective-permute-start(bf16[160,2048]{1,0:T(8,128)(2,1)S(1)} %get-tuple-element.164.refs_2_), channel_id=1, source_target_pairs={{0,16},{8,24},{16,0},{24,8},{1,17},{9,25},{17,1},{25,9},{2,18},{10... | collective-permute-start | bytes 1966088 | tf_op jit(solution)/shard_map/ppermute | solution.py:22
  195.6 25.9 %collective-permute-start.29 = (bf16[2,144,768]{2,1,0:T(8,128)(2,1)S(1)}, bf16[2,144,768]{2,1,0:T(8,128)(2,1)S(1)}, u32[]{:S(2)}, u32[]{:S(2)}) collective-permute-start(bf16[2,144,768]{2,1,0:T(8,128)(2,1)S(1)} %get-tuple-element.166.refs_2_), channel_id=1, source_target_pairs={{0,8},{8,0},{16,24},{24,16},{1,9},{9,1},{17,25},{25,17},{2,10},{10... | collective-permute-start | bytes 1327112 | tf_op jit(solution)/shard_map/ppermute | solution.py:22
  196.8 22.3 %collective-permute-start.31 = (bf16[160,2048]{1,0:T(8,128)(2,1)S(1)}, bf16[160,2048]{1,0:T(8,128)(2,1)S(1)}, u32[]{:S(2)}, u32[]{:S(2)}) collective-permute-start(bf16[160,2048]{1,0:T(8,128)(2,1)S(1)} %get-tuple-element.167), channel_id=1, source_target_pairs={{0,8},{8,0},{16,24},{24,16},{1,9},{9,1},{17,25},{25,17},{2,10},{10... | collective-permute-start | bytes 1966088 | tf_op jit(solution)/shard_map/ppermute | solution.py:22
  198.4 25.3 %collective-permute-start.35 = (bf16[256,1024]{1,0:T(8,128)(2,1)S(1)}, bf16[256,1024]{1,0:T(8,128)(2,1)S(1)}, u32[]{:S(2)}, u32[]{:S(2)}) collective-permute-start(bf16[256,1024]{1,0:T(8,128)(2,1)S(1)} %sum.6.refs_6_.refs_0_), channel_id=1, source_target_pairs={{0,4},{1,5},{2,6},{3,7},{4,0},{5,1},{6,2},{7,3},{8,12},{9,13},{10,... | collective-permute-start | bytes 1572872 | tf_op jit(solution)/shard_map/ppermute | solution.py:22
  224.4 34.4 %collective-permute-start.40 = (bf16[256,1024]{1,0:T(8,128)(2,1)S(1)}, bf16[256,1024]{1,0:T(8,128)(2,1)S(1)}, u32[]{:S(2)}, u32[]{:S(2)}) collective-permute-start(bf16[256,1024]{1,0:T(8,128)(2,1)S(1)} %sum.7.refs_2_.refs_0_), channel_id=1, source_target_pairs={{0,2},{1,3},{2,0},{3,1},{4,6},{5,7},{6,4},{7,5},{8,10},{9,11},{10,... | collective-permute-start | bytes 1572872 | tf_op jit(solution)/shard_map/ppermute | solution.py:22
  243.6 22.0 %collective-permute-start.43 = (bf16[2,144,768]{2,1,0:T(8,128)(2,1)}, bf16[2,144,768]{2,1,0:T(8,128)(2,1)S(1)}, u32[]{:S(2)}, u32[]{:S(2)}) collective-permute-start(bf16[2,144,768]{2,1,0:T(8,128)(2,1)} %get-tuple-element.175), channel_id=1, source_target_pairs={{0,2},{1,3},{2,0},{3,1},{4,6},{5,7},{6,4},{7,5},{8,10},{9,11},{10,... | collective-permute-start | bytes 1327112 | tf_op jit(solution)/shard_map/ppermute | solution.py:22
  244.3 24.0 %collective-permute-start.41 = (bf16[256,1024]{1,0:T(8,128)(2,1)S(1)}, bf16[256,1024]{1,0:T(8,128)(2,1)S(1)}, u32[]{:S(2)}, u32[]{:S(2)}) collective-permute-start(bf16[256,1024]{1,0:T(8,128)(2,1)S(1)} %sum.7.refs_2_.refs_0_), channel_id=1, source_target_pairs={{0,1},{1,0},{2,3},{3,2},{4,5},{5,4},{6,7},{7,6},{8,9},{9,8},{10,11... | collective-permute-start | bytes 1572872 | tf_op jit(solution)/shard_map/ppermute | solution.py:22
  244.3 42.0 %collective-permute-start.39 = (bf16[160,2048]{1,0:T(8,128)(2,1)S(1)}, bf16[160,2048]{1,0:T(8,128)(2,1)S(1)}, u32[]{:S(2)}, u32[]{:S(2)}) collective-permute-start(bf16[160,2048]{1,0:T(8,128)(2,1)S(1)} %sum.8.refs_4_.refs_0_), channel_id=1, source_target_pairs={{0,4},{1,5},{2,6},{3,7},{4,0},{5,1},{6,2},{7,3},{8,12},{9,13},{10,... | collective-permute-start | bytes 1966088 | tf_op jit(solution)/shard_map/ppermute | solution.py:22
  246.5 42.7 %collective-permute-start.37 = (bf16[3,256,256]{2,1,0:T(8,128)(2,1)}, bf16[3,256,256]{2,1,0:T(8,128)(2,1)S(1)}, u32[]{:S(2)}, u32[]{:S(2)}) collective-permute-start(bf16[3,256,256]{2,1,0:T(8,128)(2,1)} %get-tuple-element.173), channel_id=1, source_target_pairs={{0,16},{8,24},{16,0},{24,8},{1,17},{9,25},{17,1},{25,9},{2,18},{10... | collective-permute-start | bytes 1179656 | tf_op jit(solution)/shard_map/ppermute | solution.py:22
  258.9 30.5 %collective-permute-start.36 = (bf16[3,256,256]{2,1,0:T(8,128)(2,1)}, bf16[3,256,256]{2,1,0:T(8,128)(2,1)S(1)}, u32[]{:S(2)}, u32[]{:S(2)}) collective-permute-start(bf16[3,256,256]{2,1,0:T(8,128)(2,1)} %get-tuple-element.172.refs_2_), channel_id=1, source_target_pairs={{0,8},{8,0},{16,24},{24,16},{1,9},{9,1},{17,25},{25,17},{2,10},{10... | collective-permute-start | bytes 1179656 | tf_op jit(solution)/shard_map/ppermute | solution.py:22
  269.9 39.6 %collective-permute-start.44 = (bf16[2,144,768]{2,1,0:T(8,128)(2,1)S(1)}, bf16[2,144,768]{2,1,0:T(8,128)(2,1)S(1)}, u32[]{:S(2)}, u32[]{:S(2)}) collective-permute-start(bf16[2,144,768]{2,1,0:T(8,128)(2,1)S(1)} %sum.9.refs_4_.refs_0_), channel_id=1, source_target_pairs={{0,4},{1,5},{2,6},{3,7},{4,0},{5,1},{6,2},{7,3},{8,12},{9,13},{10,... | collective-permute-start | bytes 1327112 | tf_op jit(solution)/shard_map/ppermute | solution.py:22
  289.2 34.8 %collective-permute-start.49 = (bf16[160,2048]{1,0:T(8,128)(2,1)S(1)}, bf16[160,2048]{1,0:T(8,128)(2,1)S(1)}, u32[]{:S(2)}, u32[]{:S(2)}) collective-permute-start(bf16[160,2048]{1,0:T(8,128)(2,1)S(1)} %sum.10.refs_10_.refs_0_), channel_id=1, source_target_pairs={{0,1},{1,0},{2,3},{3,2},{4,5},{5,4},{6,7},{7,6},{8,9},{9,8},{10,11... | collective-permute-start | bytes 1966088 | tf_op jit(solution)/shard_map/ppermute | solution.py:22
  (99 other events, 1019.5 us)

commit v4 on v3

--- a/solution.py
+++ b/solution.py
@@ -44,26 +44,30 @@
 
 ANYWHERE = pl.BlockSpec(memory_space=pl.ANY)
 EVERY = range(100)
-COMPUTE = (
-    "project",
-    "own_keys",
-    "cached_keys",
-    "feed",
-    "attention_back",
-    "grad_qkv",
-    "grad_in",
-    "grad_down",
-    "tokens_back",
-)
-LONG = pl.CostEstimate(flops=10**11, bytes_accessed=10**6, transcendentals=0)
-SHORT = pl.CostEstimate(flops=10**10, bytes_accessed=10**11, transcendentals=0)
+TOKEN = (8, 128)
+COSTS = {'': (3000000000, 10000000000), 'grad_in': (10000000000, 1000000), 'grad_qkv': (10000000000, 1000000), 'attention_back': (10000000000, 1000000), 'feed': (100000000000, 1000000), 'tokens_back': (100000000000, 1000000), 'project': (1000000000, 1000000000), 'own_keys': (1000000000, 1000000000), 'cached_keys': (1000000000, 1000000000), 'bank_columns': (1000000000, 1000000000), 'cross': (1000000000, 1000000000), 'join': (1000000000, 1000000000), 'copy': (1000000000, 1000000000), 'choose_banks': (1000000000, 1000000000), 'grad_down': (3000000000, 10000000000)}
+PLAN = "ABNWYdqidiqdqtitiqFtHqG"
+
+
+def cost_of(name):
+    flops, size = COSTS.get(name, COSTS[""])
+    return pl.CostEstimate(flops=flops, bytes_accessed=size, transcendentals=0)
+
+
 OUT_HBM = {
-    "project": (0,),
-    "own_keys": EVERY,
+    "project": range(0, 20, 2),
+    "own_keys": (2,),
     "cached_keys": (0, 1),
     "feed": (0, 1, 2, 4, 5, 6, 8, 9, 10, 11, 12, 13, 14, 15),
 }
-IN_HBM = {"cached_keys": (0, 1, 2, 3), "attention_back": EVERY, "grad_qkv": (0, 1, 2, 3)}
+IN_HBM = {
+    "bank_columns": (0, 1),
+    "rows_stack": (0, 1),
+    "project": range(2, 10),
+    "attention_back": EVERY,
+    "grad_qkv": (0, 1, 2, 3),
+    "grad_out": EVERY,
+}
 
 
 def call(kernel, name, grid, ins, outs, scratch, scalars, mib, tokens=()):
@@ -94,8 +98,13 @@
         pltpu.HBM(o.shape, o.dtype) if i in pinned else o for i, o in enumerate(out_shapes)
     ]
 
+    out_shapes = out_shapes + [jax.ShapeDtypeStruct(TOKEN, jnp.int32)]
+    out_specs = out_specs + [whole(TOKEN)]
+    last = count + len(tokens) + len(outs)
+
     def body(sc, *refs):
-        kernel(sc, *refs[:count], *refs[count + len(tokens) :])
+        kernel(sc, *refs[:count], *refs[count + len(tokens) : last], *refs[last + 1 :])
+        refs[last][...] = jnp.zeros(TOKEN, jnp.int32)
 
     spec = pltpu.PrefetchScalarGridSpec(
         num_scalar_prefetch=1,
@@ -109,19 +118,31 @@
         grid_spec=spec,
         out_shape=out_shapes,
         compiler_params=params(mib),
-        cost_estimate=LONG if name in COMPUTE else SHORT,
+        cost_estimate=cost_of(name),
         name=name,
     )(scalars, *arrays, *tokens)
 
 
+def corner(value):
+    block = (1,) * (value.ndim - 2) + (min(16, value.shape[-2]), 128)
+    return pl.BlockSpec(block, lambda *_: (0,) * value.ndim)
+
+
 def gate(values, tokens):
     count = len(values)
+
+    def body(*refs):
+        refs[-1][...] = jnp.zeros(TOKEN, jnp.int32)
+
     return pl.pallas_call(
-        lambda *refs: None,
-        in_specs=[ANYWHERE] * (count + len(tokens)),
-        out_specs=[ANYWHERE] * count,
-        out_shape=[jax.ShapeDtypeStruct(v.shape, v.dtype) for v in values],
+        body,
+        grid=(1,),
+        in_specs=[ANYWHERE] * count + [corner(t) for t in tokens],
+        out_specs=[ANYWHERE] * count + [pl.BlockSpec(memory_space=pltpu.VMEM)],
+        out_shape=[jax.ShapeDtypeStruct(v.shape, v.dtype) for v in values]
+        + [jax.ShapeDtypeStruct(TOKEN, jnp.int32)],
         input_output_aliases={i: i for i in range(count)},
+        cost_estimate=cost_of("gate"),
         name="gate",
     )(*values, *tokens)
 
@@ -140,13 +161,17 @@
     return scale * (scaled - mean_one - unit * mean_two)
 
 
-def project_kernel(sc, rows, gain, bias, wq, wk, wv, normed, qkv):
-    part = wq.shape[1]
-    unit, _ = norm_stats(rows[...].astype(F32))
-    low = (unit * gain[...].astype(F32) + bias[...].astype(F32)).astype(BF16)
-    normed[...] = low
-    for i, weight in enumerate((wq, wk, wv)):
-        qkv[:, i * part : (i + 1) * part] = nn(low, weight[...]).astype(BF16)
+def project_kernel(count, sc, *refs):
+    rows, gains, weights = refs[:count], refs[count], refs[count + 1 : count + 4]
+    outs = refs[count + 4 :]
+    gain, bias = gains[0:1].astype(F32), gains[1:2].astype(F32)
+    part = weights[0].shape[1]
+    for i in range(count):
+        unit, _ = norm_stats(rows[i][...].astype(F32))
+        low = (unit * gain + bias).astype(BF16)
+        outs[2 * i][...] = low
+        for j, weight in enumerate(weights):
+            outs[2 * i + 1][:, j * part : (j + 1) * part] = nn(low, weight[...]).astype(BF16)
 
 
 def lane_masks():
@@ -328,11 +353,13 @@
 def feed_kernel(blocks, sc, *refs):
     att_in = refs[:blocks]
     rest = refs[blocks:]
-    tokens, cot, w_out, gain, bias, w_in, w_down = rest[:7]
-    mixed, grad_res, inner_keep, to_core, normed_out, att_out, branch_keep, sums = rest[7:15]
-    acts = rest[15 : 15 + blocks]
-    grad_att = rest[15 + blocks : 15 + 2 * blocks]
-    residual, normed, total, back = rest[15 + 2 * blocks :]
+    tokens, cot, w_out, gains, w_in, w_down = rest[:6]
+    rest = rest[6:]
+    gain, bias = gains[2:3].astype(F32), gains[3:4].astype(F32)
+    mixed, grad_res, inner_keep, to_core, normed_out, att_out, branch_keep, sums = rest[:8]
+    acts = rest[8 : 8 + blocks]
+    grad_att = rest[8 + blocks : 8 + 2 * blocks]
+    residual, normed, total, back = rest[8 + 2 * blocks :]
     step, steps = pl.program_id(0), pl.num_programs(0)
     part, width, tile = att_in[0].shape[1], tokens.shape[1], w_in.shape[1]
     my_block, core = sc[0], sc[1]
@@ -350,7 +377,7 @@
         to_core[:, base + width : base + 2 * width] = att_out[...]
         residual[...] = branch
         unit, _ = norm_stats(branch)
-        low = (unit * gain[...].astype(F32) + bias[...].astype(F32)).astype(BF16)
+        low = (unit * gain + bias).astype(BF16)
         normed[...] = low
         normed_out[...] = low
         to_core[:, base : base + width] = low
@@ -399,7 +426,7 @@
         away = back[...]
         sums[0:1] = jnp.sum(away * unit, 0, keepdims=True)
         sums[1:2] = jnp.sum(away, 0, keepdims=True)
-        found = cot[...].astype(F32) + norm_back(unit, scale, gain[...].astype(F32), away)
+        found = cot[...].astype(F32) + norm_back(unit, scale, gain, away)
         grad_res[...] = found
         low = found.astype(BF16)
         left, right = low[:, : width // 2], low[:, width // 2 :]
@@ -456,8 +483,8 @@
 def qkv_kernel(blocks, halved, sc, *refs):
     normed, grads = refs[:blocks], refs[blocks : 2 * blocks]
     weights = refs[2 * blocks : 2 * blocks + 3]
-    gain, bias, sums_two = refs[2 * blocks + 3 : 2 * blocks + 6]
-    outs = refs[2 * blocks + 6 :]
+    gains, sums_two = refs[2 * blocks + 3 : 2 * blocks + 5]
+    outs = refs[2 * blocks + 5 :]
     part = grads[0].shape[2]
     share = part // 2 if halved else part
     ahead = jnp.zeros((part, 1), F32)
@@ -480,7 +507,7 @@
         else:
             outs[0][0, :share, columns] = low
     flat = [jnp.broadcast_to(v, (part, 128)).T[0:1] for v in (ahead, plain)]
-    shift = (flat[0] - bias[...].astype(F32) * flat[1]) / gain[...].astype(F32)
+    shift = (flat[0] - gains[1:2].astype(F32) * flat[1]) / gains[0:1].astype(F32)
     row = lax.broadcasted_iota(jnp.int32, (16, part), 0)
     vectors = jnp.zeros((16, part), F32)
     for i, vector in enumerate((shift, flat[1], sums_two[0:1], sums_two[1:2])):
@@ -552,7 +579,7 @@
         sums[...] = total
 
 
-def tokens_kernel(blocks, sc, tokens, grad_res, gain, *refs):
+def tokens_kernel(blocks, sc, tokens, grad_res, gains, *refs):
     pieces = refs[:blocks]
     weights = refs[blocks : blocks + 3]
     grad_tokens, total = refs[blocks + 3 :]
@@ -573,7 +600,7 @@
     def _():
         unit, scale = norm_stats(tokens[...].astype(F32))
         grad_tokens[...] = grad_res[...] + norm_back(
-            unit, scale, gain[...].astype(F32), total[...]
+            unit, scale, gains[0:1].astype(F32), total[...]
         )
 
 
@@ -614,6 +641,14 @@
     out[:, :half], out[:, half:] = top[...], low[...]
 
 
+def nothing_kernel(sc):
+    pass
+
+
+def copy_kernel(sc, values, out):
+    out[...] = values[...]
+
+
 def sum_kernel(sc, *refs):
     total = refs[0][...].astype(F32)
     for ref in refs[1:-1]:
@@ -705,6 +740,28 @@
             ]
 
 
+def head_columns_kernel(blocks, keys, values, *outs):
+    part = keys.shape[2] // blocks
+    outs[-1][...] = jnp.zeros(TOKEN, jnp.int32)
+    for mask in range(blocks):
+        columns = pl.ds(pl.multiple_of((lax.axis_index("blk") ^ mask) * part, part), part)
+        outs[mask][0] = keys[:, :, columns]
+        outs[mask][1] = values[:, :, columns]
+
+
+def choose_kernel(chips, sc, *refs):
+    ins, outs, held = refs[: 2 * chips], refs[2 * chips : 3 * chips], refs[3 * chips]
+    count = ins[0].shape[1]
+    for i in range(2 * chips):
+        held[i // chips, i % chips] = ins[i][...]
+    for mask in range(chips):
+        for i in range(count):
+            bank = sc[2 + (sc[0] ^ mask) * 2 * count + sc[1] * count + i]
+            core, chip = (bank // count) % 2, bank // (2 * count)
+            for j in range(2):
+                outs[mask][j, i] = held[core ^ sc[1], chip ^ sc[0], j, bank % count]
+
+
 def gather_kernel(chips, sc, *refs):
     ins, (kept, sent) = refs[:chips], refs[chips:]
     count, tok, width = kept.shape
@@ -727,7 +784,43 @@
         outs[mask][1] = jnp.where(sc[1] == 0, other, mine)
 
 
-def fetch_banks(mem_keys, mem_values, places, groups, my_group, blocks, scalars, meanwhile):
+def fetch_shares(order, mem_keys, mem_values, places, blocks, zero, first, turn, second):
+    count, tok, width = mem_keys.shape
+    share = ((2, count, tok, width // blocks), BF16)
+    *parts, token = pl.pallas_call(
+        functools.partial(head_columns_kernel, blocks),
+        in_specs=[pl.BlockSpec(memory_space=pltpu.VMEM)] * 2,
+        out_specs=[pl.BlockSpec(memory_space=pltpu.VMEM)] * (blocks + 1),
+        out_shape=[jax.ShapeDtypeStruct(*share)] * blocks
+        + [jax.ShapeDtypeStruct(TOKEN, jnp.int32)],
+        compiler_params=params(10),
+        cost_estimate=cost_of("bank_columns"),
+        name="bank_columns",
+    )(mem_keys, mem_values)
+    order.last = (token,)
+    zero()
+    moved = [swap(parts[m], "blk", m) for m in range(1, blocks)]
+    own = swap(parts[0], "grp", 1)
+    order.last = order.last + tuple(moved) + (own,)
+    first()
+    parts = [parts[0]] + [swap(p, "grp", 2 * (m + 1)) for m, p in enumerate(moved)]
+    turn()
+    others = [own] + [swap(p, "grp", 1) for p in parts[1:]]
+    parts = order.call(
+        functools.partial(choose_kernel, blocks),
+        "choose_banks",
+        (1,),
+        parts + others,
+        [share] * blocks,
+        [pltpu.VMEM((2, blocks) + share[0], BF16)],
+        14,
+        places,
+    )
+    second()
+    return [parts[0]] + [swap(parts[m], "grp", 2 * m) for m in range(1, blocks)]
+
+
+def fetch_banks(order, mem_keys, mem_values, places, groups, my_group, blocks, first, second):
     count, tok, width = mem_keys.shape
     core, chips = my_group % 2, groups // 2
     came = swap(jnp.where(core == 0, mem_values, mem_keys), "grp", 1)
@@ -736,48 +829,45 @@
     def line(parts):
         return [parts[0]] + [swap(parts[m], "grp", 2 * m) for m in range(1, chips)]
 
-    parts = call(
+    parts = order.call(
         functools.partial(split_kernel, chips),
         "split_banks",
         (1,),
         [mem_keys, mem_values, came],
         [((2, count) + piece, BF16)] * chips,
         [],
+        10,
         places,
-        10,
-    )
-    meanwhile(0, parts)
-    parts = call(
+    )
+    first()
+    parts = order.call(
         functools.partial(route_kernel, chips),
         "route_banks",
         (1,),
         line(parts),
         [((2 * count,) + piece, BF16)] * chips,
         [pltpu.VMEM((chips, 2, count) + piece, BF16)],
+        10,
         places,
-        10,
-        meanwhile(1, parts),
-    )
-    meanwhile(2, parts)
-    kept, sent = call(
+    )
+    second()
+    kept, sent = order.call(
         functools.partial(gather_kernel, chips),
         "gather_banks",
         (1,),
         line(parts),
         [((count, tok, width), BF16)] * 2,
         [],
+        10,
         places,
-        10,
-        meanwhile(3, parts),
-    )
-    parts = call(
+    )
+    parts = order.call(
         functools.partial(columns_kernel, blocks),
         "bank_columns",
         (1,),
         [kept, swap(sent, "grp", 1)],
         [((2, count, tok, width // blocks), BF16)] * blocks,
         [],
-        scalars,
         10,
     )
     return [parts[0]] + [swap(parts[m], "blk", m) for m in range(1, blocks)]
@@ -787,12 +877,20 @@
     def __init__(self, scalars, last=()):
         self.scalars, self.last = scalars, last
 
-    def call(self, kernel, name, grid, ins, outs, scratch, mib):
+    def call(self, kernel, name, grid, ins, outs, scratch, mib, scalars=None):
         found = call(
-            kernel, name, grid, ins, outs, scratch, self.scalars, mib, tuple(self.last)
+            kernel,
+            name,
+            grid,
+            ins,
+            outs,
+            scratch,
+            self.scalars if scalars is None else scalars,
+            mib,
+            tuple(self.last),
         )
-        self.last = (found[0],)
-        return found
+        self.last = (found[-1],)
+        return found[:-1]
 
     def small(self, kernel, name, items, outs):
         ins = []
@@ -806,9 +904,12 @@
                 ins.append(item)
         return self.call(kernel, name, (1,), ins, [(o, BF16) for o in outs], [], 8)
 
+    def copy(self, value):
+        return self.small(copy_kernel, "copy", [value], [value.shape])[0]
+
     def gate(self, values):
-        found = gate(values, self.last)
-        self.last = (found[0],)
+        *found, token = gate(values, self.last)
+        self.last = (token,)
         return found
 
 
@@ -840,21 +941,9 @@
     seg_rows = blocks * tok
     tile = hidden_width // (2 * blocks)
     scalars, banks = indices(block_place, continues)
-    gain_one, bias_one = gain_one.reshape(1, width), bias_one.reshape(1, width)
-    gain_two, bias_two = gain_two.reshape(1, width), bias_two.reshape(1, width)
+    gains = jnp.stack([gain_one, bias_one, gain_two, bias_two])
     flat = tokens.reshape(rows, width)
     cot = cotangent.reshape(rows, width)
-
-    def gather_rows(values, order):
-        if blocks != 4:
-            return [values] + [swap(values, "blk", mask) for mask in range(1, blocks)]
-        one, two = swap(values, "blk", 1), swap(values, "blk", 2)
-        half = (2, rows // 2, width)
-        top, low = order.call(
-            cross_kernel, "cross", (1,), [one, two], [(half, BF16)] * 2, [], 8
-        )
-        top, low = swap(top, "blk", 2), swap(low, "blk", 1)
-        return [values, one, two, (top, low)]
 
     def head_weights(j, at=None):
         def index(i, sc):
@@ -871,49 +960,28 @@
     mem_block = (2, 1, tok, 128), lambda s, p, sc: (0, s, 0, p)
     early = {}
 
+
+    order = Order(scalars)
     rows_block = (None, rows, width)
-
-    def meanwhile(stage, parts):
-        if stage == 0:
-            both = call(
-                stack_kernel,
-                "stack",
-                (1,),
-                [flat, cot],
-                [((2, rows, width), BF16)],
-                [],
-                scalars,
-                8,
-                (parts[0],),
-            )
-            early["both"] = both[0]
-            return ()
-        if stage == 1:
-            return (early["both"],)
-        if stage == 3:
-            return (early["own"][0],)
-        order = Order(scalars, (parts[0],))
-        pieces = early["pieces"] = gather_rows(early["both"], order)
-        normed, qkv = [], []
-        for mask, piece in enumerate(pieces):
-            if isinstance(piece, tuple):
-                (piece,) = order.call(
-                    join_kernel, "join", (1,), piece, [(early["both"].shape, BF16)], [], 8
-                )
-                pieces[mask] = piece
-            found = order.call(
-                project_kernel,
-                "project",
-                (1,),
-                [(piece, rows_block, lambda i, sc: (0, 0, 0)), gain_one, bias_one]
-                + [head_weights(j, 0) for j in range(3)],
-                [((rows, width), BF16), ((rows, 3 * part), BF16)],
-                [],
-                12,
-            )
-            normed.append(found[0])
-            qkv.append(found[1].reshape(seq_count, tok, 3 * part))
-        early["normed"] = normed
+    normed, qkv, pieces = [], [], []
+
+    def project(some):
+        found = order.call(
+            functools.partial(project_kernel, len(some)),
+            "project",
+            (1,),
+            [(p, rows_block, lambda i, sc: (0, 0, 0)) for p in some]
+            + [gains]
+            + [head_weights(j, 0) for j in range(3)],
+            [((rows, width), BF16), ((rows, 3 * part), BF16)] * len(some),
+            [],
+            20,
+        )
+        pieces.extend(some)
+        normed.extend(found[::2])
+        qkv.extend(f.reshape(seq_count, tok, 3 * part) for f in found[1::2])
+
+    def own_keys():
         early["own"] = order.call(
             functools.partial(own_kernel, blocks),
             "own_keys",
@@ -923,14 +991,53 @@
             [pltpu.VMEM((3, blocks, tok, 128), BF16)],
             16,
         )
-        return ()
-
-    mem = fetch_banks(
-        mem_keys, mem_values, banks, groups, my_group, blocks, scalars, meanwhile
-    )
+
+    row_shape = (rows, width)
+    both_shape = (2, rows, width)
+    half_shape = (2, rows // 2, width)
+
+    def zero():
+        early["both"] = order.call(
+            stack_kernel, "rows_stack", (1,), [flat, cot], [(both_shape, BF16)], [], 8
+        )[0]
+
+    def first():
+        (both,) = order.gate([early["both"]])
+        masks = (1, 2) if blocks == 4 else range(1, blocks)
+        early["both"], early["rows"] = both, [swap(both, "blk", m) for m in masks]
+
+    def turn():
+        if blocks == 4:
+            top, low = order.call(
+                cross_kernel, "cross", (1,), early["rows"], [(half_shape, BF16)] * 2, [], 8
+            )
+            early["last"] = [swap(top, "blk", 2), swap(low, "blk", 1)]
+
+    def second():
+        project([early["both"]] + early["rows"])
+        if blocks == 4:
+            (piece,) = order.call(
+                join_kernel, "join", (1,), early["last"], [(both_shape, BF16)], [], 8
+            )
+            project([piece])
+        own_keys()
+
+    if blocks == groups // 2:
+        mem = fetch_shares(order, mem_keys, mem_values, banks, blocks, zero, first, turn, second)
+    else:
+        mem = fetch_banks(
+            order,
+            mem_keys,
+            mem_values,
+            banks,
+            groups,
+            my_group,
+            blocks,
+            lambda: (zero(), first(), turn()),
+            second,
+        )
     queries, keys, values, partial, counts = early["own"]
-    normed = early["normed"]
-    found = call(
+    found = order.call(
         functools.partial(cached_kernel, blocks),
         "cached_keys",
         (seq_count, pairs),
@@ -939,7 +1046,6 @@
         [(seg_shape, F32) + seg_block] * 2
         + [((seq_count, tok, part), BF16) + tok_block] * blocks,
         [pltpu.VMEM((2, seg_rows, 128), BF16), pltpu.VMEM((blocks, tok, 128), BF16)],
-        scalars,
         16,
     )
     attended_f, counts = found[:2]
@@ -950,12 +1056,12 @@
         return 2 * (sc[0] ^ (j // 2)) + j % 2
 
     base = blocks * tile
-    found = call(
+    found = order.call(
         functools.partial(feed_kernel, blocks),
         "feed",
         (2 * blocks,),
         attended
-        + [flat, cot, w_out, gain_two, bias_two]
+        + [flat, cot, w_out, gains]
         + [
             (w_in, (width, tile), lambda j, sc: (0, ff_tile(j, sc))),
             (w_down, (tile, width), lambda j, sc: (ff_tile(j, sc), 0)),
@@ -978,7 +1084,6 @@
             pltpu.VMEM((rows, width), F32),
             pltpu.VMEM((rows, width), F32),
         ],
-        scalars,
         28,
     )
     mixed, grad_res, inner_keep, to_core, normed_two, att_all, branch, sums_two = found[:8]
@@ -986,8 +1091,15 @@
     grad_att = [grad_att[0]] + [swap(grad_att[m], "blk", m) for m in range(1, blocks)]
     grad_att = [g.reshape(seq_count, tok, part) for g in grad_att]
     core_came = swap(to_core, "grp", 1)
-    order = Order(scalars, tuple(grad_att[1:]) + (core_came,))
-    acts = [acts[0]] + [swap(a, "blk", m + 1) for m, a in enumerate(order.gate(acts[1:]))]
+    order.last = order.last + tuple(grad_att[1:]) + (core_came,)
+    made = {}
+
+    def acts_path():
+        made["acts"] = [acts[0]] + [
+            swap(a, "blk", m + 1) for m, a in enumerate(order.gate(acts[1:]))
+        ]
+        return True
+        yield
 
     top = blocks // 2
 
@@ -1006,11 +1118,12 @@
     in_shape = (in_rows // 2, base)
     bits = [1 << i for i in range(blocks.bit_length() - 1)]
     results = {}
-    paths = {}
 
     def go(names):
         for name in names:
-            if name not in results:
+            if name == ".":
+                order.call(nothing_kernel, "pause", (1,), [], [], [], 4)
+            elif name not in results:
                 try:
                     next(paths[name])
                 except StopIteration as stop:
@@ -1027,17 +1140,18 @@
         return order.small(sum_kernel, "sum", items, [shape])[0]
 
     def sum_chips(mine, other):
-        held = total(mine, swap(other, "grp", 2))
+        came = swap(other, "grp", 2)
+        yield
+        held = total(mine, came)
         for bit in range(2, groups.bit_length() - 1):
             came = swap(held, "grp", 1 << bit)
             yield
             held = total(held, came)
         other = swap(held, "grp", 2)
-        core_held = swap(held, "grp", 1)
-        yield
-        return held, other, core_held, swap(other, "grp", 1)
-
-    found = order.call(
+        return held, other, swap(held, "grp", 1), swap(other, "grp", 1)
+
+    def back_path():
+        found = order.call(
         functools.partial(attention_back_kernel, blocks),
         "attention_back",
         (seq_count, pairs),
@@ -1060,9 +1174,12 @@
         ],
         24,
     )
-    own_grads = [g.reshape(3, rows, part) for g in found]
-
-    found = order.call(
+        made["grads"] = [g.reshape(3, rows, part) for g in found]
+        return True
+        yield
+
+    def in_start():
+        found = order.call(
         functools.partial(in_kernel, blocks),
         "grad_in",
         (blocks,),
@@ -1080,13 +1197,15 @@
         [pltpu.VMEM((in_rows, base), BF16)],
         28,
     )
-    in_sent, in_kept = (found[0], found[2]), (found[1], found[3])
+        made["kept"] = found[1], found[3]
+        made["came"] = swap(found[0], "blk", 1), swap(found[2], "blk", top)
+        return True
+        yield
 
     def in_path():
         firsts, rests = (1, top), (bits[1:], bits[:-1][::-1])
         masks = [[m for m in range(blocks) if not m & bit] for bit in firsts]
-        came = [swap(sent, "blk", bit) for sent, bit in zip(in_sent, firsts)]
-        yield
+        in_kept, came = made["kept"], made["came"]
         terms = [
             {m: [(in_kept[h], i), (came[h], i)] for i, m in enumerate(masks[h])} for h in range(2)
         ]
@@ -1110,28 +1229,28 @@
         mine, other = order.small(
             functools.partial(split_sum_kernel, len(items) // 2), "split", items, [in_shape] * 2
         )
-        yield
         return (yield from sum_chips(mine, other))
 
-    paths["i"] = in_path()
-    go("i")
-
-    found = order.call(
+    def down_start():
+        found = order.call(
         functools.partial(down_kernel, blocks),
         "grad_down",
         (2,),
         [
             (a, (rows, tile), lambda i, sc: (0, jnp.where(i == 0, 1 - sc[1], sc[1])))
-            for a in acts
+            for a in made["acts"]
         ]
-        + [(p, rows_block, lambda i, sc: (1, 0, 0)) for p in early["pieces"]],
+        + [(p, rows_block, lambda i, sc: (1, 0, 0)) for p in pieces],
         [((tile, width), BF16)] * 2,
         [],
         28,
     )
-    down_kept, down_came = found[1], swap(found[0], "grp", 1)
+        made["down"] = found[1], swap(found[0], "grp", 1)
+        return True
+        yield
 
     def down_path():
+        down_kept, down_came = made["down"]
         block = (tile // 2, width)
         items = [
             (v, block, lambda i, sc, h=h: (h, 0)) for h in range(2) for v in (down_kept, down_came)
@@ -1139,10 +1258,7 @@
         mine, other = order.small(
             functools.partial(split_sum_kernel, 2), "split", items, [block] * 2
         )
-        yield
         return (yield from sum_chips(mine, other))
-
-    paths["d"] = down_path()
 
     share = part // 2 if halved else part
     share_block = (1, share + 16, 3 * part), lambda m, sc: (m, 0, 0)
@@ -1150,24 +1266,26 @@
     def own_weights(j):
         return (w_qkv, (part, part), lambda m, sc: (sc[0] ^ m, j * blocks + sc[0]))
 
-    found = order.call(
+    def qkv_start():
+        found = order.call(
         functools.partial(qkv_kernel, blocks, halved),
         "grad_qkv",
         (blocks,),
         [(n, (rows, part), columns(0)) for n in normed]
-        + own_grads
+        + made["grads"]
         + [own_weights(j) for j in range(3)]
-        + [(gain_one, (1, part), columns(0)), (bias_one, (1, part), columns(0))]
+        + [(gains, (4, part), columns(0))]
         + [(sums_two, (2, part), columns(0))],
         [((blocks, share + 16, 3 * part), BF16) + share_block] * (2 if halved else 1),
         [],
         28,
     )
-    qkv_sent, qkv_kept = found[0], found[-1]
+        made["qkv"] = found[-1], swap(found[0], "grp", 1)
+        return True
+        yield
 
     def qkv_path():
-        came = swap(qkv_sent, "grp", 1)
-        yield
+        qkv_kept, came = made["qkv"]
         shape = qkv_kept.shape[1:]
         half = (blocks // 2,) + shape
         away, kept = order.small(
@@ -1187,20 +1305,28 @@
             for i, m in enumerate(sorted(held)):
                 held[m] = held[m] + [(came, i * count + k) for k in range(count)]
         mine, other = order.small(split_stack_kernel, "split", held[0], [half] * 2)
-        yield
         return (yield from sum_chips(mine, other))
 
-    paths["q"] = qkv_path()
-    go("q")
     def tokens_path():
-        held = order.gate(own_grads[1:])
-        grads = [own_grads[0]] + [swap(held[m], "blk", m + 1) for m in range(blocks - 1)]
-        yield
+        shape = (3, rows, part)
+        held = {m: [g] for m, g in enumerate(made["grads"])}
+        for bit in bits:
+            items = [v for m in sorted(held) if m & bit for v in held[m]]
+            (away,) = order.small(stack_kernel, "stack", items, [(len(items),) + shape])
+            came = swap(away, "blk", bit)
+            yield
+            held = {m: v for m, v in held.items() if not m & bit}
+            count = len(held[0])
+            for i, m in enumerate(sorted(held)):
+                held[m] = held[m] + [(came, i * count + k) for k in range(count)]
+        grads = held[0][:1] + [
+            (g, (None,) + shape, lambda i, sc, at=at: (at, 0, 0, 0)) for g, at in held[0][1:]
+        ]
         return order.call(
             functools.partial(tokens_kernel, blocks),
             "tokens_back",
             (blocks,),
-            [flat, grad_res, gain_one] + grads + [head_weights(j) for j in range(3)],
+            [flat, grad_res, gains] + grads + [head_weights(j) for j in range(3)],
             [((rows, width), F32)],
             [pltpu.VMEM((rows, width), F32)],
             24,
@@ -1249,13 +1375,25 @@
         )
         yield
 
-    paths["t"] = tokens_path()
-    paths["F"], paths["G"], paths["H"] = down_finish(), qkv_finish(), in_finish()
-    if groups == 8 and blocks == 4:
-        go("diqdiqdiqtqdFitiqHqG")
+    paths = {
+        "A": acts_path(),
+        "B": back_path(),
+        "N": in_start(),
+        "W": down_start(),
+        "Y": qkv_start(),
+        "d": down_path(),
+        "i": in_path(),
+        "q": qkv_path(),
+        "t": tokens_path(),
+        "F": down_finish(),
+        "H": in_finish(),
+        "G": qkv_finish(),
+    }
+    go(PLAN if groups == 8 and blocks == 4 else "ABNWY")
     while len(results) < len(paths):
-        for name in sorted(paths):
-            if name.islower() or "d" in results and "i" in results and "q" in results:
+        for name in paths:
+            needs = {"F": "d", "H": "i", "G": "q"}.get(name)
+            if needs is None or needs in results:
                 go(name)
     (grad_down,) = results["F"]
     grad_qkv, sums = results["G"]

time: 336 us -> 308 us (0.917)
  waiting for transfers between devices: 148 us -> 122 us
  starting transfers between devices: 52.1 us -> 69.9 us
  local copies, waits for them, and re-layouts: 20.4 us -> 7.99 us
  Pallas kernels: 112 us -> 105 us
    ppermute x51 -> x52, waiting for transfers between devices: 148 us -> 122 us  [swap(): return lax.ppermute(values, axis, [(i, i ^ mask) for i in range(size)])]
    ppermute x51 -> x52, starting transfers between devices: 52.1 us -> 69.9 us  [swap(): return lax.ppermute(values, axis, [(i, i ^ mask) for i in range(size)])]
    unnamed x144 -> x100, local copies, waits for them, and re-layouts: 19.8 us -> 7.39 us
    pallas_call x34 -> x31, Pallas kernels: 110 us -> 101 us  [call(): pl.pallas_call(body, grid_spec=spec, out_shape=out_shapes, compiler_param...]
  transfers between devices with their start and end apart: 51 -> 52, of which waited for: 23 -> 26; matrix products, arithmetic and copies ran while one was open for 0% -> 0% of each run, Pallas kernels for 23% -> 23%
where the time goes in v4:
time: 308 us; the launch traced here: 307 us
  waiting for transfers between devices  122 us (40%)
  Pallas kernels  105 us (34%)
  starting transfers between devices  69.9 us (23%)
  local copies, waits for them, and re-layouts  7.99 us (3%)
    ppermute x52, waiting for transfers between devices, swap(): return lax.ppermute(values, axis, [(i, i ^ mask) for i in range(size)])  122 us
    pallas_call x31, Pallas kernels, call(): pl.pallas_call(body, grid_spec=spec, out_shape=out_shapes, compiler_param...  101 us
    ppermute x52, starting transfers between devices, swap(): return lax.ppermute(values, axis, [(i, i ^ mask) for i in range(size)])  69.9 us
    unnamed x100, local copies, waits for them, and re-layouts  7.39 us
  transfers between devices with their start and end apart: 52, of which 26 were waited for; matrix products, arithmetic and copies ran while one was open for 0% of the time, Pallas kernels for 23%

profile of v4, /device:TPU:0, one launch (start us, length us, event | category | flops | bytes accessed | tf_op | source)
XLA Modules:
  0.0 307.3 jit_solution(4325248458615328397)
XLA Ops:
  13.0 6.2 %collective-permute-done.1.refs_3_ = bf16[2,2,128,256]{3,2,1,0:T(8,128)(2,1)S(1)} collective-permute-done((bf16[2,2,128,256]{3,2,1,0:T(8,128)(2,1)S(1)}, bf16[2,2,128,256]{3,2,1,0:T(8,128)(2,1)S(1)}, u32[]{:S(2)}, u32[]{:S(2)}) %collective-permute-start.1) | collective-permute-done | bytes 262176 | tf_op jit(solution)/shard_map/ppermute | solution.py:22
  28.1 17.5 %collective-permute-done.5.refs_1_.refs_2_.refs_6_ = bf16[2,256,1024]{2,1,0:T(8,128)(2,1)S(1)} collective-permute-done((bf16[2,256,1024]{2,1,0:T(8,128)(2,1)}, bf16[2,256,1024]{2,1,0:T(8,128)(2,1)S(1)}, u32[]{:S(2)}, u32[]{:S(2)}) %collective-permute-start.5) | collective-permute-done | bytes 1048608 | tf_op jit(solution)/shard_map/ppermute | solution.py:22
  57.7 4.7 %project.2 = (bf16[256,1024]{1,0:T(8,128)(2,1)}, bf16[256,768]{1,0:T(8,128)(2,1)S(1)}, bf16[256,1024]{1,0:T(8,128)(2,1)}, bf16[256,768]{1,0:T(8,128)(2,1)S(1)}, ...) custom-call(s32[7]{0:T(128)S(1)} %copy-done.12, ...), custom_call_target="tpu_custom_call" | custom-call | flops 1000000000 | bytes 1000000000 | tf_op jit(solution)/shard_map/project/pallas_call | solution.py:116
  66.8 6.1 %own_keys.1 = (bf16[2,512,256]{2,1,0:T(8,128)(2,1)S(1)}, bf16[2,512,256]{2,1,0:T(8,128)(2,1)S(1)}, bf16[2,512,256]{2,1,0:T(8,128)(2,1)}, f32[2,512,256]{2,1,0:T(...) custom-call(s32[7]{0:T(128)S(1)} %copy-done.12, bf16[2,128,768]{2,1,0:T(8,128)(2,1)S(1)} %bitcast.26, ...), custom_call_target="tpu_custom_call" | custom-call | flops 1000000000 | bytes 1000000000 | tf_op jit(solution)/shard_map/own_keys/pallas_call | solution.py:116
  76.2 6.5 %cached_keys.1 = (f32[2,512,256]{2,1,0:T(8,128)}, f32[2,512,256]{2,1,0:T(8,128)}, bf16[2,128,256]{2,1,0:T(8,128)(2,1)S(1)}, bf16[2,128,256]{2,1,0:T(8,128)(2,1)S...) custom-call(s32[7]{0:T(128)S(1)} %copy-done.12, ...), custom_call_target="tpu_custom_call" | custom-call | flops 1000000000 | bytes 1000000000 | tf_op jit(solution)/shard_map/cached_keys/pallas_call | solution.py:116
  89.8 20.2 %feed.1 = (bf16[256,1024]{1,0:T(8,128)(2,1)}, f32[256,1024]{1,0:T(8,128)}, bf16[256,2048]{1,0:T(8,128)(2,1)}, bf16[256,4608]{1,0:T(8,128)(2,1)S(1)}, bf16[256,10...) custom-call(s32[7]{0:T(128)S(1)} %copy-done.12, ...), custom_call_target="tpu_custom_call" | custom-call | flops 99999997952 | bytes 1000000 | tf_op jit(solution)/shard_map/feed/pallas_call | solution.py:116
  126.5 13.9 %attention_back.1 = (bf16[3,2,128,256]{3,2,1,0:T(8,128)(2,1)S(1)}, bf16[3,2,128,256]{3,2,1,0:T(8,128)(2,1)S(1)}, bf16[3,2,128,256]{3,2,1,0:T(8,128)(2,1)S(1)}, b...) custom-call(s32[7]{0:T(128)S(1)} %copy-done.12, bf16[2,512,256]{2,1,0:T(8,128)(2,1)} %copy-done.4, ...), custom_call_target="tpu_custom_call" | custom-call | flops 10000000000 | bytes 1000000 | tf_op jit(solution)/shard_map/attention_back/pallas_call | solution.py:116
  140.6 6.3 %grad_in.1 = (bf16[2,160,2048]{2,1,0:T(8,128)(2,1)S(1)}, bf16[2,160,2048]{2,1,0:T(8,128)(2,1)S(1)}, bf16[2,160,2048]{2,1,0:T(8,128)(2,1)S(1)}, bf16[2,160,2048]{2,1,0:T(8,128)(2,1)S(1)}, s32[8,128]{1,0:T(8,128)S(1)}) custom-call(s32[7]{0:T(128)S(1)} %copy-done.12, bf16[256,1024]{1,0:T(8,128)(2,1)S(1)} %copy-done.27, ...), custom_call_target="tpu_custom_call" | custom-call | flops 10000000000 | bytes 1000000 | tf_op jit(solution)/shard_map/grad_in/pallas_call | solution.py:116
  152.8 5.7 %grad_qkv.1 = (bf16[4,144,768]{2,1,0:T(8,128)(2,1)S(1)}, bf16[4,144,768]{2,1,0:T(8,128)(2,1)S(1)}, s32[8,128]{1,0:T(8,128)S(1)}) custom-call(s32[7]{0:T(128)S(1)} %copy-done.12, bf16[256,1024]{1,0:T(8,128)(2,1)} %get-tuple-element.188.refs_0_, bf16[256,1024]{1,0:T(8,128)(2,1)} %get-tuple-element.189.refs_1_, bf16[256,1024]{1,0:T(8,128)(2,1)} %get-tuple-element.190.refs_2_, ...), custom_call_target="tpu_custom_call" | custom-call | flops 10000000000 | bytes 1000000 | tf_op jit(solution)/shard_map/grad_qkv/pallas_call | solution.py:116
  159.9 5.6 %collective-permute-start.34 = (bf16[256,1024]{1,0:T(8,128)(2,1)S(1)}, bf16[256,1024]{1,0:T(8,128)(2,1)S(1)}, u32[]{:S(2)}, u32[]{:S(2)}) collective-permute-start(bf16[256,1024]{1,0:T(8,128)(2,1)S(1)} %get-tuple-element.221), channel_id=1, source_target_pairs={{0,2},{1,3},{2,0},{3,1},{4,6},{5,7},{6,4},{7,5},{8,10},{9,11},{10,... | collective-permute-start | bytes 1572872 | tf_op jit(solution)/shard_map/ppermute | solution.py:22
  166.2 9.6 %collective-permute-done.30.refs_1_ = bf16[2,160,2048]{2,1,0:T(8,128)(2,1)S(1)} collective-permute-done((bf16[2,160,2048]{2,1,0:T(8,128)(2,1)S(1)}, bf16[2,160,2048]{2,1,0:T(8,128)(2,1)S(1)}, u32[]{:S(2)}, u32[]{:S(2)}) %collective-permute-start.30) | collective-permute-done | bytes 1310752 | tf_op jit(solution)/shard_map/ppermute | solution.py:22
  181.5 6.8 %collective-permute-start.36 = (bf16[256,1024]{1,0:T(8,128)(2,1)S(1)}, bf16[256,1024]{1,0:T(8,128)(2,1)S(1)}, u32[]{:S(2)}, u32[]{:S(2)}) collective-permute-start(bf16[256,1024]{1,0:T(8,128)(2,1)S(1)} %get-tuple-element.226.refs_0_), channel_id=1, source_target_pairs={{0,4},{1,5},{2,6},{3,7},{4,0},{5,1},{6,2},{7,3},{8,12},{9,13},{10,... | collective-permute-start | bytes 1572872 | tf_op jit(solution)/shard_map/ppermute | solution.py:22
  192.3 4.1 %collective-permute-done.33.refs_5_ = bf16[160,2048]{1,0:T(8,128)(2,1)S(1)} collective-permute-done((bf16[160,2048]{1,0:T(8,128)(2,1)S(1)}, bf16[160,2048]{1,0:T(8,128)(2,1)S(1)}, u32[]{:S(2)}, u32[]{:S(2)}) %collective-permute-start.33) | collective-permute-done | bytes 655392 | tf_op jit(solution)/shard_map/ppermute | solution.py:22
  197.6 4.4 %collective-permute-done.29.refs_1_ = bf16[2,144,768]{2,1,0:T(8,128)(2,1)S(1)} collective-permute-done((bf16[2,144,768]{2,1,0:T(8,128)(2,1)S(1)}, bf16[2,144,768]{2,1,0:T(8,128)(2,1)S(1)}, u32[]{:S(2)}, u32[]{:S(2)}) %collective-permute-start.29) | collective-permute-done | bytes 442400 | tf_op jit(solution)/shard_map/ppermute | solution.py:22
  204.2 5.5 %collective-permute-start.38 = (bf16[160,2048]{1,0:T(8,128)(2,1)S(1)}, bf16[160,2048]{1,0:T(8,128)(2,1)S(1)}, u32[]{:S(2)}, u32[]{:S(2)}) collective-permute-start(bf16[160,2048]{1,0:T(8,128)(2,1)S(1)} %get-tuple-element.232), channel_id=1, source_target_pairs={{0,2},{1,3},{2,0},{3,1},{4,6},{5,7},{6,4},{7,5},{8,10},{9,11},{10,... | collective-permute-start | bytes 1966088 | tf_op jit(solution)/shard_map/ppermute | solution.py:22
  213.5 5.4 %collective-permute-start.40 = (bf16[256,1024]{1,0:T(8,128)(2,1)S(1)}, bf16[256,1024]{1,0:T(8,128)(2,1)S(1)}, u32[]{:S(2)}, u32[]{:S(2)}) collective-permute-start(bf16[256,1024]{1,0:T(8,128)(2,1)S(1)} %get-tuple-element.236.refs_0_), channel_id=1, source_target_pairs={{0,2},{1,3},{2,0},{3,1},{4,6},{5,7},{6,4},{7,5},{8,10},{9,11},{10,... | collective-permute-start | bytes 1572872 | tf_op jit(solution)/shard_map/ppermute | solution.py:22
  218.9 12.8 %collective-permute-done.38.refs_1_ = bf16[160,2048]{1,0:T(8,128)(2,1)S(1)} collective-permute-done((bf16[160,2048]{1,0:T(8,128)(2,1)S(1)}, bf16[160,2048]{1,0:T(8,128)(2,1)S(1)}, u32[]{:S(2)}, u32[]{:S(2)}) %collective-permute-start.38) | collective-permute-done | bytes 655392 | tf_op jit(solution)/shard_map/ppermute | solution.py:22
  236.1 9.8 %collective-permute-done.40.refs_1_ = bf16[256,1024]{1,0:T(8,128)(2,1)S(1)} collective-permute-done((bf16[256,1024]{1,0:T(8,128)(2,1)S(1)}, bf16[256,1024]{1,0:T(8,128)(2,1)S(1)}, u32[]{:S(2)}, u32[]{:S(2)}) %collective-permute-start.40) | collective-permute-done | bytes 524320 | tf_op jit(solution)/shard_map/ppermute | solution.py:22
  247.7 6.6 %collective-permute-done.44.refs_1_ = bf16[160,2048]{1,0:T(8,128)(2,1)S(1)} collective-permute-done((bf16[160,2048]{1,0:T(8,128)(2,1)S(1)}, bf16[160,2048]{1,0:T(8,128)(2,1)S(1)}, u32[]{:S(2)}, u32[]{:S(2)}) %collective-permute-start.44) | collective-permute-done | bytes 655392 | tf_op jit(solution)/shard_map/ppermute | solution.py:22
  255.0 5.0 %collective-permute-done.43.refs_1_ = bf16[2,144,768]{2,1,0:T(8,128)(2,1)S(1)} collective-permute-done((bf16[2,144,768]{2,1,0:T(8,128)(2,1)S(1)}, bf16[2,144,768]{2,1,0:T(8,128)(2,1)S(1)}, u32[]{:S(2)}, u32[]{:S(2)}) %collective-permute-start.43) | collective-permute-done | bytes 442400 | tf_op jit(solution)/shard_map/ppermute | solution.py:22
  266.9 10.9 %collective-permute-done.46.refs_1_ = bf16[160,2048]{1,0:T(8,128)(2,1)S(1)} collective-permute-done((bf16[160,2048]{1,0:T(8,128)(2,1)S(1)}, bf16[160,2048]{1,0:T(8,128)(2,1)S(1)}, u32[]{:S(2)}, u32[]{:S(2)}) %collective-permute-start.46) | collective-permute-done | bytes 655392 | tf_op jit(solution)/shard_map/ppermute | solution.py:22
  277.8 5.4 %tokens_back.1 = (f32[256,1024]{1,0:T(8,128)}, s32[8,128]{1,0:T(8,128)S(1)}) custom-call(s32[7]{0:T(128)S(1)} %copy-done.12, bf16[256,1024]{1,0:T(8,128)(2,1)S(1)} %bitcast.46, f32[256,1024]{1,0:T(8,128)S(1)} %copy-done.33, bf16[4,1024]{1,0:T(4,128)(2,1)S(1)} %copy-done.10, bf16[3,256,256]{2,1,0:T(8,128)(2,1)S(1)} %bitcast.52, ...), custom_call_target="tpu_custom_call" | custom-call | flops 99999997952 | bytes 1000000 | tf_op jit(solution)/shard_map/tokens_back/pallas_call | solution.py:116
  283.2 4.6 %in_finish.1 = (f32[256,4096]{1,0:T(8,128)}, f32[256,1024]{1,0:T(8,128)}, s32[8,128]{1,0:T(8,128)S(1)}) custom-call(s32[7]{0:T(128)S(1)} %copy-done.12, bf16[160,2048]{1,0:T(8,128)(2,1)S(1)} %get-tuple-element.246.refs_0_, bf16[160,2048]{1,0:T(8,128)(2,1)S(1)} %collective-permute-done.46.refs_1_, bf16[160,2048]{1,0:T(8,128)(2,1)S(1)} %collective-permute-done.47.refs_2_, ...), custom_call_target="tpu_custom_call" | custom-call | flops 3000000000 | bytes 10000000000 | tf_op jit(solution)/shard_map/in_finish/pallas_call | solution.py:116
  289.1 12.0 %collective-permute-done.49.refs_1_ = bf16[2,144,768]{2,1,0:T(8,128)(2,1)S(1)} collective-permute-done((bf16[2,144,768]{2,1,0:T(8,128)(2,1)S(1)}, bf16[2,144,768]{2,1,0:T(8,128)(2,1)S(1)}, u32[]{:S(2)}, u32[]{:S(2)}) %collective-permute-start.49) | collective-permute-done | bytes 442400 | tf_op jit(solution)/shard_map/ppermute | solution.py:22
  (224 shorter events, 110.3 us)
Async XLA Ops:
  21.6 24.0 %collective-permute-start.5 = (bf16[2,256,1024]{2,1,0:T(8,128)(2,1)}, bf16[2,256,1024]{2,1,0:T(8,128)(2,1)S(1)}, u32[]{:S(2)}, u32[]{:S(2)}) collective-permute-start(bf16[2,256,1024]{2,1,0:T(8,128)(2,1)} %get-tuple-element.141.refs_0_.refs_4_), channel_id=1, source_target_pairs={{0,16},{8,24},{16,0},{24,8},{1,17},{9,25},{17,1},{25,9},{2,18},{10... | collective-permute-start | bytes 3145736 | tf_op jit(solution)/shard_map/ppermute | solution.py:22
  23.1 22.7 %collective-permute-start.4 = (bf16[2,256,1024]{2,1,0:T(8,128)(2,1)}, bf16[2,256,1024]{2,1,0:T(8,128)(2,1)S(1)}, u32[]{:S(2)}, u32[]{:S(2)}) collective-permute-start(bf16[2,256,1024]{2,1,0:T(8,128)(2,1)} %get-tuple-element.141.refs_0_.refs_4_), channel_id=1, source_target_pairs={{0,8},{8,0},{16,24},{24,16},{1,9},{9,1},{17,25},{25,17},{2,10},{10... | collective-permute-start | bytes 3145736 | tf_op jit(solution)/shard_map/ppermute | solution.py:22
  23.7 26.5 %collective-permute-start.6 = (bf16[2,2,128,256]{3,2,1,0:T(8,128)(2,1)}, bf16[2,2,128,256]{3,2,1,0:T(8,128)(2,1)S(1)}, u32[]{:S(2)}, u32[]{:S(2)}) collective-permute-start(bf16[2,2,128,256]{3,2,1,0:T(8,128)(2,1)} %copy-done.40), channel_id=1, source_target_pairs={{0,2},{1,3},{2,0},{3,1},{4,6},{5,7},{6,4},{7,5},{8,10},{9,11},{10,... | collective-permute-start | bytes 786440 | tf_op jit(solution)/shard_map/ppermute | solution.py:22
  25.3 24.9 %collective-permute-start.7 = (bf16[2,2,128,256]{3,2,1,0:T(8,128)(2,1)}, bf16[2,2,128,256]{3,2,1,0:T(8,128)(2,1)S(1)}, u32[]{:S(2)}, u32[]{:S(2)}) collective-permute-start(bf16[2,2,128,256]{3,2,1,0:T(8,128)(2,1)} %copy-done.39), channel_id=1, source_target_pairs={{0,4},{1,5},{2,6},{3,7},{4,0},{5,1},{6,2},{7,3},{8,12},{9,13},{10,... | collective-permute-start | bytes 786440 | tf_op jit(solution)/shard_map/ppermute | solution.py:22
  27.8 22.8 %collective-permute-start.8 = (bf16[2,2,128,256]{3,2,1,0:T(8,128)(2,1)}, bf16[2,2,128,256]{3,2,1,0:T(8,128)(2,1)S(1)}, u32[]{:S(2)}, u32[]{:S(2)}) collective-permute-start(bf16[2,2,128,256]{3,2,1,0:T(8,128)(2,1)} %copy-done.38), channel_id=1, source_target_pairs={{0,6},{1,7},{2,4},{3,5},{4,2},{5,3},{6,0},{7,1},{8,14},{9,15},{10,... | collective-permute-start | bytes 786440 | tf_op jit(solution)/shard_map/ppermute | solution.py:22
  54.8 21.3 %collective-permute-start.15 = (bf16[2,2,128,256]{3,2,1,0:T(8,128)(2,1)S(1)}, bf16[2,2,128,256]{3,2,1,0:T(8,128)(2,1)S(1)}, u32[]{:S(2)}, u32[]{:S(2)}) collective-permute-start(bf16[2,2,128,256]{3,2,1,0:T(8,128)(2,1)S(1)} %get-tuple-element.162), channel_id=1, source_target_pairs={{0,4},{1,5},{2,6},{3,7},{4,0},{5,1},{6,2},{7,3},{8,12},{9,13},{10,... | collective-permute-start | bytes 786440 | tf_op jit(solution)/shard_map/ppermute | solution.py:22
  122.3 26.5 %collective-permute-start.24 = (bf16[256,1024]{1,0:T(8,128)(2,1)}, bf16[256,1024]{1,0:T(8,128)(2,1)S(1)}, u32[]{:S(2)}, u32[]{:S(2)}) collective-permute-start(bf16[256,1024]{1,0:T(8,128)(2,1)} %get-tuple-element.195), channel_id=1, source_target_pairs={{0,8},{8,0},{16,24},{24,16},{1,9},{9,1},{17,25},{25,17},{2,10},{10... | collective-permute-start | bytes 1572872 | tf_op jit(solution)/shard_map/ppermute | solution.py:22
  123.4 25.5 %collective-permute-start.25 = (bf16[256,1024]{1,0:T(8,128)(2,1)}, bf16[256,1024]{1,0:T(8,128)(2,1)S(1)}, u32[]{:S(2)}, u32[]{:S(2)}) collective-permute-start(bf16[256,1024]{1,0:T(8,128)(2,1)} %get-tuple-element.196), channel_id=1, source_target_pairs={{0,16},{8,24},{16,0},{24,8},{1,17},{9,25},{17,1},{25,9},{2,18},{10... | collective-permute-start | bytes 1572872 | tf_op jit(solution)/shard_map/ppermute | solution.py:22
  124.3 24.6 %collective-permute-start.26 = (bf16[256,1024]{1,0:T(8,128)(2,1)}, bf16[256,1024]{1,0:T(8,128)(2,1)S(1)}, u32[]{:S(2)}, u32[]{:S(2)}) collective-permute-start(bf16[256,1024]{1,0:T(8,128)(2,1)} %get-tuple-element.197), channel_id=1, source_target_pairs={{0,24},{8,16},{16,8},{24,0},{1,25},{9,17},{17,9},{25,1},{2,26},{10... | collective-permute-start | bytes 1572872 | tf_op jit(solution)/shard_map/ppermute | solution.py:22
  146.8 29.0 %collective-permute-start.30 = (bf16[2,160,2048]{2,1,0:T(8,128)(2,1)S(1)}, bf16[2,160,2048]{2,1,0:T(8,128)(2,1)S(1)}, u32[]{:S(2)}, u32[]{:S(2)}) collective-permute-start(bf16[2,160,2048]{2,1,0:T(8,128)(2,1)S(1)} %get-tuple-element.214), channel_id=1, source_target_pairs={{0,8},{8,0},{16,24},{24,16},{1,9},{9,1},{17,25},{25,17},{2,10},{10... | collective-permute-start | bytes 3932168 | tf_op jit(solution)/shard_map/ppermute | solution.py:22
  147.9 29.2 %collective-permute-start.31 = (bf16[2,160,2048]{2,1,0:T(8,128)(2,1)S(1)}, bf16[2,160,2048]{2,1,0:T(8,128)(2,1)S(1)}, u32[]{:S(2)}, u32[]{:S(2)}) collective-permute-start(bf16[2,160,2048]{2,1,0:T(8,128)(2,1)S(1)} %get-tuple-element.216), channel_id=1, source_target_pairs={{0,16},{8,24},{16,0},{24,8},{1,17},{9,25},{17,1},{25,9},{2,18},{10... | collective-permute-start | bytes 3932168 | tf_op jit(solution)/shard_map/ppermute | solution.py:22
  159.9 20.9 %collective-permute-start.34 = (bf16[256,1024]{1,0:T(8,128)(2,1)S(1)}, bf16[256,1024]{1,0:T(8,128)(2,1)S(1)}, u32[]{:S(2)}, u32[]{:S(2)}) collective-permute-start(bf16[256,1024]{1,0:T(8,128)(2,1)S(1)} %get-tuple-element.221), channel_id=1, source_target_pairs={{0,2},{1,3},{2,0},{3,1},{4,6},{5,7},{6,4},{7,5},{8,10},{9,11},{10,... | collective-permute-start | bytes 1572872 | tf_op jit(solution)/shard_map/ppermute | solution.py:22
  180.1 21.9 %collective-permute-start.29 = (bf16[2,144,768]{2,1,0:T(8,128)(2,1)S(1)}, bf16[2,144,768]{2,1,0:T(8,128)(2,1)S(1)}, u32[]{:S(2)}, u32[]{:S(2)}) collective-permute-start(bf16[2,144,768]{2,1,0:T(8,128)(2,1)S(1)} %get-tuple-element.212), channel_id=1, source_target_pairs={{0,8},{8,0},{16,24},{24,16},{1,9},{9,1},{17,25},{25,17},{2,10},{10... | collective-permute-start | bytes 1327112 | tf_op jit(solution)/shard_map/ppermute | solution.py:22
  181.5 28.2 %collective-permute-start.36 = (bf16[256,1024]{1,0:T(8,128)(2,1)S(1)}, bf16[256,1024]{1,0:T(8,128)(2,1)S(1)}, u32[]{:S(2)}, u32[]{:S(2)}) collective-permute-start(bf16[256,1024]{1,0:T(8,128)(2,1)S(1)} %get-tuple-element.226.refs_0_), channel_id=1, source_target_pairs={{0,4},{1,5},{2,6},{3,7},{4,0},{5,1},{6,2},{7,3},{8,12},{9,13},{10,... | collective-permute-start | bytes 1572872 | tf_op jit(solution)/shard_map/ppermute | solution.py:22
  204.2 27.6 %collective-permute-start.38 = (bf16[160,2048]{1,0:T(8,128)(2,1)S(1)}, bf16[160,2048]{1,0:T(8,128)(2,1)S(1)}, u32[]{:S(2)}, u32[]{:S(2)}) collective-permute-start(bf16[160,2048]{1,0:T(8,128)(2,1)S(1)} %get-tuple-element.232), channel_id=1, source_target_pairs={{0,2},{1,3},{2,0},{3,1},{4,6},{5,7},{6,4},{7,5},{8,10},{9,11},{10,... | collective-permute-start | bytes 1966088 | tf_op jit(solution)/shard_map/ppermute | solution.py:22
  212.2 33.8 %collective-permute-start.37 = (bf16[2,3,256,256]{3,2,1,0:T(8,128)(2,1)S(1)}, bf16[2,3,256,256]{3,2,1,0:T(8,128)(2,1)S(1)}, u32[]{:S(2)}, u32[]{:S(2)}) collective-permute-start(bf16[2,3,256,256]{3,2,1,0:T(8,128)(2,1)S(1)} %get-tuple-element.230), channel_id=1, source_target_pairs={{0,8},{8,0},{16,24},{24,16},{1,9},{9,1},{17,25},{25,17},{2,10},{10... | collective-permute-start | bytes 2359304 | tf_op jit(solution)/shard_map/ppermute | solution.py:22
  213.5 32.4 %collective-permute-start.40 = (bf16[256,1024]{1,0:T(8,128)(2,1)S(1)}, bf16[256,1024]{1,0:T(8,128)(2,1)S(1)}, u32[]{:S(2)}, u32[]{:S(2)}) collective-permute-start(bf16[256,1024]{1,0:T(8,128)(2,1)S(1)} %get-tuple-element.236.refs_0_), channel_id=1, source_target_pairs={{0,2},{1,3},{2,0},{3,1},{4,6},{5,7},{6,4},{7,5},{8,10},{9,11},{10,... | collective-permute-start | bytes 1572872 | tf_op jit(solution)/shard_map/ppermute | solution.py:22
  232.5 21.8 %collective-permute-start.44 = (bf16[160,2048]{1,0:T(8,128)(2,1)S(1)}, bf16[160,2048]{1,0:T(8,128)(2,1)S(1)}, u32[]{:S(2)}, u32[]{:S(2)}) collective-permute-start(bf16[160,2048]{1,0:T(8,128)(2,1)S(1)} %get-tuple-element.239.refs_0_), channel_id=1, source_target_pairs={{0,4},{1,5},{2,6},{3,7},{4,0},{5,1},{6,2},{7,3},{8,12},{9,13},{10,... | collective-permute-start | bytes 1966088 | tf_op jit(solution)/shard_map/ppermute | solution.py:22
  233.6 27.1 %collective-permute-start.41 = (bf16[256,1024]{1,0:T(8,128)(2,1)S(1)}, bf16[256,1024]{1,0:T(8,128)(2,1)S(1)}, u32[]{:S(2)}, u32[]{:S(2)}) collective-permute-start(bf16[256,1024]{1,0:T(8,128)(2,1)S(1)} %get-tuple-element.236.refs_0_), channel_id=1, source_target_pairs={{0,1},{1,0},{2,3},{3,2},{4,5},{5,4},{6,7},{7,6},{8,9},{9,8},{10,11... | collective-permute-start | bytes 1572872 | tf_op jit(solution)/shard_map/ppermute | solution.py:22
  233.6 26.4 %collective-permute-start.43 = (bf16[2,144,768]{2,1,0:T(8,128)(2,1)S(1)}, bf16[2,144,768]{2,1,0:T(8,128)(2,1)S(1)}, u32[]{:S(2)}, u32[]{:S(2)}) collective-permute-start(bf16[2,144,768]{2,1,0:T(8,128)(2,1)S(1)} %get-tuple-element.238), channel_id=1, source_target_pairs={{0,2},{1,3},{2,0},{3,1},{4,6},{5,7},{6,4},{7,5},{8,10},{9,11},{10,... | collective-permute-start | bytes 1327112 | tf_op jit(solution)/shard_map/ppermute | solution.py:22
  246.5 31.3 %collective-permute-start.39 = (bf16[2,3,256,256]{3,2,1,0:T(8,128)(2,1)S(1)}, bf16[2,3,256,256]{3,2,1,0:T(8,128)(2,1)S(1)}, u32[]{:S(2)}, u32[]{:S(2)}) collective-permute-start(bf16[2,3,256,256]{3,2,1,0:T(8,128)(2,1)S(1)} %get-tuple-element.235), channel_id=1, source_target_pairs={{0,16},{8,24},{16,0},{24,8},{1,17},{9,25},{17,1},{25,9},{2,18},{10... | collective-permute-start | bytes 2359304 | tf_op jit(solution)/shard_map/ppermute | solution.py:22
  255.0 22.8 %collective-permute-start.46 = (bf16[160,2048]{1,0:T(8,128)(2,1)S(1)}, bf16[160,2048]{1,0:T(8,128)(2,1)S(1)}, u32[]{:S(2)}, u32[]{:S(2)}) collective-permute-start(bf16[160,2048]{1,0:T(8,128)(2,1)S(1)} %get-tuple-element.246.refs_0_), channel_id=1, source_target_pairs={{0,2},{1,3},{2,0},{3,1},{4,6},{5,7},{6,4},{7,5},{8,10},{9,11},{10,... | collective-permute-start | bytes 1966088 | tf_op jit(solution)/shard_map/ppermute | solution.py:22
  260.1 23.2 %collective-permute-start.47 = (bf16[160,2048]{1,0:T(8,128)(2,1)S(1)}, bf16[160,2048]{1,0:T(8,128)(2,1)S(1)}, u32[]{:S(2)}, u32[]{:S(2)}) collective-permute-start(bf16[160,2048]{1,0:T(8,128)(2,1)S(1)} %get-tuple-element.246.refs_0_), channel_id=1, source_target_pairs={{0,1},{1,0},{2,3},{3,2},{4,5},{5,4},{6,7},{7,6},{8,9},{9,8},{10,11... | collective-permute-start | bytes 1966088 | tf_op jit(solution)/shard_map/ppermute | solution.py:22
  260.7 27.1 %collective-permute-start.45 = (bf16[2,144,768]{2,1,0:T(8,128)(2,1)S(1)}, bf16[2,144,768]{2,1,0:T(8,128)(2,1)S(1)}, u32[]{:S(2)}, u32[]{:S(2)}) collective-permute-start(bf16[2,144,768]{2,1,0:T(8,128)(2,1)S(1)} %get-tuple-element.245.refs_0_), channel_id=1, source_target_pairs={{0,4},{1,5},{2,6},{3,7},{4,0},{5,1},{6,2},{7,3},{8,12},{9,13},{10,... | collective-permute-start | bytes 1327112 | tf_op jit(solution)/shard_map/ppermute | solution.py:22
  (78 other events, 936.2 us)

commit v5 on v4

--- a/solution.py
+++ b/solution.py
@@ -46,7 +46,7 @@
 EVERY = range(100)
 TOKEN = (8, 128)
 COSTS = {'': (3000000000, 10000000000), 'grad_in': (10000000000, 1000000), 'grad_qkv': (10000000000, 1000000), 'attention_back': (10000000000, 1000000), 'feed': (100000000000, 1000000), 'tokens_back': (100000000000, 1000000), 'project': (1000000000, 1000000000), 'own_keys': (1000000000, 1000000000), 'cached_keys': (1000000000, 1000000000), 'bank_columns': (1000000000, 1000000000), 'cross': (1000000000, 1000000000), 'join': (1000000000, 1000000000), 'copy': (1000000000, 1000000000), 'choose_banks': (1000000000, 1000000000), 'grad_down': (3000000000, 10000000000)}
-PLAN = "ABNWYdqidiqdqtitiqFtHqG"
+PLAN = "ABNWYdqidiqdqtitiqFtqiHqG"
 
 
 def cost_of(name):
@@ -558,25 +558,31 @@
 
 
 def qkv_finish_kernel(blocks, halved, sc, *refs):
-    parts, (grad_qkv, sums, held) = refs[:4], refs[4:]
-    half, _, part = parts[0].shape
-    share = grad_qkv.shape[0]
+    parts, grad_qkv, sums = refs[:4], refs[4], refs[5:]
+    half, high, wide = parts[0].shape
+    share, width = grad_qkv.shape[0], grad_qkv.shape[1] // 3
+    part = wide // 3
     core, low = sc[1], sc[sc.shape[0] - 1]
-    mine = (pl.program_id(0) == core) if halved else True
-    for i in range(4):
-        for j in range(half):
-            held[i // 2, (low ^ (i % 2)) * half + j] = parts[i][j].astype(F32)
-    for mask in range(blocks):
-        columns = pl.ds(pl.multiple_of((sc[0] ^ mask) * part, part), part)
-        grad_qkv[:, columns] = jnp.where(mine, held[0, mask, :share], held[1, mask, :share])
-
-    @pl.when((pl.program_id(0) == 0) & (pl.program_id(1) == 0))
+    for i in range(4 if halved else 2):
+
+        @pl.when(pl.program_id(0) == ((core ^ (i // 2)) if halved else 0))
+        def _():
+            for j in range(half):
+                mask = (low ^ (i % 2)) * half + j
+                for k in range(3):
+                    first = k * width + (sc[0] ^ mask) * part
+                    columns = pl.ds(pl.multiple_of(first, part), part)
+                    piece = parts[i][j, :share, k * part : (k + 1) * part]
+                    grad_qkv[:, columns] = piece.astype(F32)
+
+    @pl.when(pl.program_id(0) == 0)
     def _():
-        total = jnp.zeros((8, part), F32)
-        for i in range(2 if halved else 1):
-            for mask in range(blocks):
-                total = total + held[i, mask, share : share + 8]
-        sums[...] = total
+        total = jnp.zeros((high - share, part), F32)
+        for i in range(4 if halved else 2):
+            for j in range(half):
+                total = total + parts[i][j, share:, :part].astype(F32)
+        for i, out in enumerate(sums):
+            out[...] = total[i]
 
 
 def tokens_kernel(blocks, sc, tokens, grad_res, gains, *refs):
@@ -1139,7 +1145,7 @@
             shape = first[1]
         return order.small(sum_kernel, "sum", items, [shape])[0]
 
-    def sum_chips(mine, other):
+    def sum_chips(mine, other, late=True):
         came = swap(other, "grp", 2)
         yield
         held = total(mine, came)
@@ -1148,7 +1154,11 @@
             yield
             held = total(held, came)
         other = swap(held, "grp", 2)
-        return held, other, swap(held, "grp", 1), swap(other, "grp", 1)
+        core_held = swap(held, "grp", 1)
+        if late:
+            yield
+            other = order.copy(other)
+        return held, other, core_held, swap(other, "grp", 1)
 
     def back_path():
         found = order.call(
@@ -1258,7 +1268,7 @@
         mine, other = order.small(
             functools.partial(split_sum_kernel, 2), "split", items, [block] * 2
         )
-        return (yield from sum_chips(mine, other))
+        return (yield from sum_chips(mine, other, False))
 
     share = part // 2 if halved else part
     share_block = (1, share + 16, 3 * part), lambda m, sc: (m, 0, 0)
@@ -1360,17 +1370,14 @@
         yield
 
     def qkv_finish():
-        high = share + 16
         return order.call(
             functools.partial(qkv_finish_kernel, blocks, halved),
             "qkv_finish",
-            (2 if halved else 1, 3),
-            [(a, (blocks // 2, high, part), lambda k, i, sc: (0, 0, i)) for a in results["q"]],
-            [
-                ((part, 3 * width), F32, (share, width), lambda k, i, sc: (k, i)),
-                ((8, part), F32),
-            ],
-            [pltpu.VMEM((2, blocks, high, part), F32)],
+            (2 if halved else 1,),
+            list(results["q"]),
+            [((part, 3 * width), F32, (share, 3 * width), lambda k, sc: (k, 0))]
+            + [((part,), F32)] * 4,
+            [],
             16,
         )
         yield
@@ -1396,7 +1403,7 @@
             if needs is None or needs in results:
                 go(name)
     (grad_down,) = results["F"]
-    grad_qkv, sums = results["G"]
+    grad_qkv, *sums = results["G"]
     grad_in, grad_out = results["H"]
     (grad_tokens,) = results["t"]
     return (

time: 308 us -> 300 us (0.974)
  waiting for transfers between devices: 122 us -> 115 us
    ppermute x52, waiting for transfers between devices: 122 us -> 115 us  [swap(): return lax.ppermute(values, axis, [(i, i ^ mask) for i in range(size)])]
    pallas_call x31 -> x33, Pallas kernels: 101 us -> 101 us  [call(): pl.pallas_call(body, grid_spec=spec, out_shape=out_shapes, compiler_param...]
  transfers between devices with their start and end apart: 52 -> 52, of which waited for: 26 -> 29; matrix products, arithmetic and copies ran while one was open for 0% -> 0% of each run, Pallas kernels for 23% -> 24%
where the time goes in v5:
time: 300 us
  waiting for transfers between devices  115 us (38%)
  Pallas kernels  105 us (35%)
  starting transfers between devices  70.1 us (23%)
  local copies, waits for them, and re-layouts  7.41 us (2%)
    ppermute x52, waiting for transfers between devices, swap(): return lax.ppermute(values, axis, [(i, i ^ mask) for i in range(size)])  115 us
    pallas_call x33, Pallas kernels, call(): pl.pallas_call(body, grid_spec=spec, out_shape=out_shapes, compiler_param...  101 us
    ppermute x52, starting transfers between devices, swap(): return lax.ppermute(values, axis, [(i, i ^ mask) for i in range(size)])  70.1 us
    unnamed x100, local copies, waits for them, and re-layouts  7.39 us
  transfers between devices with their start and end apart: 52, of which 29 were waited for; matrix products, arithmetic and copies ran while one was open for 0% of the time, Pallas kernels for 24%

profile of v5, /device:TPU:0, one launch (start us, length us, event | category | flops | bytes accessed | tf_op | source)
XLA Modules:
  0.0 299.8 jit_solution(7582364655007172788)
XLA Ops:
  13.0 6.2 %collective-permute-done.1.refs_3_ = bf16[2,2,128,256]{3,2,1,0:T(8,128)(2,1)S(1)} collective-permute-done((bf16[2,2,128,256]{3,2,1,0:T(8,128)(2,1)S(1)}, bf16[2,2,128,256]{3,2,1,0:T(8,128)(2,1)S(1)}, u32[]{:S(2)}, u32[]{:S(2)}) %collective-permute-start.1) | collective-permute-done | bytes 262176 | tf_op jit(solution)/shard_map/ppermute | solution.py:22
  28.1 17.5 %collective-permute-done.5.refs_1_.refs_2_.refs_6_ = bf16[2,256,1024]{2,1,0:T(8,128)(2,1)S(1)} collective-permute-done((bf16[2,256,1024]{2,1,0:T(8,128)(2,1)}, bf16[2,256,1024]{2,1,0:T(8,128)(2,1)S(1)}, u32[]{:S(2)}, u32[]{:S(2)}) %collective-permute-start.5) | collective-permute-done | bytes 1048608 | tf_op jit(solution)/shard_map/ppermute | solution.py:22
  57.7 4.7 %project.2 = (bf16[256,1024]{1,0:T(8,128)(2,1)}, bf16[256,768]{1,0:T(8,128)(2,1)S(1)}, bf16[256,1024]{1,0:T(8,128)(2,1)}, bf16[256,768]{1,0:T(8,128)(2,1)S(1)}, ...) custom-call(s32[7]{0:T(128)S(1)} %copy-done.12, ...), custom_call_target="tpu_custom_call" | custom-call | flops 1000000000 | bytes 1000000000 | tf_op jit(solution)/shard_map/project/pallas_call | solution.py:116
  66.8 6.1 %own_keys.1 = (bf16[2,512,256]{2,1,0:T(8,128)(2,1)S(1)}, bf16[2,512,256]{2,1,0:T(8,128)(2,1)S(1)}, bf16[2,512,256]{2,1,0:T(8,128)(2,1)}, f32[2,512,256]{2,1,0:T(...) custom-call(s32[7]{0:T(128)S(1)} %copy-done.12, bf16[2,128,768]{2,1,0:T(8,128)(2,1)S(1)} %bitcast.22, ...), custom_call_target="tpu_custom_call" | custom-call | flops 1000000000 | bytes 1000000000 | tf_op jit(solution)/shard_map/own_keys/pallas_call | solution.py:116
  76.2 6.5 %cached_keys.1 = (f32[2,512,256]{2,1,0:T(8,128)}, f32[2,512,256]{2,1,0:T(8,128)}, bf16[2,128,256]{2,1,0:T(8,128)(2,1)S(1)}, bf16[2,128,256]{2,1,0:T(8,128)(2,1)S...) custom-call(s32[7]{0:T(128)S(1)} %copy-done.12, ...), custom_call_target="tpu_custom_call" | custom-call | flops 1000000000 | bytes 1000000000 | tf_op jit(solution)/shard_map/cached_keys/pallas_call | solution.py:116
  89.8 20.2 %feed.1 = (bf16[256,1024]{1,0:T(8,128)(2,1)}, f32[256,1024]{1,0:T(8,128)}, bf16[256,2048]{1,0:T(8,128)(2,1)}, bf16[256,4608]{1,0:T(8,128)(2,1)S(1)}, bf16[256,10...) custom-call(s32[7]{0:T(128)S(1)} %copy-done.12, ...), custom_call_target="tpu_custom_call" | custom-call | flops 99999997952 | bytes 1000000 | tf_op jit(solution)/shard_map/feed/pallas_call | solution.py:116
  126.5 13.9 %attention_back.1 = (bf16[3,2,128,256]{3,2,1,0:T(8,128)(2,1)S(1)}, bf16[3,2,128,256]{3,2,1,0:T(8,128)(2,1)S(1)}, bf16[3,2,128,256]{3,2,1,0:T(8,128)(2,1)S(1)}, b...) custom-call(s32[7]{0:T(128)S(1)} %copy-done.12, bf16[2,512,256]{2,1,0:T(8,128)(2,1)} %copy-done.4, ...), custom_call_target="tpu_custom_call" | custom-call | flops 10000000000 | bytes 1000000 | tf_op jit(solution)/shard_map/attention_back/pallas_call | solution.py:116
  140.6 6.3 %grad_in.1 = (bf16[2,160,2048]{2,1,0:T(8,128)(2,1)S(1)}, bf16[2,160,2048]{2,1,0:T(8,128)(2,1)S(1)}, bf16[2,160,2048]{2,1,0:T(8,128)(2,1)S(1)}, bf16[2,160,2048]{2,1,0:T(8,128)(2,1)S(1)}, s32[8,128]{1,0:T(8,128)S(1)}) custom-call(s32[7]{0:T(128)S(1)} %copy-done.12, bf16[256,1024]{1,0:T(8,128)(2,1)S(1)} %copy-done.27, ...), custom_call_target="tpu_custom_call" | custom-call | flops 10000000000 | bytes 1000000 | tf_op jit(solution)/shard_map/grad_in/pallas_call | solution.py:116
  152.8 5.7 %grad_qkv.1 = (bf16[4,144,768]{2,1,0:T(8,128)(2,1)S(1)}, bf16[4,144,768]{2,1,0:T(8,128)(2,1)S(1)}, s32[8,128]{1,0:T(8,128)S(1)}) custom-call(s32[7]{0:T(128)S(1)} %copy-done.12, bf16[256,1024]{1,0:T(8,128)(2,1)} %get-tuple-element.195.refs_0_, bf16[256,1024]{1,0:T(8,128)(2,1)} %get-tuple-element.196.refs_1_, bf16[256,1024]{1,0:T(8,128)(2,1)} %get-tuple-element.197.refs_2_, ...), custom_call_target="tpu_custom_call" | custom-call | flops 10000000000 | bytes 1000000 | tf_op jit(solution)/shard_map/grad_qkv/pallas_call | solution.py:116
  159.9 5.6 %collective-permute-start.34 = (bf16[256,1024]{1,0:T(8,128)(2,1)S(1)}, bf16[256,1024]{1,0:T(8,128)(2,1)S(1)}, u32[]{:S(2)}, u32[]{:S(2)}) collective-permute-start(bf16[256,1024]{1,0:T(8,128)(2,1)S(1)} %get-tuple-element.228), channel_id=1, source_target_pairs={{0,2},{1,3},{2,0},{3,1},{4,6},{5,7},{6,4},{7,5},{8,10},{9,11},{10,... | collective-permute-start | bytes 1572872 | tf_op jit(solution)/shard_map/ppermute | solution.py:22
  166.2 9.5 %collective-permute-done.30.refs_1_ = bf16[2,160,2048]{2,1,0:T(8,128)(2,1)S(1)} collective-permute-done((bf16[2,160,2048]{2,1,0:T(8,128)(2,1)S(1)}, bf16[2,160,2048]{2,1,0:T(8,128)(2,1)S(1)}, u32[]{:S(2)}, u32[]{:S(2)}) %collective-permute-start.30) | collective-permute-done | bytes 1310752 | tf_op jit(solution)/shard_map/ppermute | solution.py:22
  181.5 6.8 %collective-permute-start.36 = (bf16[256,1024]{1,0:T(8,128)(2,1)S(1)}, bf16[256,1024]{1,0:T(8,128)(2,1)S(1)}, u32[]{:S(2)}, u32[]{:S(2)}) collective-permute-start(bf16[256,1024]{1,0:T(8,128)(2,1)S(1)} %get-tuple-element.233.refs_0_), channel_id=1, source_target_pairs={{0,4},{1,5},{2,6},{3,7},{4,0},{5,1},{6,2},{7,3},{8,12},{9,13},{10,... | collective-permute-start | bytes 1572872 | tf_op jit(solution)/shard_map/ppermute | solution.py:22
  188.3 4.0 %collective-permute-done.32.refs_2_ = bf16[160,2048]{1,0:T(8,128)(2,1)S(1)} collective-permute-done((bf16[160,2048]{1,0:T(8,128)(2,1)S(1)}, bf16[160,2048]{1,0:T(8,128)(2,1)S(1)}, u32[]{:S(2)}, u32[]{:S(2)}) %collective-permute-start.32) | collective-permute-done | bytes 655392 | tf_op jit(solution)/shard_map/ppermute | solution.py:22
  192.3 4.1 %collective-permute-done.33.refs_5_ = bf16[160,2048]{1,0:T(8,128)(2,1)S(1)} collective-permute-done((bf16[160,2048]{1,0:T(8,128)(2,1)S(1)}, bf16[160,2048]{1,0:T(8,128)(2,1)S(1)}, u32[]{:S(2)}, u32[]{:S(2)}) %collective-permute-start.33) | collective-permute-done | bytes 655392 | tf_op jit(solution)/shard_map/ppermute | solution.py:22
  197.6 4.5 %collective-permute-done.29.refs_1_ = bf16[2,144,768]{2,1,0:T(8,128)(2,1)S(1)} collective-permute-done((bf16[2,144,768]{2,1,0:T(8,128)(2,1)S(1)}, bf16[2,144,768]{2,1,0:T(8,128)(2,1)S(1)}, u32[]{:S(2)}, u32[]{:S(2)}) %collective-permute-start.29) | collective-permute-done | bytes 442400 | tf_op jit(solution)/shard_map/ppermute | solution.py:22
  204.2 5.4 %collective-permute-start.38 = (bf16[160,2048]{1,0:T(8,128)(2,1)S(1)}, bf16[160,2048]{1,0:T(8,128)(2,1)S(1)}, u32[]{:S(2)}, u32[]{:S(2)}) collective-permute-start(bf16[160,2048]{1,0:T(8,128)(2,1)S(1)} %get-tuple-element.239), channel_id=1, source_target_pairs={{0,2},{1,3},{2,0},{3,1},{4,6},{5,7},{6,4},{7,5},{8,10},{9,11},{10,... | collective-permute-start | bytes 1966088 | tf_op jit(solution)/shard_map/ppermute | solution.py:22
  213.5 5.4 %collective-permute-start.40 = (bf16[256,1024]{1,0:T(8,128)(2,1)S(1)}, bf16[256,1024]{1,0:T(8,128)(2,1)S(1)}, u32[]{:S(2)}, u32[]{:S(2)}) collective-permute-start(bf16[256,1024]{1,0:T(8,128)(2,1)S(1)} %get-tuple-element.243.refs_0_), channel_id=1, source_target_pairs={{0,2},{1,3},{2,0},{3,1},{4,6},{5,7},{6,4},{7,5},{8,10},{9,11},{10,... | collective-permute-start | bytes 1572872 | tf_op jit(solution)/shard_map/ppermute | solution.py:22
  218.9 12.7 %collective-permute-done.38.refs_1_ = bf16[160,2048]{1,0:T(8,128)(2,1)S(1)} collective-permute-done((bf16[160,2048]{1,0:T(8,128)(2,1)S(1)}, bf16[160,2048]{1,0:T(8,128)(2,1)S(1)}, u32[]{:S(2)}, u32[]{:S(2)}) %collective-permute-start.38) | collective-permute-done | bytes 655392 | tf_op jit(solution)/shard_map/ppermute | solution.py:22
  236.1 9.9 %collective-permute-done.40.refs_1_ = bf16[256,1024]{1,0:T(8,128)(2,1)S(1)} collective-permute-done((bf16[256,1024]{1,0:T(8,128)(2,1)S(1)}, bf16[256,1024]{1,0:T(8,128)(2,1)S(1)}, u32[]{:S(2)}, u32[]{:S(2)}) %collective-permute-start.40) | collective-permute-done | bytes 524320 | tf_op jit(solution)/shard_map/ppermute | solution.py:22
  247.6 6.6 %collective-permute-done.44.refs_1_ = bf16[160,2048]{1,0:T(8,128)(2,1)S(1)} collective-permute-done((bf16[160,2048]{1,0:T(8,128)(2,1)S(1)}, bf16[160,2048]{1,0:T(8,128)(2,1)S(1)}, u32[]{:S(2)}, u32[]{:S(2)}) %collective-permute-start.44) | collective-permute-done | bytes 655392 | tf_op jit(solution)/shard_map/ppermute | solution.py:22
  266.7 5.4 %tokens_back.1 = (f32[256,1024]{1,0:T(8,128)}, s32[8,128]{1,0:T(8,128)S(1)}) custom-call(s32[7]{0:T(128)S(1)} %copy-done.12, bf16[256,1024]{1,0:T(8,128)(2,1)S(1)} %bitcast.42, f32[256,1024]{1,0:T(8,128)S(1)} %copy-done.33, bf16[4,1024]{1,0:T(4,128)(2,1)S(1)} %copy-done.10, bf16[3,256,256]{2,1,0:T(8,128)(2,1)S(1)} %bitcast.48, ...), custom_call_target="tpu_custom_call" | custom-call | flops 99999997952 | bytes 1000000 | tf_op jit(solution)/shard_map/tokens_back/pallas_call | solution.py:116
  272.0 7.4 %collective-permute-done.45.refs_1_ = bf16[2,144,768]{2,1,0:T(8,128)(2,1)S(1)} collective-permute-done((bf16[2,144,768]{2,1,0:T(8,128)(2,1)S(1)}, bf16[2,144,768]{2,1,0:T(8,128)(2,1)S(1)}, u32[]{:S(2)}, u32[]{:S(2)}) %collective-permute-start.45) | collective-permute-done | bytes 442400 | tf_op jit(solution)/shard_map/ppermute | solution.py:22
  284.4 4.6 %in_finish.1 = (f32[256,4096]{1,0:T(8,128)}, f32[256,1024]{1,0:T(8,128)}, s32[8,128]{1,0:T(8,128)S(1)}) custom-call(s32[7]{0:T(128)S(1)} %copy-done.12, bf16[160,2048]{1,0:T(8,128)(2,1)S(1)} %get-tuple-element.255.refs_0_, bf16[160,2048]{1,0:T(8,128)(2,1)S(1)} %get-tuple-element.257.refs_1_, bf16[160,2048]{1,0:T(8,128)(2,1)S(1)} %collective-permute-done.48.refs_2_, ...), custom_call_target="tpu_custom_call" | custom-call | flops 3000000000 | bytes 10000000000 | tf_op jit(solution)/shard_map/in_finish/pallas_call | solution.py:116
  289.0 5.9 %collective-permute-done.46.refs_0_ = bf16[2,144,768]{2,1,0:T(8,128)(2,1)S(1)} collective-permute-done((bf16[2,144,768]{2,1,0:T(8,128)(2,1)S(1)}, bf16[2,144,768]{2,1,0:T(8,128)(2,1)S(1)}, u32[]{:S(2)}, u32[]{:S(2)}) %collective-permute-start.46) | collective-permute-done | bytes 442400 | tf_op jit(solution)/shard_map/ppermute | solution.py:22
  (225 shorter events, 113.3 us)
Async XLA Ops:
  21.6 24.0 %collective-permute-start.5 = (bf16[2,256,1024]{2,1,0:T(8,128)(2,1)}, bf16[2,256,1024]{2,1,0:T(8,128)(2,1)S(1)}, u32[]{:S(2)}, u32[]{:S(2)}) collective-permute-start(bf16[2,256,1024]{2,1,0:T(8,128)(2,1)} %get-tuple-element.148.refs_0_.refs_4_), channel_id=1, source_target_pairs={{0,16},{8,24},{16,0},{24,8},{1,17},{9,25},{17,1},{25,9},{2,18},{10... | collective-permute-start | bytes 3145736 | tf_op jit(solution)/shard_map/ppermute | solution.py:22
  23.2 22.7 %collective-permute-start.4 = (bf16[2,256,1024]{2,1,0:T(8,128)(2,1)}, bf16[2,256,1024]{2,1,0:T(8,128)(2,1)S(1)}, u32[]{:S(2)}, u32[]{:S(2)}) collective-permute-start(bf16[2,256,1024]{2,1,0:T(8,128)(2,1)} %get-tuple-element.148.refs_0_.refs_4_), channel_id=1, source_target_pairs={{0,8},{8,0},{16,24},{24,16},{1,9},{9,1},{17,25},{25,17},{2,10},{10... | collective-permute-start | bytes 3145736 | tf_op jit(solution)/shard_map/ppermute | solution.py:22
  23.7 26.5 %collective-permute-start.6 = (bf16[2,2,128,256]{3,2,1,0:T(8,128)(2,1)}, bf16[2,2,128,256]{3,2,1,0:T(8,128)(2,1)S(1)}, u32[]{:S(2)}, u32[]{:S(2)}) collective-permute-start(bf16[2,2,128,256]{3,2,1,0:T(8,128)(2,1)} %copy-done.40), channel_id=1, source_target_pairs={{0,2},{1,3},{2,0},{3,1},{4,6},{5,7},{6,4},{7,5},{8,10},{9,11},{10,... | collective-permute-start | bytes 786440 | tf_op jit(solution)/shard_map/ppermute | solution.py:22
  25.3 24.9 %collective-permute-start.7 = (bf16[2,2,128,256]{3,2,1,0:T(8,128)(2,1)}, bf16[2,2,128,256]{3,2,1,0:T(8,128)(2,1)S(1)}, u32[]{:S(2)}, u32[]{:S(2)}) collective-permute-start(bf16[2,2,128,256]{3,2,1,0:T(8,128)(2,1)} %copy-done.39), channel_id=1, source_target_pairs={{0,4},{1,5},{2,6},{3,7},{4,0},{5,1},{6,2},{7,3},{8,12},{9,13},{10,... | collective-permute-start | bytes 786440 | tf_op jit(solution)/shard_map/ppermute | solution.py:22
  27.9 22.8 %collective-permute-start.8 = (bf16[2,2,128,256]{3,2,1,0:T(8,128)(2,1)}, bf16[2,2,128,256]{3,2,1,0:T(8,128)(2,1)S(1)}, u32[]{:S(2)}, u32[]{:S(2)}) collective-permute-start(bf16[2,2,128,256]{3,2,1,0:T(8,128)(2,1)} %copy-done.38), channel_id=1, source_target_pairs={{0,6},{1,7},{2,4},{3,5},{4,2},{5,3},{6,0},{7,1},{8,14},{9,15},{10,... | collective-permute-start | bytes 786440 | tf_op jit(solution)/shard_map/ppermute | solution.py:22
  54.9 21.3 %collective-permute-start.15 = (bf16[2,2,128,256]{3,2,1,0:T(8,128)(2,1)S(1)}, bf16[2,2,128,256]{3,2,1,0:T(8,128)(2,1)S(1)}, u32[]{:S(2)}, u32[]{:S(2)}) collective-permute-start(bf16[2,2,128,256]{3,2,1,0:T(8,128)(2,1)S(1)} %get-tuple-element.169), channel_id=1, source_target_pairs={{0,4},{1,5},{2,6},{3,7},{4,0},{5,1},{6,2},{7,3},{8,12},{9,13},{10,... | collective-permute-start | bytes 786440 | tf_op jit(solution)/shard_map/ppermute | solution.py:22
  122.4 26.5 %collective-permute-start.24 = (bf16[256,1024]{1,0:T(8,128)(2,1)}, bf16[256,1024]{1,0:T(8,128)(2,1)S(1)}, u32[]{:S(2)}, u32[]{:S(2)}) collective-permute-start(bf16[256,1024]{1,0:T(8,128)(2,1)} %get-tuple-element.202), channel_id=1, source_target_pairs={{0,8},{8,0},{16,24},{24,16},{1,9},{9,1},{17,25},{25,17},{2,10},{10... | collective-permute-start | bytes 1572872 | tf_op jit(solution)/shard_map/ppermute | solution.py:22
  123.4 25.5 %collective-permute-start.25 = (bf16[256,1024]{1,0:T(8,128)(2,1)}, bf16[256,1024]{1,0:T(8,128)(2,1)S(1)}, u32[]{:S(2)}, u32[]{:S(2)}) collective-permute-start(bf16[256,1024]{1,0:T(8,128)(2,1)} %get-tuple-element.203), channel_id=1, source_target_pairs={{0,16},{8,24},{16,0},{24,8},{1,17},{9,25},{17,1},{25,9},{2,18},{10... | collective-permute-start | bytes 1572872 | tf_op jit(solution)/shard_map/ppermute | solution.py:22
  124.3 24.6 %collective-permute-start.26 = (bf16[256,1024]{1,0:T(8,128)(2,1)}, bf16[256,1024]{1,0:T(8,128)(2,1)S(1)}, u32[]{:S(2)}, u32[]{:S(2)}) collective-permute-start(bf16[256,1024]{1,0:T(8,128)(2,1)} %get-tuple-element.204), channel_id=1, source_target_pairs={{0,24},{8,16},{16,8},{24,0},{1,25},{9,17},{17,9},{25,1},{2,26},{10... | collective-permute-start | bytes 1572872 | tf_op jit(solution)/shard_map/ppermute | solution.py:22
  146.8 28.9 %collective-permute-start.30 = (bf16[2,160,2048]{2,1,0:T(8,128)(2,1)S(1)}, bf16[2,160,2048]{2,1,0:T(8,128)(2,1)S(1)}, u32[]{:S(2)}, u32[]{:S(2)}) collective-permute-start(bf16[2,160,2048]{2,1,0:T(8,128)(2,1)S(1)} %get-tuple-element.221), channel_id=1, source_target_pairs={{0,8},{8,0},{16,24},{24,16},{1,9},{9,1},{17,25},{25,17},{2,10},{10... | collective-permute-start | bytes 3932168 | tf_op jit(solution)/shard_map/ppermute | solution.py:22
  147.9 29.2 %collective-permute-start.31 = (bf16[2,160,2048]{2,1,0:T(8,128)(2,1)S(1)}, bf16[2,160,2048]{2,1,0:T(8,128)(2,1)S(1)}, u32[]{:S(2)}, u32[]{:S(2)}) collective-permute-start(bf16[2,160,2048]{2,1,0:T(8,128)(2,1)S(1)} %get-tuple-element.223), channel_id=1, source_target_pairs={{0,16},{8,24},{16,0},{24,8},{1,17},{9,25},{17,1},{25,9},{2,18},{10... | collective-permute-start | bytes 3932168 | tf_op jit(solution)/shard_map/ppermute | solution.py:22
  159.9 20.9 %collective-permute-start.34 = (bf16[256,1024]{1,0:T(8,128)(2,1)S(1)}, bf16[256,1024]{1,0:T(8,128)(2,1)S(1)}, u32[]{:S(2)}, u32[]{:S(2)}) collective-permute-start(bf16[256,1024]{1,0:T(8,128)(2,1)S(1)} %get-tuple-element.228), channel_id=1, source_target_pairs={{0,2},{1,3},{2,0},{3,1},{4,6},{5,7},{6,4},{7,5},{8,10},{9,11},{10,... | collective-permute-start | bytes 1572872 | tf_op jit(solution)/shard_map/ppermute | solution.py:22
  180.1 21.9 %collective-permute-start.29 = (bf16[2,144,768]{2,1,0:T(8,128)(2,1)S(1)}, bf16[2,144,768]{2,1,0:T(8,128)(2,1)S(1)}, u32[]{:S(2)}, u32[]{:S(2)}) collective-permute-start(bf16[2,144,768]{2,1,0:T(8,128)(2,1)S(1)} %get-tuple-element.219), channel_id=1, source_target_pairs={{0,8},{8,0},{16,24},{24,16},{1,9},{9,1},{17,25},{25,17},{2,10},{10... | collective-permute-start | bytes 1327112 | tf_op jit(solution)/shard_map/ppermute | solution.py:22
  181.5 28.1 %collective-permute-start.36 = (bf16[256,1024]{1,0:T(8,128)(2,1)S(1)}, bf16[256,1024]{1,0:T(8,128)(2,1)S(1)}, u32[]{:S(2)}, u32[]{:S(2)}) collective-permute-start(bf16[256,1024]{1,0:T(8,128)(2,1)S(1)} %get-tuple-element.233.refs_0_), channel_id=1, source_target_pairs={{0,4},{1,5},{2,6},{3,7},{4,0},{5,1},{6,2},{7,3},{8,12},{9,13},{10,... | collective-permute-start | bytes 1572872 | tf_op jit(solution)/shard_map/ppermute | solution.py:22
  204.2 27.4 %collective-permute-start.38 = (bf16[160,2048]{1,0:T(8,128)(2,1)S(1)}, bf16[160,2048]{1,0:T(8,128)(2,1)S(1)}, u32[]{:S(2)}, u32[]{:S(2)}) collective-permute-start(bf16[160,2048]{1,0:T(8,128)(2,1)S(1)} %get-tuple-element.239), channel_id=1, source_target_pairs={{0,2},{1,3},{2,0},{3,1},{4,6},{5,7},{6,4},{7,5},{8,10},{9,11},{10,... | collective-permute-start | bytes 1966088 | tf_op jit(solution)/shard_map/ppermute | solution.py:22
  212.2 33.8 %collective-permute-start.37 = (bf16[2,3,256,256]{3,2,1,0:T(8,128)(2,1)S(1)}, bf16[2,3,256,256]{3,2,1,0:T(8,128)(2,1)S(1)}, u32[]{:S(2)}, u32[]{:S(2)}) collective-permute-start(bf16[2,3,256,256]{3,2,1,0:T(8,128)(2,1)S(1)} %get-tuple-element.237), channel_id=1, source_target_pairs={{0,8},{8,0},{16,24},{24,16},{1,9},{9,1},{17,25},{25,17},{2,10},{10... | collective-permute-start | bytes 2359304 | tf_op jit(solution)/shard_map/ppermute | solution.py:22
  213.5 32.5 %collective-permute-start.40 = (bf16[256,1024]{1,0:T(8,128)(2,1)S(1)}, bf16[256,1024]{1,0:T(8,128)(2,1)S(1)}, u32[]{:S(2)}, u32[]{:S(2)}) collective-permute-start(bf16[256,1024]{1,0:T(8,128)(2,1)S(1)} %get-tuple-element.243.refs_0_), channel_id=1, source_target_pairs={{0,2},{1,3},{2,0},{3,1},{4,6},{5,7},{6,4},{7,5},{8,10},{9,11},{10,... | collective-permute-start | bytes 1572872 | tf_op jit(solution)/shard_map/ppermute | solution.py:22
  232.3 21.9 %collective-permute-start.44 = (bf16[160,2048]{1,0:T(8,128)(2,1)S(1)}, bf16[160,2048]{1,0:T(8,128)(2,1)S(1)}, u32[]{:S(2)}, u32[]{:S(2)}) collective-permute-start(bf16[160,2048]{1,0:T(8,128)(2,1)S(1)} %get-tuple-element.246.refs_0_), channel_id=1, source_target_pairs={{0,4},{1,5},{2,6},{3,7},{4,0},{5,1},{6,2},{7,3},{8,12},{9,13},{10,... | collective-permute-start | bytes 1966088 | tf_op jit(solution)/shard_map/ppermute | solution.py:22
  233.6 24.3 %collective-permute-start.41 = (bf16[256,1024]{1,0:T(8,128)(2,1)S(1)}, bf16[256,1024]{1,0:T(8,128)(2,1)S(1)}, u32[]{:S(2)}, u32[]{:S(2)}) collective-permute-start(bf16[256,1024]{1,0:T(8,128)(2,1)S(1)} %get-tuple-element.243.refs_0_), channel_id=1, source_target_pairs={{0,1},{1,0},{2,3},{3,2},{4,5},{5,4},{6,7},{7,6},{8,9},{9,8},{10,11... | collective-permute-start | bytes 1572872 | tf_op jit(solution)/shard_map/ppermute | solution.py:22
  233.6 23.6 %collective-permute-start.43 = (bf16[2,144,768]{2,1,0:T(8,128)(2,1)S(1)}, bf16[2,144,768]{2,1,0:T(8,128)(2,1)S(1)}, u32[]{:S(2)}, u32[]{:S(2)}) collective-permute-start(bf16[2,144,768]{2,1,0:T(8,128)(2,1)S(1)} %get-tuple-element.245), channel_id=1, source_target_pairs={{0,2},{1,3},{2,0},{3,1},{4,6},{5,7},{6,4},{7,5},{8,10},{9,11},{10,... | collective-permute-start | bytes 1327112 | tf_op jit(solution)/shard_map/ppermute | solution.py:22
  246.6 20.0 %collective-permute-start.39 = (bf16[2,3,256,256]{3,2,1,0:T(8,128)(2,1)S(1)}, bf16[2,3,256,256]{3,2,1,0:T(8,128)(2,1)S(1)}, u32[]{:S(2)}, u32[]{:S(2)}) collective-permute-start(bf16[2,3,256,256]{3,2,1,0:T(8,128)(2,1)S(1)} %get-tuple-element.242), channel_id=1, source_target_pairs={{0,16},{8,24},{16,0},{24,8},{1,17},{9,25},{17,1},{25,9},{2,18},{10... | collective-permute-start | bytes 2359304 | tf_op jit(solution)/shard_map/ppermute | solution.py:22
  254.9 29.3 %collective-permute-start.48 = (bf16[160,2048]{1,0:T(8,128)(2,1)S(1)}, bf16[160,2048]{1,0:T(8,128)(2,1)S(1)}, u32[]{:S(2)}, u32[]{:S(2)}) collective-permute-start(bf16[160,2048]{1,0:T(8,128)(2,1)S(1)} %get-tuple-element.255.refs_0_), channel_id=1, source_target_pairs={{0,1},{1,0},{2,3},{3,2},{4,5},{5,4},{6,7},{7,6},{8,9},{9,8},{10,11... | collective-permute-start | bytes 1966088 | tf_op jit(solution)/shard_map/ppermute | solution.py:22
  257.2 24.4 %collective-permute-start.47 = (bf16[160,2048]{1,0:T(8,128)(2,1)S(1)}, bf16[160,2048]{1,0:T(8,128)(2,1)S(1)}, u32[]{:S(2)}, u32[]{:S(2)}) collective-permute-start(bf16[160,2048]{1,0:T(8,128)(2,1)S(1)} %get-tuple-element.255.refs_0_), channel_id=1, source_target_pairs={{0,2},{1,3},{2,0},{3,1},{4,6},{5,7},{6,4},{7,5},{8,10},{9,11},{10,... | collective-permute-start | bytes 1966088 | tf_op jit(solution)/shard_map/ppermute | solution.py:22
  257.9 21.5 %collective-permute-start.45 = (bf16[2,144,768]{2,1,0:T(8,128)(2,1)S(1)}, bf16[2,144,768]{2,1,0:T(8,128)(2,1)S(1)}, u32[]{:S(2)}, u32[]{:S(2)}) collective-permute-start(bf16[2,144,768]{2,1,0:T(8,128)(2,1)S(1)} %get-tuple-element.252.refs_0_), channel_id=1, source_target_pairs={{0,4},{1,5},{2,6},{3,7},{4,0},{5,1},{6,2},{7,3},{8,12},{9,13},{10,... | collective-permute-start | bytes 1327112 | tf_op jit(solution)/shard_map/ppermute | solution.py:22
  (78 other events, 913.6 us)

commit v6 on v5

--- a/solution.py
+++ b/solution.py
@@ -46,7 +46,7 @@
 EVERY = range(100)
 TOKEN = (8, 128)
 COSTS = {'': (3000000000, 10000000000), 'grad_in': (10000000000, 1000000), 'grad_qkv': (10000000000, 1000000), 'attention_back': (10000000000, 1000000), 'feed': (100000000000, 1000000), 'tokens_back': (100000000000, 1000000), 'project': (1000000000, 1000000000), 'own_keys': (1000000000, 1000000000), 'cached_keys': (1000000000, 1000000000), 'bank_columns': (1000000000, 1000000000), 'cross': (1000000000, 1000000000), 'join': (1000000000, 1000000000), 'copy': (1000000000, 1000000000), 'choose_banks': (1000000000, 1000000000), 'grad_down': (3000000000, 10000000000)}
-PLAN = "ABNWYdqidiqdqtitiqFtqiHqG"
+PLAN = "ABNWYdqidiqqtidtiqFtqiHqG"
 
 
 def cost_of(name):

time: 300 us -> 312 us (1.040)
  waiting for transfers between devices: 115 us -> 136 us
  starting transfers between devices: 70.1 us -> 60.6 us
    ppermute x52, waiting for transfers between devices: 115 us -> 136 us  [swap(): return lax.ppermute(values, axis, [(i, i ^ mask) for i in range(size)])]
    ppermute x52, starting transfers between devices: 70.1 us -> 60.6 us  [swap(): return lax.ppermute(values, axis, [(i, i ^ mask) for i in range(size)])]
  transfers between devices with their start and end apart: 52 -> 52, of which waited for: 29 -> 28; matrix products, arithmetic and copies ran while one was open for 0% -> 0% of each run, Pallas kernels for 24% -> 23%
where the time goes in v6:
time: 312 us
  waiting for transfers between devices  136 us (44%)
  Pallas kernels  105 us (34%)
  starting transfers between devices  60.6 us (19%)
  local copies, waits for them, and re-layouts  7.41 us (2%)
    ppermute x52, waiting for transfers between devices, swap(): return lax.ppermute(values, axis, [(i, i ^ mask) for i in range(size)])  136 us
    pallas_call x33, Pallas kernels, call(): pl.pallas_call(body, grid_spec=spec, out_shape=out_shapes, compiler_param...  101 us
    ppermute x52, starting transfers between devices, swap(): return lax.ppermute(values, axis, [(i, i ^ mask) for i in range(size)])  60.6 us
    unnamed x100, local copies, waits for them, and re-layouts  7.39 us
  transfers between devices with their start and end apart: 52, of which 28 were waited for; matrix products, arithmetic and copies ran while one was open for 0% of the time, Pallas kernels for 23%

profile of v6, /device:TPU:0, one launch (start us, length us, event | category | flops | bytes accessed | tf_op | source)
XLA Modules:
  0.0 311.8 jit_solution(8450529903214627620)
XLA Ops:
  13.0 6.2 %collective-permute-done.1.refs_3_ = bf16[2,2,128,256]{3,2,1,0:T(8,128)(2,1)S(1)} collective-permute-done((bf16[2,2,128,256]{3,2,1,0:T(8,128)(2,1)S(1)}, bf16[2,2,128,256]{3,2,1,0:T(8,128)(2,1)S(1)}, u32[]{:S(2)}, u32[]{:S(2)}) %collective-permute-start.1) | collective-permute-done | bytes 262176 | tf_op jit(solution)/shard_map/ppermute | solution.py:22
  28.1 17.5 %collective-permute-done.5.refs_1_.refs_2_.refs_6_ = bf16[2,256,1024]{2,1,0:T(8,128)(2,1)S(1)} collective-permute-done((bf16[2,256,1024]{2,1,0:T(8,128)(2,1)}, bf16[2,256,1024]{2,1,0:T(8,128)(2,1)S(1)}, u32[]{:S(2)}, u32[]{:S(2)}) %collective-permute-start.5) | collective-permute-done | bytes 1048608 | tf_op jit(solution)/shard_map/ppermute | solution.py:22
  57.7 4.7 %project.2 = (bf16[256,1024]{1,0:T(8,128)(2,1)}, bf16[256,768]{1,0:T(8,128)(2,1)S(1)}, bf16[256,1024]{1,0:T(8,128)(2,1)}, bf16[256,768]{1,0:T(8,128)(2,1)S(1)}, ...) custom-call(s32[7]{0:T(128)S(1)} %copy-done.12, ...), custom_call_target="tpu_custom_call" | custom-call | flops 1000000000 | bytes 1000000000 | tf_op jit(solution)/shard_map/project/pallas_call | solution.py:116
  66.8 6.1 %own_keys.1 = (bf16[2,512,256]{2,1,0:T(8,128)(2,1)S(1)}, bf16[2,512,256]{2,1,0:T(8,128)(2,1)S(1)}, bf16[2,512,256]{2,1,0:T(8,128)(2,1)}, f32[2,512,256]{2,1,0:T(...) custom-call(s32[7]{0:T(128)S(1)} %copy-done.12, bf16[2,128,768]{2,1,0:T(8,128)(2,1)S(1)} %bitcast.22, ...), custom_call_target="tpu_custom_call" | custom-call | flops 1000000000 | bytes 1000000000 | tf_op jit(solution)/shard_map/own_keys/pallas_call | solution.py:116
  76.2 6.5 %cached_keys.1 = (f32[2,512,256]{2,1,0:T(8,128)}, f32[2,512,256]{2,1,0:T(8,128)}, bf16[2,128,256]{2,1,0:T(8,128)(2,1)S(1)}, bf16[2,128,256]{2,1,0:T(8,128)(2,1)S...) custom-call(s32[7]{0:T(128)S(1)} %copy-done.12, ...), custom_call_target="tpu_custom_call" | custom-call | flops 1000000000 | bytes 1000000000 | tf_op jit(solution)/shard_map/cached_keys/pallas_call | solution.py:116
  89.8 20.2 %feed.1 = (bf16[256,1024]{1,0:T(8,128)(2,1)}, f32[256,1024]{1,0:T(8,128)}, bf16[256,2048]{1,0:T(8,128)(2,1)}, bf16[256,4608]{1,0:T(8,128)(2,1)S(1)}, bf16[256,10...) custom-call(s32[7]{0:T(128)S(1)} %copy-done.12, ...), custom_call_target="tpu_custom_call" | custom-call | flops 99999997952 | bytes 1000000 | tf_op jit(solution)/shard_map/feed/pallas_call | solution.py:116
  116.4 3.9 %collective-permute-done.21 = bf16[256,256]{1,0:T(8,128)(2,1)S(1)} collective-permute-done((bf16[256,256]{1,0:T(8,128)(2,1)}, bf16[256,256]{1,0:T(8,128)(2,1)S(1)}, u32[]{:S(2)}, u32[]{:S(2)}) %collective-permute-start.21) | collective-permute-done | bytes 131104 | tf_op jit(solution)/shard_map/ppermute | solution.py:22
  126.5 13.9 %attention_back.1 = (bf16[3,2,128,256]{3,2,1,0:T(8,128)(2,1)S(1)}, bf16[3,2,128,256]{3,2,1,0:T(8,128)(2,1)S(1)}, bf16[3,2,128,256]{3,2,1,0:T(8,128)(2,1)S(1)}, b...) custom-call(s32[7]{0:T(128)S(1)} %copy-done.12, bf16[2,512,256]{2,1,0:T(8,128)(2,1)} %copy-done.4, ...), custom_call_target="tpu_custom_call" | custom-call | flops 10000000000 | bytes 1000000 | tf_op jit(solution)/shard_map/attention_back/pallas_call | solution.py:116
  140.6 6.3 %grad_in.1 = (bf16[2,160,2048]{2,1,0:T(8,128)(2,1)S(1)}, bf16[2,160,2048]{2,1,0:T(8,128)(2,1)S(1)}, bf16[2,160,2048]{2,1,0:T(8,128)(2,1)S(1)}, bf16[2,160,2048]{2,1,0:T(8,128)(2,1)S(1)}, s32[8,128]{1,0:T(8,128)S(1)}) custom-call(s32[7]{0:T(128)S(1)} %copy-done.12, bf16[256,1024]{1,0:T(8,128)(2,1)S(1)} %copy-done.27, ...), custom_call_target="tpu_custom_call" | custom-call | flops 10000000000 | bytes 1000000 | tf_op jit(solution)/shard_map/grad_in/pallas_call | solution.py:116
  152.8 5.7 %grad_qkv.1 = (bf16[4,144,768]{2,1,0:T(8,128)(2,1)S(1)}, bf16[4,144,768]{2,1,0:T(8,128)(2,1)S(1)}, s32[8,128]{1,0:T(8,128)S(1)}) custom-call(s32[7]{0:T(128)S(1)} %copy-done.12, bf16[256,1024]{1,0:T(8,128)(2,1)} %get-tuple-element.195.refs_0_, bf16[256,1024]{1,0:T(8,128)(2,1)} %get-tuple-element.196.refs_1_, bf16[256,1024]{1,0:T(8,128)(2,1)} %get-tuple-element.197.refs_2_, ...), custom_call_target="tpu_custom_call" | custom-call | flops 10000000000 | bytes 1000000 | tf_op jit(solution)/shard_map/grad_qkv/pallas_call | solution.py:116
  159.9 5.6 %collective-permute-start.34 = (bf16[256,1024]{1,0:T(8,128)(2,1)S(1)}, bf16[256,1024]{1,0:T(8,128)(2,1)S(1)}, u32[]{:S(2)}, u32[]{:S(2)}) collective-permute-start(bf16[256,1024]{1,0:T(8,128)(2,1)S(1)} %get-tuple-element.228), channel_id=1, source_target_pairs={{0,2},{1,3},{2,0},{3,1},{4,6},{5,7},{6,4},{7,5},{8,10},{9,11},{10,... | collective-permute-start | bytes 1572872 | tf_op jit(solution)/shard_map/ppermute | solution.py:22
  166.2 9.6 %collective-permute-done.30.refs_1_ = bf16[2,160,2048]{2,1,0:T(8,128)(2,1)S(1)} collective-permute-done((bf16[2,160,2048]{2,1,0:T(8,128)(2,1)S(1)}, bf16[2,160,2048]{2,1,0:T(8,128)(2,1)S(1)}, u32[]{:S(2)}, u32[]{:S(2)}) %collective-permute-start.30) | collective-permute-done | bytes 1310752 | tf_op jit(solution)/shard_map/ppermute | solution.py:22
  181.5 10.8 %collective-permute-done.32.refs_2_ = bf16[160,2048]{1,0:T(8,128)(2,1)S(1)} collective-permute-done((bf16[160,2048]{1,0:T(8,128)(2,1)S(1)}, bf16[160,2048]{1,0:T(8,128)(2,1)S(1)}, u32[]{:S(2)}, u32[]{:S(2)}) %collective-permute-start.32) | collective-permute-done | bytes 655392 | tf_op jit(solution)/shard_map/ppermute | solution.py:22
  192.3 4.1 %collective-permute-done.33.refs_5_ = bf16[160,2048]{1,0:T(8,128)(2,1)S(1)} collective-permute-done((bf16[160,2048]{1,0:T(8,128)(2,1)S(1)}, bf16[160,2048]{1,0:T(8,128)(2,1)S(1)}, u32[]{:S(2)}, u32[]{:S(2)}) %collective-permute-start.33) | collective-permute-done | bytes 655392 | tf_op jit(solution)/shard_map/ppermute | solution.py:22
  197.6 4.4 %collective-permute-done.29.refs_1_ = bf16[2,144,768]{2,1,0:T(8,128)(2,1)S(1)} collective-permute-done((bf16[2,144,768]{2,1,0:T(8,128)(2,1)S(1)}, bf16[2,144,768]{2,1,0:T(8,128)(2,1)S(1)}, u32[]{:S(2)}, u32[]{:S(2)}) %collective-permute-start.29) | collective-permute-done | bytes 442400 | tf_op jit(solution)/shard_map/ppermute | solution.py:22
  204.2 5.4 %collective-permute-start.38 = (bf16[160,2048]{1,0:T(8,128)(2,1)S(1)}, bf16[160,2048]{1,0:T(8,128)(2,1)S(1)}, u32[]{:S(2)}, u32[]{:S(2)}) collective-permute-start(bf16[160,2048]{1,0:T(8,128)(2,1)S(1)} %get-tuple-element.238), channel_id=1, source_target_pairs={{0,2},{1,3},{2,0},{3,1},{4,6},{5,7},{6,4},{7,5},{8,10},{9,11},{10,... | collective-permute-start | bytes 1966088 | tf_op jit(solution)/shard_map/ppermute | solution.py:22
  213.4 18.5 %collective-permute-done.38.refs_1_ = bf16[160,2048]{1,0:T(8,128)(2,1)S(1)} collective-permute-done((bf16[160,2048]{1,0:T(8,128)(2,1)S(1)}, bf16[160,2048]{1,0:T(8,128)(2,1)S(1)}, u32[]{:S(2)}, u32[]{:S(2)}) %collective-permute-start.38) | collective-permute-done | bytes 655392 | tf_op jit(solution)/shard_map/ppermute | solution.py:22
  237.3 21.0 %collective-permute-done.40.refs_1_ = bf16[256,1024]{1,0:T(8,128)(2,1)S(1)} collective-permute-done((bf16[256,1024]{1,0:T(8,128)(2,1)S(1)}, bf16[256,1024]{1,0:T(8,128)(2,1)S(1)}, u32[]{:S(2)}, u32[]{:S(2)}) %collective-permute-start.40) | collective-permute-done | bytes 524320 | tf_op jit(solution)/shard_map/ppermute | solution.py:22
  262.5 5.8 %collective-permute-done.43.refs_1_ = bf16[2,144,768]{2,1,0:T(8,128)(2,1)S(1)} collective-permute-done((bf16[2,144,768]{2,1,0:T(8,128)(2,1)S(1)}, bf16[2,144,768]{2,1,0:T(8,128)(2,1)S(1)}, u32[]{:S(2)}, u32[]{:S(2)}) %collective-permute-start.43) | collective-permute-done | bytes 442400 | tf_op jit(solution)/shard_map/ppermute | solution.py:22
  275.1 3.8 %collective-permute-done.39.refs_5_.refs_6_ = bf16[2,3,256,256]{3,2,1,0:T(8,128)(2,1)S(1)} collective-permute-done((bf16[2,3,256,256]{3,2,1,0:T(8,128)(2,1)S(1)}, bf16[2,3,256,256]{3,2,1,0:T(8,128)(2,1)S(1)}, u32[]{:S(2)}, u32[]{:S(2)}) %collective-permute-start.39) | collective-permute-done | bytes 786464 | tf_op jit(solution)/shard_map/ppermute | solution.py:22
  278.9 5.4 %tokens_back.1 = (f32[256,1024]{1,0:T(8,128)}, s32[8,128]{1,0:T(8,128)S(1)}) custom-call(s32[7]{0:T(128)S(1)} %copy-done.12, bf16[256,1024]{1,0:T(8,128)(2,1)S(1)} %bitcast.42, f32[256,1024]{1,0:T(8,128)S(1)} %copy-done.33, bf16[4,1024]{1,0:T(4,128)(2,1)S(1)} %copy-done.10, bf16[3,256,256]{2,1,0:T(8,128)(2,1)S(1)} %bitcast.48, ...), custom_call_target="tpu_custom_call" | custom-call | flops 99999997952 | bytes 1000000 | tf_op jit(solution)/shard_map/tokens_back/pallas_call | solution.py:116
  284.3 6.9 %collective-permute-done.45.refs_1_ = bf16[2,144,768]{2,1,0:T(8,128)(2,1)S(1)} collective-permute-done((bf16[2,144,768]{2,1,0:T(8,128)(2,1)S(1)}, bf16[2,144,768]{2,1,0:T(8,128)(2,1)S(1)}, u32[]{:S(2)}, u32[]{:S(2)}) %collective-permute-start.45) | collective-permute-done | bytes 442400 | tf_op jit(solution)/shard_map/ppermute | solution.py:22
  296.3 4.6 %in_finish.1 = (f32[256,4096]{1,0:T(8,128)}, f32[256,1024]{1,0:T(8,128)}, s32[8,128]{1,0:T(8,128)S(1)}) custom-call(s32[7]{0:T(128)S(1)} %copy-done.12, bf16[160,2048]{1,0:T(8,128)(2,1)S(1)} %get-tuple-element.255.refs_0_, bf16[160,2048]{1,0:T(8,128)(2,1)S(1)} %get-tuple-element.257.refs_1_, bf16[160,2048]{1,0:T(8,128)(2,1)S(1)} %collective-permute-done.48.refs_2_, ...), custom_call_target="tpu_custom_call" | custom-call | flops 3000000000 | bytes 10000000000 | tf_op jit(solution)/shard_map/in_finish/pallas_call | solution.py:116
  300.9 6.0 %collective-permute-done.46.refs_0_ = bf16[2,144,768]{2,1,0:T(8,128)(2,1)S(1)} collective-permute-done((bf16[2,144,768]{2,1,0:T(8,128)(2,1)S(1)}, bf16[2,144,768]{2,1,0:T(8,128)(2,1)S(1)}, u32[]{:S(2)}, u32[]{:S(2)}) %collective-permute-start.46) | collective-permute-done | bytes 442400 | tf_op jit(solution)/shard_map/ppermute | solution.py:22
  (225 shorter events, 107.4 us)
Async XLA Ops:
  21.6 24.0 %collective-permute-start.5 = (bf16[2,256,1024]{2,1,0:T(8,128)(2,1)}, bf16[2,256,1024]{2,1,0:T(8,128)(2,1)S(1)}, u32[]{:S(2)}, u32[]{:S(2)}) collective-permute-start(bf16[2,256,1024]{2,1,0:T(8,128)(2,1)} %get-tuple-element.148.refs_0_.refs_4_), channel_id=1, source_target_pairs={{0,16},{8,24},{16,0},{24,8},{1,17},{9,25},{17,1},{25,9},{2,18},{10... | collective-permute-start | bytes 3145736 | tf_op jit(solution)/shard_map/ppermute | solution.py:22
  23.2 22.7 %collective-permute-start.4 = (bf16[2,256,1024]{2,1,0:T(8,128)(2,1)}, bf16[2,256,1024]{2,1,0:T(8,128)(2,1)S(1)}, u32[]{:S(2)}, u32[]{:S(2)}) collective-permute-start(bf16[2,256,1024]{2,1,0:T(8,128)(2,1)} %get-tuple-element.148.refs_0_.refs_4_), channel_id=1, source_target_pairs={{0,8},{8,0},{16,24},{24,16},{1,9},{9,1},{17,25},{25,17},{2,10},{10... | collective-permute-start | bytes 3145736 | tf_op jit(solution)/shard_map/ppermute | solution.py:22
  23.7 26.5 %collective-permute-start.6 = (bf16[2,2,128,256]{3,2,1,0:T(8,128)(2,1)}, bf16[2,2,128,256]{3,2,1,0:T(8,128)(2,1)S(1)}, u32[]{:S(2)}, u32[]{:S(2)}) collective-permute-start(bf16[2,2,128,256]{3,2,1,0:T(8,128)(2,1)} %copy-done.40), channel_id=1, source_target_pairs={{0,2},{1,3},{2,0},{3,1},{4,6},{5,7},{6,4},{7,5},{8,10},{9,11},{10,... | collective-permute-start | bytes 786440 | tf_op jit(solution)/shard_map/ppermute | solution.py:22
  25.3 24.9 %collective-permute-start.7 = (bf16[2,2,128,256]{3,2,1,0:T(8,128)(2,1)}, bf16[2,2,128,256]{3,2,1,0:T(8,128)(2,1)S(1)}, u32[]{:S(2)}, u32[]{:S(2)}) collective-permute-start(bf16[2,2,128,256]{3,2,1,0:T(8,128)(2,1)} %copy-done.39), channel_id=1, source_target_pairs={{0,4},{1,5},{2,6},{3,7},{4,0},{5,1},{6,2},{7,3},{8,12},{9,13},{10,... | collective-permute-start | bytes 786440 | tf_op jit(solution)/shard_map/ppermute | solution.py:22
  27.9 22.8 %collective-permute-start.8 = (bf16[2,2,128,256]{3,2,1,0:T(8,128)(2,1)}, bf16[2,2,128,256]{3,2,1,0:T(8,128)(2,1)S(1)}, u32[]{:S(2)}, u32[]{:S(2)}) collective-permute-start(bf16[2,2,128,256]{3,2,1,0:T(8,128)(2,1)} %copy-done.38), channel_id=1, source_target_pairs={{0,6},{1,7},{2,4},{3,5},{4,2},{5,3},{6,0},{7,1},{8,14},{9,15},{10,... | collective-permute-start | bytes 786440 | tf_op jit(solution)/shard_map/ppermute | solution.py:22
  54.9 21.3 %collective-permute-start.15 = (bf16[2,2,128,256]{3,2,1,0:T(8,128)(2,1)S(1)}, bf16[2,2,128,256]{3,2,1,0:T(8,128)(2,1)S(1)}, u32[]{:S(2)}, u32[]{:S(2)}) collective-permute-start(bf16[2,2,128,256]{3,2,1,0:T(8,128)(2,1)S(1)} %get-tuple-element.169), channel_id=1, source_target_pairs={{0,4},{1,5},{2,6},{3,7},{4,0},{5,1},{6,2},{7,3},{8,12},{9,13},{10,... | collective-permute-start | bytes 786440 | tf_op jit(solution)/shard_map/ppermute | solution.py:22
  122.4 26.5 %collective-permute-start.24 = (bf16[256,1024]{1,0:T(8,128)(2,1)}, bf16[256,1024]{1,0:T(8,128)(2,1)S(1)}, u32[]{:S(2)}, u32[]{:S(2)}) collective-permute-start(bf16[256,1024]{1,0:T(8,128)(2,1)} %get-tuple-element.202), channel_id=1, source_target_pairs={{0,8},{8,0},{16,24},{24,16},{1,9},{9,1},{17,25},{25,17},{2,10},{10... | collective-permute-start | bytes 1572872 | tf_op jit(solution)/shard_map/ppermute | solution.py:22
  123.4 25.5 %collective-permute-start.25 = (bf16[256,1024]{1,0:T(8,128)(2,1)}, bf16[256,1024]{1,0:T(8,128)(2,1)S(1)}, u32[]{:S(2)}, u32[]{:S(2)}) collective-permute-start(bf16[256,1024]{1,0:T(8,128)(2,1)} %get-tuple-element.203), channel_id=1, source_target_pairs={{0,16},{8,24},{16,0},{24,8},{1,17},{9,25},{17,1},{25,9},{2,18},{10... | collective-permute-start | bytes 1572872 | tf_op jit(solution)/shard_map/ppermute | solution.py:22
  124.3 24.6 %collective-permute-start.26 = (bf16[256,1024]{1,0:T(8,128)(2,1)}, bf16[256,1024]{1,0:T(8,128)(2,1)S(1)}, u32[]{:S(2)}, u32[]{:S(2)}) collective-permute-start(bf16[256,1024]{1,0:T(8,128)(2,1)} %get-tuple-element.204), channel_id=1, source_target_pairs={{0,24},{8,16},{16,8},{24,0},{1,25},{9,17},{17,9},{25,1},{2,26},{10... | collective-permute-start | bytes 1572872 | tf_op jit(solution)/shard_map/ppermute | solution.py:22
  146.9 28.9 %collective-permute-start.30 = (bf16[2,160,2048]{2,1,0:T(8,128)(2,1)S(1)}, bf16[2,160,2048]{2,1,0:T(8,128)(2,1)S(1)}, u32[]{:S(2)}, u32[]{:S(2)}) collective-permute-start(bf16[2,160,2048]{2,1,0:T(8,128)(2,1)S(1)} %get-tuple-element.221), channel_id=1, source_target_pairs={{0,8},{8,0},{16,24},{24,16},{1,9},{9,1},{17,25},{25,17},{2,10},{10... | collective-permute-start | bytes 3932168 | tf_op jit(solution)/shard_map/ppermute | solution.py:22
  147.9 29.2 %collective-permute-start.31 = (bf16[2,160,2048]{2,1,0:T(8,128)(2,1)S(1)}, bf16[2,160,2048]{2,1,0:T(8,128)(2,1)S(1)}, u32[]{:S(2)}, u32[]{:S(2)}) collective-permute-start(bf16[2,160,2048]{2,1,0:T(8,128)(2,1)S(1)} %get-tuple-element.223), channel_id=1, source_target_pairs={{0,16},{8,24},{16,0},{24,8},{1,17},{9,25},{17,1},{25,9},{2,18},{10... | collective-permute-start | bytes 3932168 | tf_op jit(solution)/shard_map/ppermute | solution.py:22
  159.9 20.9 %collective-permute-start.34 = (bf16[256,1024]{1,0:T(8,128)(2,1)S(1)}, bf16[256,1024]{1,0:T(8,128)(2,1)S(1)}, u32[]{:S(2)}, u32[]{:S(2)}) collective-permute-start(bf16[256,1024]{1,0:T(8,128)(2,1)S(1)} %get-tuple-element.228), channel_id=1, source_target_pairs={{0,2},{1,3},{2,0},{3,1},{4,6},{5,7},{6,4},{7,5},{8,10},{9,11},{10,... | collective-permute-start | bytes 1572872 | tf_op jit(solution)/shard_map/ppermute | solution.py:22
  180.1 21.9 %collective-permute-start.29 = (bf16[2,144,768]{2,1,0:T(8,128)(2,1)S(1)}, bf16[2,144,768]{2,1,0:T(8,128)(2,1)S(1)}, u32[]{:S(2)}, u32[]{:S(2)}) collective-permute-start(bf16[2,144,768]{2,1,0:T(8,128)(2,1)S(1)} %get-tuple-element.219), channel_id=1, source_target_pairs={{0,8},{8,0},{16,24},{24,16},{1,9},{9,1},{17,25},{25,17},{2,10},{10... | collective-permute-start | bytes 1327112 | tf_op jit(solution)/shard_map/ppermute | solution.py:22
  204.2 27.7 %collective-permute-start.38 = (bf16[160,2048]{1,0:T(8,128)(2,1)S(1)}, bf16[160,2048]{1,0:T(8,128)(2,1)S(1)}, u32[]{:S(2)}, u32[]{:S(2)}) collective-permute-start(bf16[160,2048]{1,0:T(8,128)(2,1)S(1)} %get-tuple-element.238), channel_id=1, source_target_pairs={{0,2},{1,3},{2,0},{3,1},{4,6},{5,7},{6,4},{7,5},{8,10},{9,11},{10,... | collective-permute-start | bytes 1966088 | tf_op jit(solution)/shard_map/ppermute | solution.py:22
  209.6 23.0 %collective-permute-start.37 = (bf16[256,1024]{1,0:T(8,128)(2,1)S(1)}, bf16[256,1024]{1,0:T(8,128)(2,1)S(1)}, u32[]{:S(2)}, u32[]{:S(2)}) collective-permute-start(bf16[256,1024]{1,0:T(8,128)(2,1)S(1)} %get-tuple-element.236.refs_0_), channel_id=1, source_target_pairs={{0,4},{1,5},{2,6},{3,7},{4,0},{5,1},{6,2},{7,3},{8,12},{9,13},{10,... | collective-permute-start | bytes 1572872 | tf_op jit(solution)/shard_map/ppermute | solution.py:22
  212.2 46.1 %collective-permute-start.36 = (bf16[2,3,256,256]{3,2,1,0:T(8,128)(2,1)S(1)}, bf16[2,3,256,256]{3,2,1,0:T(8,128)(2,1)S(1)}, u32[]{:S(2)}, u32[]{:S(2)}) collective-permute-start(bf16[2,3,256,256]{3,2,1,0:T(8,128)(2,1)S(1)} %get-tuple-element.235), channel_id=1, source_target_pairs={{0,8},{8,0},{16,24},{24,16},{1,9},{9,1},{17,25},{25,17},{2,10},{10... | collective-permute-start | bytes 2359304 | tf_op jit(solution)/shard_map/ppermute | solution.py:22
  233.3 25.0 %collective-permute-start.40 = (bf16[256,1024]{1,0:T(8,128)(2,1)S(1)}, bf16[256,1024]{1,0:T(8,128)(2,1)S(1)}, u32[]{:S(2)}, u32[]{:S(2)}) collective-permute-start(bf16[256,1024]{1,0:T(8,128)(2,1)S(1)} %get-tuple-element.243.refs_0_), channel_id=1, source_target_pairs={{0,2},{1,3},{2,0},{3,1},{4,6},{5,7},{6,4},{7,5},{8,10},{9,11},{10,... | collective-permute-start | bytes 1572872 | tf_op jit(solution)/shard_map/ppermute | solution.py:22
  235.4 26.3 %collective-permute-start.44 = (bf16[160,2048]{1,0:T(8,128)(2,1)S(1)}, bf16[160,2048]{1,0:T(8,128)(2,1)S(1)}, u32[]{:S(2)}, u32[]{:S(2)}) collective-permute-start(bf16[160,2048]{1,0:T(8,128)(2,1)S(1)} %get-tuple-element.246.refs_0_), channel_id=1, source_target_pairs={{0,4},{1,5},{2,6},{3,7},{4,0},{5,1},{6,2},{7,3},{8,12},{9,13},{10,... | collective-permute-start | bytes 1966088 | tf_op jit(solution)/shard_map/ppermute | solution.py:22
  236.4 31.9 %collective-permute-start.43 = (bf16[2,144,768]{2,1,0:T(8,128)(2,1)S(1)}, bf16[2,144,768]{2,1,0:T(8,128)(2,1)S(1)}, u32[]{:S(2)}, u32[]{:S(2)}) collective-permute-start(bf16[2,144,768]{2,1,0:T(8,128)(2,1)S(1)} %get-tuple-element.245), channel_id=1, source_target_pairs={{0,2},{1,3},{2,0},{3,1},{4,6},{5,7},{6,4},{7,5},{8,10},{9,11},{10,... | collective-permute-start | bytes 1327112 | tf_op jit(solution)/shard_map/ppermute | solution.py:22
  237.3 32.0 %collective-permute-start.41 = (bf16[256,1024]{1,0:T(8,128)(2,1)S(1)}, bf16[256,1024]{1,0:T(8,128)(2,1)S(1)}, u32[]{:S(2)}, u32[]{:S(2)}) collective-permute-start(bf16[256,1024]{1,0:T(8,128)(2,1)S(1)} %get-tuple-element.243.refs_0_), channel_id=1, source_target_pairs={{0,1},{1,0},{2,3},{3,2},{4,5},{5,4},{6,7},{7,6},{8,9},{9,8},{10,11... | collective-permute-start | bytes 1572872 | tf_op jit(solution)/shard_map/ppermute | solution.py:22
  258.9 20.0 %collective-permute-start.39 = (bf16[2,3,256,256]{3,2,1,0:T(8,128)(2,1)S(1)}, bf16[2,3,256,256]{3,2,1,0:T(8,128)(2,1)S(1)}, u32[]{:S(2)}, u32[]{:S(2)}) collective-permute-start(bf16[2,3,256,256]{3,2,1,0:T(8,128)(2,1)S(1)} %get-tuple-element.242), channel_id=1, source_target_pairs={{0,16},{8,24},{16,0},{24,8},{1,17},{9,25},{17,1},{25,9},{2,18},{10... | collective-permute-start | bytes 2359304 | tf_op jit(solution)/shard_map/ppermute | solution.py:22
  262.4 33.9 %collective-permute-start.48 = (bf16[160,2048]{1,0:T(8,128)(2,1)S(1)}, bf16[160,2048]{1,0:T(8,128)(2,1)S(1)}, u32[]{:S(2)}, u32[]{:S(2)}) collective-permute-start(bf16[160,2048]{1,0:T(8,128)(2,1)S(1)} %get-tuple-element.255.refs_0_), channel_id=1, source_target_pairs={{0,1},{1,0},{2,3},{3,2},{4,5},{5,4},{6,7},{7,6},{8,9},{9,8},{10,11... | collective-permute-start | bytes 1966088 | tf_op jit(solution)/shard_map/ppermute | solution.py:22
  268.3 25.1 %collective-permute-start.47 = (bf16[160,2048]{1,0:T(8,128)(2,1)S(1)}, bf16[160,2048]{1,0:T(8,128)(2,1)S(1)}, u32[]{:S(2)}, u32[]{:S(2)}) collective-permute-start(bf16[160,2048]{1,0:T(8,128)(2,1)S(1)} %get-tuple-element.255.refs_0_), channel_id=1, source_target_pairs={{0,2},{1,3},{2,0},{3,1},{4,6},{5,7},{6,4},{7,5},{8,10},{9,11},{10,... | collective-permute-start | bytes 1966088 | tf_op jit(solution)/shard_map/ppermute | solution.py:22
  269.3 21.9 %collective-permute-start.45 = (bf16[2,144,768]{2,1,0:T(8,128)(2,1)S(1)}, bf16[2,144,768]{2,1,0:T(8,128)(2,1)S(1)}, u32[]{:S(2)}, u32[]{:S(2)}) collective-permute-start(bf16[2,144,768]{2,1,0:T(8,128)(2,1)S(1)} %get-tuple-element.252.refs_0_), channel_id=1, source_target_pairs={{0,4},{1,5},{2,6},{3,7},{4,0},{5,1},{6,2},{7,3},{8,12},{9,13},{10,... | collective-permute-start | bytes 1327112 | tf_op jit(solution)/shard_map/ppermute | solution.py:22
  (78 other events, 914.0 us)
